TPU v7x, 32 devices: a whole 2x2x4 slice. The times are simulated.
32 devices in a mesh: grp: 4 (over z), gx: 4 (over y, x), gy: 2 (over core).
Axes of the slice: x: 2, y: 2, z: 4, core: 2. Of those that a mesh axis runs over, the one named last changes fastest.
Arguments:
- state: float32 [8, 4, 125, 4, 256], P(('grp', 'gy'), None, None, 'gx'), may hold values from -6 to 6
- damping: float32 [4, 256], P('gx'), may hold values from 0.5 to 20
- absorb_mask: int32 [4, 256], P('gx'), may hold values 0 or 1
- lift_gain: float32 [64], replicated, may hold values from -3 to 3
- proj_weight: float32 [64], replicated, may hold values from -0.75 to 0.75
- spectral: float32 [4096, 64, 64], P('gx'), may hold values from -3 to 3
- moment_one: bfloat16 [4096, 64, 64], P('gx'), may hold values from -5 to 5
- moment_two: bfloat16 [4096, 64, 64], P('gx'), may hold values from 0.0099487305 to 1
Outputs:
- new_state: float32 [8, 4, 125, 4, 256], P(('grp', 'gy'), None, None, 'gx')
- new_spectral: float32 [4096, 64, 64], P('gx')
- new_moment_one: bfloat16 [4096, 64, 64], P('gx')
- new_moment_two: bfloat16 [4096, 64, 64], P('gx')
All inputs are finite; a program needn't handle non-finite values. No bound on the sum of `absorb_mask` on one device may be relied on, other than what follows from the above.
Results may differ from a plain program's by a relative error of at most 0.0004.
Values may be sent and summed in bfloat16 or wider, within the bound.
No kernel may reach another device: no remote copies, remote signals or barrier semaphores. Data moves between devices by JAX's collectives and lax.ppermute only.
A program may use at most 128 MiB of HBM per device.

v0:
```python
import math

import jax
import jax.numpy as jnp
import numpy as np
from jax import lax
from jax.sharding import PartitionSpec as P

KM = 16
TY = 64
TZ = 64
MODES = 4096


HIGHEST = lax.Precision.HIGHEST
TIME_STEP = 0.02
FACE_GAIN = 10.0
LOSS_SCALE = 1.0 / 2048.0
LEARN_RATE = 0.001
BETA_ONE = 0.9
BETA_TWO = 0.999
BIAS_ONE = 1.0 - BETA_ONE**10
BIAS_TWO = 1.0 - BETA_TWO**10
EPSILON = 1e-08
HALF_ROOT = 1.0 / math.sqrt(2.0)
GAUSS_NORM = 1.0 / math.sqrt(2.0 * math.pi)


def extended(array, sides, width):
    for axis, dim in sides:
        count, length = (lax.axis_size(axis), array.shape[dim])
        up = [(i, (i + 1) % count) for i in range(count - 1)]
        down = [(j, i) for i, j in up]
        last = lax.slice_in_dim(array, length - width, length, axis=dim)
        initial = lax.slice_in_dim(array, 0, width, axis=dim)
        before = lax.ppermute(last, axis, up)
        after = lax.ppermute(initial, axis, down)
        array = jnp.concatenate([before, array, after], axis=dim)
    return array


def from_behind(array, axis, by):
    count = lax.axis_size(axis)
    return lax.ppermute(array, axis, [(i, (i + by) % count) for i in range(count)])


def lagrange(gll_nodes, column, target_point):
    result_value = 1.0
    for other_node in range(len(gll_nodes)):
        if other_node != column:
            result_value = (
                result_value
                * (target_point - gll_nodes[other_node])
                / (gll_nodes[column] - gll_nodes[other_node])
            )
    return result_value


def lagrange_slope(gll_nodes, column, target_point):
    slope_total = 0.0
    for skipped in range(len(gll_nodes)):
        if skipped != column:
            factor = 1.0 / (gll_nodes[column] - gll_nodes[skipped])
            for other_node in range(len(gll_nodes)):
                if other_node != column and other_node != skipped:
                    factor = (
                        factor
                        * (target_point - gll_nodes[other_node])
                        / (gll_nodes[column] - gll_nodes[other_node])
                    )
            slope_total = slope_total + factor
    return slope_total


def gll_tables():
    gll_nodes = [-1.0, -math.sqrt(3.0 / 7.0), 0.0, math.sqrt(3.0 / 7.0), 1.0]
    slopes = np.zeros((5, 5))
    interp = np.zeros((4, 5))
    for node_row in range(5):
        for column in range(5):
            slopes[node_row, column] = lagrange_slope(gll_nodes, column, gll_nodes[node_row])
    for sample in range(4):
        for column in range(5):
            interp[sample, column] = lagrange(gll_nodes, column, -1.0 + (2.0 * sample + 1.0) / 4.0)
    return (jnp.asarray(slopes, dtype=jnp.float32), jnp.asarray(interp, dtype=jnp.float32))


def fourier_table(length, kept):
    angles = np.arange(length) * (2.0 * math.pi / length)
    table_rows = []
    for freq_index in range(kept // 2 + 1):
        factor = math.sqrt(1.0 / length) if freq_index == 0 else math.sqrt(2.0 / length)
        table_rows.append(factor * np.cos(freq_index * angles))
    for freq_index in range(1, kept // 2):
        table_rows.append(math.sqrt(2.0 / length) * np.sin(freq_index * angles))
    return np.stack(table_rows)


def joint_table(length_y, length_z, kept):
    joined = np.kron(fourier_table(length_y, kept), fourier_table(length_z, kept))
    return jnp.asarray(joined, dtype=jnp.float32).astype(jnp.bfloat16)


def apply_along(matrix, field_values, node_axis):
    applied = jnp.tensordot(matrix, field_values, axes=((1,), (node_axis,)), precision=HIGHEST)
    return jnp.moveaxis(applied, 0, node_axis)


def shift_elements(pack, elem_step, z_count, along_z):
    total_elems = pack.shape[-1]
    padding = jnp.zeros(pack.shape[:-1] + (abs(elem_step),), pack.dtype)
    if elem_step > 0:
        shifted = jnp.concatenate([padding, pack[..., : total_elems - elem_step]], axis=-1)
    else:
        shifted = jnp.concatenate([pack[..., -elem_step:], padding], axis=-1)
    if along_z:
        position = lax.broadcasted_iota(jnp.int32, (total_elems,), 0) % z_count
        edge_index = 0 if elem_step > 0 else z_count - 1
        shifted = jnp.where(position == edge_index, 0.0, shifted)
    return shifted


def place_faces(low_face, high_face, node_axis):
    empty_face = jnp.zeros_like(low_face)
    return jnp.stack([low_face, empty_face, empty_face, empty_face, high_face], axis=node_axis)


def rates_of(fields, sink_rate, x_neighbours, z_count, slopes):
    pressure = fields[0]
    pressure_rate = jnp.zeros_like(pressure)
    velocity_rates = []
    for direction in range(3):
        velocity = fields[1 + direction]
        pressure_rate = pressure_rate - 2.0 * apply_along(slopes, velocity, direction)
        change = -2.0 * apply_along(slopes, pressure, direction)
        low_pack = jnp.stack(
            [jnp.take(pressure, 0, axis=direction), jnp.take(velocity, 0, axis=direction)]
        )
        high_pack = jnp.stack(
            [jnp.take(pressure, 4, axis=direction), jnp.take(velocity, 4, axis=direction)]
        )
        if direction == 0:
            from_low, from_high = x_neighbours(low_pack, high_pack)
        else:
            elem_step = z_count if direction == 1 else 1
            from_low = shift_elements(high_pack, elem_step, z_count, direction == 2)
            from_high = shift_elements(low_pack, -elem_step, z_count, direction == 2)
        jump_low = low_pack - from_low
        jump_high = high_pack - from_high
        low_rate = -FACE_GAIN * (jump_low[1] + jump_low[0])
        high_rate = FACE_GAIN * (jump_high[1] - jump_high[0])
        pressure_rate = pressure_rate + place_faces(low_rate, high_rate, direction)
        change = change + place_faces(low_rate, -high_rate, direction)
        velocity_rates.append(change)
    rates = jnp.stack([pressure_rate] + velocity_rates)
    return rates - sink_rate * fields


def advance(fields, sink_rate, x_neighbours, z_count, slopes):
    first_rate = rates_of(fields, sink_rate, x_neighbours, z_count, slopes)
    mid_section = fields + TIME_STEP * first_rate
    second_rate = rates_of(mid_section, sink_rate, x_neighbours, z_count, slopes)
    return 0.5 * (fields + mid_section + TIME_STEP * second_rate)


def regrid(pressure, interp):
    result_grid = apply_along(interp, pressure, 0)
    result_grid = apply_along(interp, result_grid, 1)
    return apply_along(interp, result_grid, 2)


def lift_field(inputs, lift_gain):
    scaled = lift_gain[None, :, None, None] * inputs[:, None].astype(jnp.float32)
    return jax.nn.gelu(scaled, approximate=False).astype(jnp.bfloat16)


def to_basis(field_values, table_x, table_yz, kept):
    along_yz = jnp.einsum(
        "tcxp,qp->tcxq", field_values, table_yz, preferred_element_type=jnp.float32
    )
    basis_coeffs = jnp.einsum(
        "tcxq,ax->aqtc", along_yz, table_x.astype(jnp.float32), precision=HIGHEST
    )
    return basis_coeffs.reshape(kept * kept * kept, field_values.shape[0], field_values.shape[1])


def from_basis(mixed_modes, table_x, table_yz, kept):
    shaped = mixed_modes.reshape(kept, kept * kept, mixed_modes.shape[1], mixed_modes.shape[2])
    along_x = jnp.einsum("aqto,ax->toxq", shaped, table_x, preferred_element_type=jnp.float32)
    return jnp.einsum("toxq,qp->toxp", along_x, table_yz.astype(jnp.float32), precision=HIGHEST)


def backward(pre_act, targets, proj_weight):
    active = jax.nn.gelu(pre_act, approximate=False)
    predicted = jnp.einsum("toxp,o->txp", active, proj_weight, precision=HIGHEST)
    misfit = predicted - targets.astype(jnp.float32)
    gelu_slope = (
        0.5 * (1.0 + lax.erf(pre_act * HALF_ROOT))
        + pre_act * jnp.exp(-0.5 * pre_act * pre_act) * GAUSS_NORM
    )
    scaled = 2.0 * LOSS_SCALE * misfit[:, None] * proj_weight[None, :, None, None] * gelu_slope
    return scaled.astype(jnp.bfloat16)


def adam_update(spectral, moment_one, moment_two, gradient):
    first_moment = BETA_ONE * moment_one.astype(jnp.float32) + (1.0 - BETA_ONE) * gradient
    second_moment = (
        BETA_TWO * moment_two.astype(jnp.float32) + (1.0 - BETA_TWO) * gradient * gradient
    )
    denominator = jnp.sqrt(second_moment / BIAS_TWO) + EPSILON
    new_spectral = spectral - LEARN_RATE * (first_moment / BIAS_ONE) / denominator
    return (new_spectral, first_moment.astype(jnp.bfloat16), second_moment.astype(jnp.bfloat16))


def slab_faces(low_pack, high_pack):
    pack_shape = low_pack.shape
    both_sides = jnp.stack([low_pack, high_pack]).reshape(2, -1, pack_shape[-1])
    padded = extended(both_sides, (("gx", 0),), 1)
    return (padded[0].reshape(pack_shape), padded[3].reshape(pack_shape))


def per_device(
    state, damping, absorb_mask, lift_gain, proj_weight, spectral, moment_one, moment_two
):
    slopes, interp = gll_tables()
    elements = state.shape[-1]
    z_count = TZ // 4
    rows_y = elements // z_count
    fields = state.reshape(4, 5, 5, 5, 1, elements)
    sink_rate = absorb_mask.astype(jnp.float32) * damping
    new_fields = advance(fields, sink_rate, slab_faces, z_count, slopes)
    snap_pair = jnp.stack([regrid(fields[0], interp), regrid(new_fields[0], interp)]).astype(
        jnp.bfloat16
    )
    snap_pair = snap_pair.reshape(2, 4, 4, 4, rows_y, z_count)
    outgoing = jnp.transpose(snap_pair, (0, 1, 4, 2, 5, 3)).reshape(2, 4, TY * TZ)
    tile_data = from_behind(outgoing, "grp", 1)
    inputs = tile_data[0][None]
    targets = tile_data[1][None]
    slab_count = lax.axis_size("gx")
    table_x_all = jnp.asarray(fourier_table(4 * slab_count, KM), dtype=jnp.float32).astype(
        jnp.bfloat16
    )
    table_x = lax.dynamic_slice_in_dim(table_x_all, 4 * lax.axis_index("gx"), 4, 1)
    table_yz = joint_table(TY, TZ, KM)
    mode_rows = MODES // slab_count

    def coefficients(field_values):
        partial_value = to_basis(field_values, table_x, table_yz, KM).reshape(MODES, -1)
        summed = lax.psum_scatter(partial_value, "gx", scatter_dimension=0, tiled=True)
        return summed.reshape(mode_rows, field_values.shape[0], field_values.shape[1])

    lifted = lift_field(inputs, lift_gain)
    coeffs = coefficients(lifted)
    mixed_modes = jnp.einsum("mtc,mco->mto", coeffs, spectral, precision=HIGHEST).astype(
        jnp.bfloat16
    )
    every_mode = lax.all_gather(mixed_modes, "gx", axis=0, tiled=True)
    pre_act = from_basis(every_mode, table_x, table_yz, KM)
    grad_pre = backward(pre_act, targets, proj_weight)
    grad_coeffs = coefficients(grad_pre)
    local_grad = jnp.einsum("mtc,mto->mco", coeffs, grad_coeffs, precision=HIGHEST)
    gradient = lax.psum(local_grad, ("grp", "gy"))
    new_spectral, new_moment_one, new_moment_two = adam_update(
        spectral, moment_one, moment_two, gradient
    )
    return (new_fields.reshape(state.shape), new_spectral, new_moment_one, new_moment_two)


def solution(mesh):
    in_specs = (
        P(("grp", "gy"), None, None, "gx", None),
        P("gx", None),
        P("gx", None),
        P(),
        P(),
        P("gx", None, None),
        P("gx", None, None),
        P("gx", None, None),
    )
    out_specs = (
        P(("grp", "gy"), None, None, "gx", None),
        P("gx", None, None),
        P("gx", None, None),
        P("gx", None, None),
    )
    return jax.shard_map(
        per_device, mesh=mesh, in_specs=in_specs, out_specs=out_specs, check_vma=False
    )
```

profile of v0, /device:TPU:0, one launch (start us, length us, event | category | flops | bytes accessed | tf_op | source)
XLA Modules:
  0.0 561.7 jit_solution(11006033665297060539)
XLA Ops:
  7.3 2.6 slice_reduce_fusion.3
  10.0 1.3 collective-permute-start.1
  11.8 0.6 fusion.248
  12.5 0.3 fusion.344
  12.8 0.3 fusion.186
  13.1 0.3 fusion.196
  13.9 0.3 fusion.194
  14.5 0.3 fusion.189
  14.8 0.3 fusion.343
  16.1 0.8 collective-permute-done.1
  17.0 4.8 collective-permute-start
  21.8 1.7 collective-permute-done
  23.8 1.2 fusion.135
  25.6 0.3 fusion.181
  26.3 0.3 fusion.177
  26.7 0.3 fusion.175
  27.0 0.3 fusion.179
  27.4 0.3 fusion.183
  27.9 1.3 collective-permute-start.3
  29.6 5.1 collective-permute-done.3
  34.8 17.7 %collective-permute-start.2 = (f32[1,50,256]{2,0,1:T(1,128)S(1)}, f32[1,50,256]{2,0,1:T(1,128)S(1)}, u32[]{:S(2)}, u32[]{:S(2)}) collective-permute-start(f32[1,50,256]{2,0,1:T(1,128)S(1)} %bitcast.463), channel_id=1, source_target_pairs={{0,2},{2,4},{4,6},{1,3},{3,5},{5,7},{8,10},{10,12},{12,14},{9,11},... | collective-permute-start | bytes 153608 | tf_op jit(solution)/shard_map/ppermute | solution.py:36
  53.2 0.3 fusion.192
  53.5 0.3 copy-done.7
  54.7 3.2 copy.503
  58.0 4.0 reshape.1145
  62.0 1.6 collective-permute-start.4
  63.6 4.5 collective-permute-done.4
  68.1 10.8 %fusion.125 = f32[64,4,256]{2,0,1:T(8,128)S(1)} fusion(bf16[256,4096,1]{1,0,2:T(8,128)(2,1)} %constant.442, f32[4,4096]{1,0:T(4,128)S(1)} %fusion.245, f32[64]{0:T(128)} %param.27), kind=kOutput, calls=%fused_computation.147 | convolution fusion | flops 606076928 | bytes 2425088 | tf_op jit(solution)/shard_map/tcxp,qp->tcxq/dot_general | solution.py:178
  79.0 0.7 fusion.152
  79.7 1.6 copy.539
  81.3 26.9 %reduce-scatter.3.cloned.1.call-done = f32[1024,64]{0,1:T(8,128)} async-done(((f32[4096,64]{0,1:T(8,128)}), f32[1024,64]{0,1:T(8,128)}) %reduce-scatter.3.cloned.1.call-update) | async-done | bytes 262160 | tf_op jit(solution)/shard_map/reduce_scatter | solution.py:250
  108.2 8.0 %multiply_reduce_fusion = bf16[1024,64]{0,1:T(8,128)(2,1)S(1)} fusion(f32[1024,64,64]{0,2,1:T(8,128)} %param.29, f32[1024,64]{0,1:T(8,128)} %reduce-scatter.3.cloned.1.call-done), kind=kLoop, calls=%fused_computation.2 | loop fusion | flops 8323072 | bytes 17170432 | tf_op jit(solution)/shard_map/mtc,mco->mto/dot_general | solution.py:255
  116.2 10.4 %all-gather = bf16[4096,64]{0,1:T(8,128)(2,1)S(1)} all-gather(bf16[1024,64]{0,1:T(8,128)(2,1)S(1)} %multiply_reduce_fusion), channel_id=2, replica_groups=mesh['grp'=4,'gx'=4,'gy'=2] {'gx'}, dimensions={0}, use_global_device_ids=true | all-gather | bytes 655360 | tf_op jit(solution)/shard_map/all_gather | solution.py:258
  126.9 5.8 %fusion.140 = (u8[64,4096]{1,0:T(8,128)(4,1)S(1)}, u8[64,4096]{1,0:T(8,128)(4,1)S(1)}, u8[64,4096]{1,0:T(8,128)(4,1)S(1)}, f32[64,4,4096]{2,0,1:T(8,128)S(1)}) fusion(bf16[256,4096,1]{1,0,2:T(8,128)(2,1)} %constant.442, f32[64,4,256]{2,1,0:T(4,128)S(1)} %convolution_bitcast_fusion), kind=kOutput, calls=%fused_computation.166 | convolution fusion | flops 3241410560 | bytes 7340032 | tf_op jit(solution)/shard_map/toxq,qp->toxp/dot_general | solution.py:190
  132.7 1.1 and_convert_fusion
  133.8 1.1 and_convert_fusion.1
  134.9 1.1 and_convert_fusion.2
  136.1 12.4 %fusion.36 = f32[1,4,4096]{2,0,1:T(1,128)S(1)} fusion(pred[64,4,4096]{2,0,1:T(32,128)(4,1)S(1)} %and_convert_fusion.2, pred[64,4,4096]{2,0,1:T(32,128)(4,1)S(1)} %and_convert_fusion.1, pred[64,4,4096]{2,0,1:T(32,128)(4,1)S(1)} %and_convert_fusion, f32[64,4,4096]{2,0,1:T(8,128)S(1)} %get-tuple-element.159, f32[64]{0:T(128)S(1)} %copy-done.23), kind=kOutput, calls=%fused_computation.46 | convolution fusion | flops 76546048 | bytes 7405824 | tf_op jit(solution)/shard_map/toxp,o->txp/dot_general | solution.py:195
  148.6 2.1 fusion.127
  150.7 0.7 fusion.148
  151.4 1.6 copy.541
  153.2 27.7 %reduce-scatter.5.cloned.1.call-done = f32[1024,64]{0,1:T(8,128)} async-done(((f32[4096,64]{0,1:T(8,128)}), f32[1024,64]{0,1:T(8,128)}) %reduce-scatter.5.cloned.1.call-update) | async-done | bytes 262160 | tf_op jit(solution)/shard_map/reduce_scatter | solution.py:250
  180.9 9.3 %broadcast_multiply_fusion = f32[1024,64,64]{0,2,1:T(8,128)} fusion(f32[1024,64]{0,1:T(8,128)} %reduce-scatter.5.cloned.1.call-done, f32[1024,64]{0,1:T(8,128)S(1)} %copy-done.13), kind=kLoop, calls=%fused_computation.7 | loop fusion | flops 4194304 | bytes 17301504 | tf_op jit(solution)/shard_map/mtc,mto->mco/dot_general | solution.py:262
  190.3 0.8 copy-done.10
  192.6 1.2 fusion.147
  193.8 1.3 copy.507
  195.1 328.2 %all-reduce.10.cloned.1.call-done = f32[1024,64,64]{0,2,1:T(8,128)} async-done(((f32[1024,64,64]{0,2,1:T(8,128)}), f32[1024,64,64]{0,2,1:T(8,128)}) %all-reduce.10.cloned.1.call-update) | async-done | bytes 16777232 | tf_op jit(solution)/shard_map/psum | solution.py:263
  523.3 31.6 %fusion.2 = (bf16[1024,64,64]{0,2,1:T(8,128)(2,1)}, f32[1024,64,64]{0,2,1:T(8,128)}, bf16[1024,64,64]{0,2,1:T(8,128)(2,1)}) fusion(f32[1024,64,64]{0,2,1:T(8,128)} %all-reduce.10.cloned.1.call-done, bf16[1024,64,64]{0,2,1:T(8,128)(2,1)} %param.31, f32[1024,64,64]{0,2,1:T(8,128)} %param.29, bf16[1024,64,64]{0,2,1:T(8,128)(2,1)} %param.30), kind=kLoop, calls=%fused_computation.6 | loop fusion | flops 67108864 | bytes 83886080 | tf_op jit(solution)/shard_map/convert_element_type | solution.py:212
  (165 shorter events, 7.2 us)
Async XLA Ops:
  7.2 5.3 copy-start.16
  7.2 6.7 %copy-start.19 = (f32[4,5,1,1]{1,0,3,2:T(4,128)S(1)}, f32[4,5,1,1]{1,0,3,2:T(4,128)}, u32[]{:S(2)}) copy-start(f32[4,5,1,1]{1,0,3,2:T(4,128)} %constant.441) | copy-start | bytes 244
  7.2 8.0 %copy-start.22 = (s32[1,256]{1,0:T(1,128)S(1)}, s32[1,256]{1,0:T(1,128)}, u32[]{:S(2)}) copy-start(s32[1,256]{1,0:T(1,128)} %param.26) | copy-start | bytes 3076
  7.2 8.0 %copy-start.21 = (f32[1,256]{1,0:T(1,128)S(1)}, f32[1,256]{1,0:T(1,128)}, u32[]{:S(2)}) copy-start(f32[1,256]{1,0:T(1,128)} %param.25) | copy-start | bytes 3076
  7.2 101.0 %reduce-scatter.3.cloned.1.call-start = ((), (), s32[]{:S(2)}) async-start(), calls=%async_computation.2 | async-start | bytes 1310720 | tf_op jit(solution)/shard_map/reduce_scatter | solution.py:250
  10.0 6.9 %collective-permute-start.1 = (f32[1,50,256]{2,0,1:T(1,128)S(1)}, f32[1,50,256]{2,0,1:T(1,128)S(1)}, u32[]{:S(2)}, u32[]{:S(2)}) collective-permute-start(f32[1,50,256]{2,0,1:T(1,128)S(1)} %bitcast.460), channel_id=1, source_target_pairs={{2,0},{4,2},{6,4},{3,1},{5,3},{7,5},{10,8},{12,10},{14,12},{11,9},... | collective-permute-start | bytes 153608 | tf_op jit(solution)/shard_map/ppermute | solution.py:37
  11.3 4.4 copy-start
  11.8 11.8 %copy-start.17 = (f32[5,5,1,1,256]{4,0,2,1,3:T(8,128)}, f32[5,5,1,1,256]{4,0,2,1,3:T(8,128)S(1)}, u32[]{:S(2)}) copy-start(f32[5,5,1,1,256]{4,0,2,1,3:T(8,128)S(1)} %fusion.243) | copy-start | bytes 76804
  12.8 2.6 copy-start.1
  13.8 11.2 %copy-start.14 = (f32[5,5,1,1,256]{4,0,2,1,3:T(8,128)}, f32[5,5,1,1,256]{4,0,2,1,3:T(8,128)S(1)}, u32[]{:S(2)}) copy-start(f32[5,5,1,1,256]{4,0,2,1,3:T(8,128)S(1)} %fusion.235) | copy-start | bytes 76804
  15.4 10.2 %copy-start.9 = (f32[5,5,5,1,256]{4,0,1,2,3:T(8,128)}, f32[5,5,5,1,256]{4,0,1,2,3:T(8,128)S(1)}, u32[]{:S(2)}) copy-start(f32[5,5,5,1,256]{4,0,1,2,3:T(8,128)S(1)} %get-tuple-element.158) | copy-start | bytes 384004
  17.0 6.6 %collective-permute-start = (f32[1,50,256]{2,0,1:T(1,128)S(1)}, f32[1,50,256]{2,0,1:T(1,128)S(1)}, u32[]{:S(2)}, u32[]{:S(2)}) collective-permute-start(f32[1,50,256]{2,0,1:T(1,128)S(1)} %bitcast.462), channel_id=1, source_target_pairs={{0,2},{2,4},{4,6},{1,3},{3,5},{5,7},{8,10},{10,12},{12,14},{9,11},... | collective-permute-start | bytes 153608 | tf_op jit(solution)/shard_map/ppermute | solution.py:36
  25.0 2.0 copy-start.11
  27.9 6.8 %collective-permute-start.3 = (f32[1,50,256]{2,0,1:T(1,128)S(1)}, f32[1,50,256]{2,0,1:T(1,128)S(1)}, u32[]{:S(2)}, u32[]{:S(2)}) collective-permute-start(f32[1,50,256]{2,0,1:T(1,128)S(1)} %bitcast.461), channel_id=1, source_target_pairs={{2,0},{4,2},{6,4},{3,1},{5,3},{7,5},{10,8},{12,10},{14,12},{11,9},... | collective-permute-start | bytes 153608 | tf_op jit(solution)/shard_map/ppermute | solution.py:37
  34.8 17.7 %collective-permute-start.2 = (f32[1,50,256]{2,0,1:T(1,128)S(1)}, f32[1,50,256]{2,0,1:T(1,128)S(1)}, u32[]{:S(2)}, u32[]{:S(2)}) collective-permute-start(f32[1,50,256]{2,0,1:T(1,128)S(1)} %bitcast.463), channel_id=1, source_target_pairs={{0,2},{2,4},{4,6},{1,3},{3,5},{5,7},{8,10},{10,12},{12,14},{9,11},... | collective-permute-start | bytes 153608 | tf_op jit(solution)/shard_map/ppermute | solution.py:36
  53.0 1.4 copy-start.3
  53.2 0.7 copy-start.7
  53.2 1.2 copy-start.5
  62.0 6.1 %collective-permute-start.4 = (bf16[2,4,4096]{2,1,0:T(4,128)(2,1)S(1)}, bf16[2,4,4096]{2,1,0:T(4,128)(2,1)S(1)}, u32[]{:S(2)}, u32[]{:S(2)}) collective-permute-start(bf16[2,4,4096]{2,1,0:T(4,128)(2,1)S(1)} %reshape.1145), channel_id=1, source_target_pairs={{0,8},{8,16},{16,24},{24,0},{1,9},{9,17},{17,25},{25,1},{2,10},{10... | collective-permute-start | bytes 196616 | tf_op jit(solution)/shard_map/ppermute | solution.py:44
  68.1 10.8 %copy-start.20 = (bf16[16,16]{0,1:T(8,128)(2,1)S(1)}, bf16[16,16]{0,1:T(8,128)(2,1)}, u32[]{:S(2)}) copy-start(bf16[16,16]{0,1:T(8,128)(2,1)} %constant.389) | copy-start | bytes 1540
  81.3 99.6 %reduce-scatter.5.cloned.1.call-start = ((), (), s32[]{:S(2)}) async-start(), calls=%async_computation.3 | async-start | bytes 1310720 | tf_op jit(solution)/shard_map/reduce_scatter | solution.py:250
  126.9 9.1 %copy-start.23 = (f32[64]{0:T(128)S(1)}, f32[64]{0:T(128)}, u32[]{:S(2)}) copy-start(f32[64]{0:T(128)} %param.28) | copy-start | bytes 772
  136.0 12.5 %copy-start.24 = (bf16[256,4096,1]{1,0,2:T(8,128)(2,1)S(1)}, bf16[256,4096,1]{1,0,2:T(8,128)(2,1)}, u32[]{:S(2)}) copy-start(bf16[256,4096,1]{1,0,2:T(8,128)(2,1)} %constant.442) | copy-start | bytes 6291460
  150.7 30.2 %copy-start.13 = (f32[1024,64]{0,1:T(8,128)S(1)}, f32[1024,64]{0,1:T(8,128)}, u32[]{:S(2)}) copy-start(f32[1024,64]{0,1:T(8,128)} %reduce-scatter.3.cloned.1.call-done) | copy-start | bytes 786436
  153.0 370.3 %all-reduce.10.cloned.1.call-start = ((), (), s32[]{:S(2)}) async-start(), calls=%async_computation.4 | async-start | bytes 33554432 | tf_op jit(solution)/shard_map/psum | solution.py:263
  190.2 0.9 copy-start.10
  190.2 1.1 copy-start.2
  190.2 1.1 copy-start.15
  190.2 1.1 copy-start.18
  190.2 1.4 copy-start.12
  190.2 1.7 copy-start.4
  190.3 1.9 copy-start.8
  190.3 2.0 copy-start.6
Sparse Core Ops, SparseCore 0:
  81.4 26.7 reduce-scatter.2
  153.1 27.7 reduce-scatter.4
  190.4 332.8 all-reduce.9
where the time goes:
time: 564 us; the launch traced here: 562 us
  waiting for transfers between devices  395 us (70%)
  other arithmetic  56.5 us (10%)
  matrix products  39.2 us (7%)
  starting transfers between devices  27 us (5%)
  local copies, waits for them, and re-layouts  18.4 us (3%)
  between operations  15.2 us (3%)
  blocking collectives  10.4 us (2%)
    psum x1, waiting for transfers between devices, per_device(): gradient = lax.psum(local_grad, ('grp', 'gy'))  328 us
    reduce_scatter x2, waiting for transfers between devices, coefficients(): lax.psum_scatter(partial_value, 'gx', scatter_dimension=0, tiled=True)  54.5 us
    convert_element_type x1, other arithmetic, adam_update(): second_moment.astype(jnp.bfloat16)  31.6 us
    ppermute x2, starting transfers between devices, extended(): before = lax.ppermute(last, axis, up)  22.5 us
    dot_general x2, matrix products, to_basis(): jnp.einsum('tcxp,qp->tcxq', field_values, table_yz, preferred_element_typ...  12.9 us
    dot_general x1, matrix products, backward(): jnp.einsum('toxp,o->txp', active, proj_weight, precision=HIGHEST)  12.4 us
  transfers between devices with their start and end apart: 8, of which 7 were waited for; matrix products, arithmetic and copies ran while one was open for 2% of the time, Pallas kernels for 0%

commit v1 on v0

v1 whole, which is shorter than its diff:
```python
import functools
import math

import jax
import jax.numpy as jnp
import ml_dtypes
import numpy as np
from jax import lax
from jax.experimental import pallas as pl
from jax.experimental.pallas import tpu as pltpu
from jax.sharding import PartitionSpec as P

KM = 16
TY = 64
TZ = 64
MODES = KM * KM * KM
JOINT = KM * KM
EZ = TZ // 4
LANES = 128
NODES = 125
PLANES = 4
CELLS = 16

HIGHEST = lax.Precision.HIGHEST
F32 = jnp.float32
BF16 = jnp.bfloat16
TIME_STEP = 0.02
FACE_GAIN = 10.0
LOSS_SCALE = 1.0 / 2048.0
LEARN_RATE = 0.001
BETA_ONE = 0.9
BETA_TWO = 0.999
BIAS_ONE = 1.0 - BETA_ONE**10
BIAS_TWO = 1.0 - BETA_TWO**10
EPSILON = 1e-08
GAUSS_NORM = 1.0 / math.sqrt(2.0 * math.pi)
VMEM_LIMIT = 48 * 1024 * 1024

TAIL_SCALE = 0.32
TAIL = (
    0.12766152875085093,
    0.12766094645791293,
    0.11462235951270612,
    0.08782909645624029,
    0.058653976831234717,
    -0.009377604773061265,
    0.065328090206421,
    -0.1467075324124934,
    0.09540730271922851,
    -0.021078179724135896,
)


def lagrange(nodes, column, target):
    value = 1.0
    for other in range(len(nodes)):
        if other != column:
            value = value * (target - nodes[other]) / (nodes[column] - nodes[other])
    return value


def lagrange_slope(nodes, column, target):
    total = 0.0
    for skipped in range(len(nodes)):
        if skipped != column:
            factor = 1.0 / (nodes[column] - nodes[skipped])
            for other in range(len(nodes)):
                if other != column and other != skipped:
                    factor = factor * (target - nodes[other]) / (nodes[column] - nodes[other])
            total = total + factor
    return total


def padded_to(matrix, shape):
    out = np.zeros(shape, np.float32)
    out[: matrix.shape[0], : matrix.shape[1]] = matrix
    return out


def solver_tables():
    nodes = [-1.0, -math.sqrt(3.0 / 7.0), 0.0, math.sqrt(3.0 / 7.0), 1.0]
    slopes = np.zeros((5, 5))
    interp = np.zeros((4, 5))
    for row in range(5):
        for column in range(5):
            slopes[row, column] = lagrange_slope(nodes, column, nodes[row])
    for sample in range(4):
        for column in range(5):
            interp[sample, column] = lagrange(nodes, column, -1.0 + (2.0 * sample + 1.0) / 4.0)
    slopes = slopes.astype(np.float32).astype(np.float64)
    interp = interp.astype(np.float32).astype(np.float64)
    eye = np.eye(5)
    along = (
        np.kron(slopes, np.eye(25)),
        np.kron(eye, np.kron(slopes, eye)),
        np.kron(np.eye(25), slopes),
    )
    square = [padded_to(-2.0 * m, (LANES, LANES)) for m in along]
    to_velocity = np.concatenate(square, axis=0)
    to_pressure = np.concatenate(square, axis=1)
    to_grid = padded_to(np.kron(interp, np.kron(interp, interp)), (64, LANES))
    faces = np.zeros((LANES, LANES), np.float32)
    index = np.arange(NODES)
    for direction, place in enumerate((index // 25, index // 5 % 5, index % 5)):
        faces[:NODES, 2 * direction] = np.where(place == 0, -FACE_GAIN, 0.0)
        faces[:NODES, 2 * direction + 1] = np.where(place == 4, FACE_GAIN, 0.0)
    return to_velocity, to_pressure, to_grid, faces


def fourier_table(length, kept):
    angles = np.arange(length) * (2.0 * math.pi / length)
    rows = []
    for k in range(kept // 2 + 1):
        factor = math.sqrt(1.0 / length) if k == 0 else math.sqrt(2.0 / length)
        rows.append(factor * np.cos(k * angles))
    for k in range(1, kept // 2):
        rows.append(math.sqrt(2.0 / length) * np.sin(k * angles))
    return np.stack(rows)


def rounded(table):
    return table.astype(np.float32).astype(ml_dtypes.bfloat16)


def joint_table():
    joined = rounded(np.kron(fourier_table(TY, KM), fourier_table(TZ, KM)))
    joined = joined.reshape(JOINT, TY // 4, 4, TZ // 4, 4)
    return np.ascontiguousarray(joined.transpose(0, 2, 4, 1, 3).reshape(JOINT, TY * TZ))


def params(**more):
    return pltpu.CompilerParams(vmem_limit_bytes=VMEM_LIMIT, **more)


SMEM_SPEC = pl.BlockSpec(memory_space=pltpu.SMEM)


def column_of(row):
    n = row.shape[1]
    square = jnp.broadcast_to(row, (n, n))
    at_row = lax.broadcasted_iota(jnp.int32, (n, n), 0)
    at_lane = lax.broadcasted_iota(jnp.int32, (n, n), 1)
    return jnp.sum(jnp.where(at_row == at_lane, square, 0.0), axis=1, keepdims=True)


def normal_parts(x):
    bell = jnp.exp(-0.5 * x * x)
    t = 1.0 / (1.0 + TAIL_SCALE * jnp.abs(x))
    tail = jnp.full_like(t, TAIL[-1])
    for factor in TAIL[-2::-1]:
        tail = tail * t + factor
    tail = tail * t * bell
    return jnp.where(x < 0.0, tail, 1.0 - tail), bell


def read_field(ref, field):
    start = 2 * NODES * field
    halves = [ref[pl.ds(start + h, NODES, stride=2), :] for h in range(2)]
    both = jnp.concatenate(halves, axis=1)
    return jnp.concatenate([both, jnp.zeros((LANES - NODES, both.shape[1]), F32)], axis=0)


def x_faces(pressure, velocity, up_ref, down_ref):
    up_ref[...] = pltpu.roll(pressure + velocity, 28, 0)[:32]
    down_ref[...] = (velocity - pressure)[:32]


def grid_values(to_grid, pressure):
    return lax.dot(to_grid, pressure, precision=HIGHEST, preferred_element_type=F32)


def rates(fields, sink, below, above, to_velocity, to_pressure, faces):
    pressure = fields[0]
    change = lax.dot(to_velocity, pressure, precision=HIGHEST, preferred_element_type=F32)
    rate = lax.dot(
        to_pressure, jnp.concatenate(fields[1:], axis=0), precision=HIGHEST, preferred_element_type=F32
    )
    cells = pressure.shape[1]
    cell = lax.broadcasted_iota(jnp.int32, (1, cells), 1)
    depth = cell & (EZ - 1)
    velocity_rates = []
    for d in range(3):
        velocity = fields[1 + d]
        up = velocity + pressure
        down = velocity - pressure
        if d == 0:
            pad = jnp.zeros((LANES - 32, cells), F32)
            from_low = jnp.concatenate([below, pad], axis=0)
            from_high = pltpu.roll(jnp.concatenate([above, pad], axis=0), 100, 0)
        else:
            nodes, step = ((20, EZ), (4, 1))[d - 1]
            from_low = pltpu.roll(pltpu.roll(up, LANES - nodes, 0), step, 1)
            from_high = pltpu.roll(pltpu.roll(down, nodes, 0), cells - step, 1)
            first = cell < EZ if d == 1 else depth == 0
            last = cell >= cells - EZ if d == 1 else depth == EZ - 1
            from_low = jnp.where(first, 0.0, from_low)
            from_high = jnp.where(last, 0.0, from_high)
        low = faces[:, 2 * d : 2 * d + 1] * (up - from_low)
        high = faces[:, 2 * d + 1 : 2 * d + 2] * (down - from_high)
        rate = rate + (low + high)
        velocity_rates.append(change[d * LANES : (d + 1) * LANES] + (low - high))
    return [r - sink * q for r, q in zip([rate] + velocity_rates, fields)]


def lift_kernel(half, with_faces, state_ref, gain_ref, to_grid_ref, table_ref, out_ref, *more):
    pressure = read_field(state_ref, 0)
    if with_faces:
        up_ref, down_ref = more[:2]
        x_faces(pressure, read_field(state_ref, 1), up_ref, down_ref)
    planes = out_ref.shape[0]
    rows = planes * CELLS
    grid = grid_values(to_grid_ref[half * rows : (half + 1) * rows, :], pressure)
    grid = grid.astype(BF16).astype(F32)
    gain = column_of(gain_ref[...])
    cells = grid.shape[1]
    total = jnp.zeros((planes * gain.shape[0], JOINT), F32)
    for j in range(CELLS):
        parts = []
        for k in range(planes):
            at = k * CELLS + j
            scaled = gain * grid[at : at + 1, :]
            parts.append((scaled * normal_parts(scaled)[0]).astype(BF16))
        lifted = jnp.concatenate(parts, axis=0)
        total = total + jnp.dot(
            lifted, table_ref[j * cells : (j + 1) * cells, :], preferred_element_type=F32
        )
    for k in range(planes):
        out_ref[k] = total[k * gain.shape[0] : (k + 1) * gain.shape[0]]


def first_stage_kernel(
    state_ref, below_ref, above_ref, mask_ref, damping_ref, vel_ref, pre_ref, faces_ref,
    mid_ref, up_ref, down_ref,
):
    fields = [read_field(state_ref, f) for f in range(4)]
    sink = mask_ref[...].astype(F32) * damping_ref[...]
    rate = rates(
        fields, sink, below_ref[...], above_ref[...], vel_ref[...], pre_ref[...], faces_ref[...]
    )
    mid = [q + TIME_STEP * r for q, r in zip(fields, rate)]
    for f in range(4):
        mid_ref[f] = mid[f]
    x_faces(mid[0], mid[1], up_ref, down_ref)


def second_stage_kernel(
    state_ref, mid_ref, below_ref, above_ref, mask_ref, damping_ref, vel_ref, pre_ref, faces_ref,
    to_grid_ref, new_ref, target_ref,
):
    mid = [mid_ref[f] for f in range(4)]
    sink = mask_ref[...].astype(F32) * damping_ref[...]
    rate = rates(
        mid, sink, below_ref[...], above_ref[...], vel_ref[...], pre_ref[...], faces_ref[...]
    )
    for f in range(4):
        new = 0.5 * (read_field(state_ref, f) + mid[f] + TIME_STEP * rate[f])
        for h in range(2):
            new_ref[pl.ds(2 * NODES * f + h, NODES, stride=2), :] = new[
                :NODES, h * LANES : (h + 1) * LANES
            ]
        if f == 0:
            target_ref[...] = grid_values(to_grid_ref[...], new).astype(BF16).astype(F32)


def owned(me, modes):
    if modes >= JOINT:
        return me * (modes // JOINT), modes // JOINT, None
    per = JOINT // modes
    return me // per, 1, pl.multiple_of(lax.rem(me, per) * modes, modes)


def sum_over_x(me_ref, fx_ref, gathered, halves, out_ref):
    me = me_ref[0]
    modes = out_ref.shape[1]
    first, count, offset = owned(me, modes)
    width = min(modes, JOINT)
    totals = [None] * count
    for slab, read in gathered(me):
        for h in range(halves):
            for k in range(PLANES // halves):
                block = read(h, k, offset, width)
                x = PLANES * slab + h * (PLANES // halves) + k
                for i in range(count):
                    term = fx_ref[first + i, x] * block
                    totals[i] = term if totals[i] is None else totals[i] + term
    for i in range(count):
        out_ref[:, i * width : (i + 1) * width] = totals[i]


def gathered_planes(refs, count, halves):
    def walk(me):
        per = len(refs) // halves
        if per == count:
            for b in range(count):
                slab = lax.rem(me + (count - b), count)

                def read(h, k, offset, width, b=b):
                    ref = refs[h * per + b]
                    return ref[k] if offset is None else ref[k, :, pl.ds(offset, width)]

                yield slab, read
        else:
            for b in range(count):

                def read(h, k, offset, width, b=b):
                    ref = refs[h]
                    return ref[b, k] if offset is None else ref[b, k, :, pl.ds(offset, width)]

                yield b, read

    return walk


def mix_kernel(count, halves, me_ref, fx_ref, *refs):
    parts = refs[:-4]
    spectral_ref, coeffs_ref, mixed_ref, total_ref = refs[-4:]
    step = pl.program_id(0)

    @pl.when(step == 0)
    def _():
        sum_over_x(me_ref, fx_ref, gathered_planes(parts, count, halves), halves, coeffs_ref)
        total_ref[...] = jnp.zeros_like(total_ref)

    block = spectral_ref.shape[0]
    modes = total_ref.shape[1]

    @pl.loop(0, modes // LANES)
    def _(tile):
        at = pl.ds(pl.multiple_of(tile * LANES, LANES), LANES)
        total = total_ref[:, at]
        rows = coeffs_ref[pl.ds(pl.multiple_of(step * block, block), block), at]
        for c in range(block):
            total = total + rows[c : c + 1] * spectral_ref[c, :, at]
        total_ref[:, at] = total

    @pl.when(step == pl.num_programs(0) - 1)
    def _():
        mixed_ref[...] = total_ref[...].astype(BF16)


def coeffs_kernel(count, halves, me_ref, fx_ref, *refs):
    sum_over_x(me_ref, fx_ref, gathered_planes(refs[:-1], count, halves), halves, refs[-1])


def backward_kernel(count, half, me_ref, fx_ref, *refs):
    parts = refs[:-6]
    weight_ref, target_ref, forward_ref, table_ref, out_ref, along_ref = refs[-6:]
    me = me_ref[0]
    planes, channels = out_ref.shape[:2]
    modes = parts[0].shape[-1]
    width = min(modes, JOINT)
    along_ref[...] = jnp.zeros_like(along_ref)
    for b in range(count):
        if len(parts) == count:
            ref, slab = parts[b], lax.rem(me + (count - b), count)
        else:
            ref, slab = parts[0].at[b], b
        first, functions, offset = owned(slab, modes)
        for i in range(functions):
            block = ref[:, i * width : (i + 1) * width].astype(F32)
            for k in range(planes):
                x = PLANES * me + half * planes + k
                at = (pl.ds(k * channels, channels), slice(None) if offset is None else pl.ds(offset, width))
                along_ref[at] += fx_ref[first + i, x] * block
    along = along_ref[...]
    high = along.astype(BF16)
    rest = along - high.astype(F32)
    middle = rest.astype(BF16)
    low = (rest - middle.astype(F32)).astype(BF16)
    thirds = jnp.concatenate([high, middle, low], axis=0)
    weight = column_of(weight_ref[...])
    rows = planes * channels
    cells = target_ref.shape[1]
    total = jnp.zeros((rows, JOINT), F32)
    for j in range(CELLS):
        spread = jnp.dot(
            thirds, forward_ref[:, j * cells : (j + 1) * cells], preferred_element_type=F32
        )
        parts_of = []
        for k in range(planes):
            r = k * channels
            pre = (
                spread[2 * rows + r : 2 * rows + r + channels]
                + spread[rows + r : rows + r + channels]
            ) + spread[r : r + channels]
            phi, bell = normal_parts(pre)
            predicted = jnp.sum(pre * phi * weight, axis=0, keepdims=True)
            at = (half * planes + k) * CELLS + j
            misfit = 2.0 * LOSS_SCALE * (predicted - target_ref[at : at + 1, :])
            slope = phi + pre * bell * GAUSS_NORM
            parts_of.append((misfit * weight * slope).astype(BF16))
        total = total + jnp.dot(
            jnp.concatenate(parts_of, axis=0),
            table_ref[j * cells : (j + 1) * cells, :],
            preferred_element_type=F32,
        )
    for k in range(planes):
        out_ref[k] = total[k * channels : (k + 1) * channels]


def update_kernel(tiles, chained, *refs):
    coeffs, grads = refs[:tiles], refs[tiles : 2 * tiles]
    spectral_ref, one_ref, two_ref = refs[2 * tiles : 2 * tiles + 3]
    new_ref, new_one_ref, new_two_ref = refs[-3:]
    block, width, modes = spectral_ref.shape

    @pl.loop(0, modes // LANES)
    def _(tile):
        at = pl.ds(pl.multiple_of(tile * LANES, LANES), LANES)
        held = [g[:, at] for g in grads]
        for c in range(block):
            gradient = coeffs[0][c : c + 1, at] * held[0]
            for t in range(1, tiles):
                gradient = gradient + coeffs[t][c : c + 1, at] * held[t]
            first = BETA_ONE * one_ref[c, :, at].astype(F32) + (1.0 - BETA_ONE) * gradient
            second = (
                BETA_TWO * two_ref[c, :, at].astype(F32) + (1.0 - BETA_TWO) * gradient * gradient
            )
            denominator = jnp.sqrt(second * (1.0 / BIAS_TWO)) + EPSILON
            new_ref[c, :, at] = spectral_ref[c, :, at] - (LEARN_RATE / BIAS_ONE) * first / denominator
            new_one_ref[c, :, at] = first.astype(BF16)
            new_two_ref[c, :, at] = second.astype(BF16)


def from_ring(array, axis):
    count = lax.axis_size(axis)
    if count > 8:
        return [lax.all_gather(array, axis)]
    return [array] + [
        lax.ppermute(array, axis, [(i, (i + b) % count) for i in range(count)])
        for b in range(1, count)
    ]


def of_every_tile(array):
    behind = from_ring(array, "grp")
    count = lax.axis_size("gy")
    for b in range(1, count):
        behind = behind + [
            lax.ppermute(a, "gy", [(i, (i + b) % count) for i in range(count)])
            for a in behind[: lax.axis_size("grp")]
        ]
    return behind


def from_sides(up, down):
    count = lax.axis_size("gx")
    below = lax.ppermute(up, "gx", [(i, i + 1) for i in range(count - 1)])
    above = lax.ppermute(down, "gx", [(i + 1, i) for i in range(count - 1)])
    return below, above


HALVES = 2
MIX_BLOCK = 8
UPDATE_BLOCK = 16
UPDATE_CHUNKS = 4


def per_device(
    state, damping, absorb_mask, lift_gain, proj_weight, spectral, moment_one, moment_two
):
    count = lax.axis_size("gx")
    cells = state.shape[-1]
    channels = lift_gain.shape[0]
    modes = spectral.shape[0]
    planes = PLANES // HALVES
    to_velocity, to_pressure, to_grid, faces = (jnp.asarray(t) for t in solver_tables())
    joint = joint_table()
    forward = jnp.asarray(joint)
    table = jnp.asarray(np.ascontiguousarray(joint.T))
    fx = jnp.asarray(rounded(fourier_table(PLANES * count, KM)).astype(np.float32))
    me = lax.axis_index("gx").astype(jnp.int32).reshape(1)
    flat = state.reshape(-1, LANES)
    gain_row = lift_gain.reshape(1, channels)
    weight_row = proj_weight.reshape(1, channels)
    spectral_t, one_t, two_t = (
        jnp.transpose(a, (1, 2, 0)) for a in (spectral, moment_one, moment_two)
    )
    face = jax.ShapeDtypeStruct((32, cells), F32)
    half_planes = jax.ShapeDtypeStruct((planes, channels, JOINT), F32)

    def lift(half):
        return pl.pallas_call(
            functools.partial(lift_kernel, half, half == 0),
            out_shape=[half_planes] + ([face, face] if half == 0 else []),
            compiler_params=params(),
            name=f"lift_{half}",
        )(flat, gain_row, to_grid, table)

    lifted, up, down = lift(0)
    gathered = [from_ring(lifted, "gx")]
    below, above = from_sides(up, down)
    for half in range(1, HALVES):
        gathered.append(from_ring(lift(half)[0], "gx"))
    mid, up, down = pl.pallas_call(
        first_stage_kernel,
        out_shape=[jax.ShapeDtypeStruct((4, LANES, cells), F32), face, face],
        compiler_params=params(),
        name="first_stage",
    )(flat, below, above, absorb_mask, damping, to_velocity, to_pressure, faces)
    below, above = from_sides(up, down)

    flat_parts = [a for half in gathered for a in half]
    whole = [pl.BlockSpec(a.shape, lambda i, n=a.ndim: (0,) * n) for a in flat_parts]
    coeffs, mixed = pl.pallas_call(
        functools.partial(mix_kernel, count, HALVES),
        grid=(channels // MIX_BLOCK,),
        in_specs=[SMEM_SPEC, SMEM_SPEC]
        + whole
        + [pl.BlockSpec((MIX_BLOCK, channels, modes), lambda i: (i, 0, 0))],
        out_specs=[pl.BlockSpec((channels, modes), lambda i: (0, 0))] * 2,
        out_shape=[
            jax.ShapeDtypeStruct((channels, modes), F32),
            jax.ShapeDtypeStruct((channels, modes), BF16),
        ],
        scratch_shapes=[pltpu.VMEM((channels, modes), F32)],
        compiler_params=params(dimension_semantics=("arbitrary",)),
        name="mix",
    )(me, fx, *flat_parts, spectral_t)
    every_mixed = from_ring(mixed, "gx")
    every_coeffs = of_every_tile(coeffs)

    new_flat, target = pl.pallas_call(
        second_stage_kernel,
        out_shape=[
            jax.ShapeDtypeStruct(flat.shape, F32),
            jax.ShapeDtypeStruct((PLANES * CELLS, cells), F32),
        ],
        compiler_params=params(),
        name="second_stage",
    )(
        flat, mid, below, above, absorb_mask, damping, to_velocity, to_pressure, faces, to_grid
    )

    vmem = pl.BlockSpec(memory_space=pltpu.VMEM)
    gathered = []
    for half in range(HALVES):
        (back,) = pl.pallas_call(
            functools.partial(backward_kernel, count, half),
            in_specs=[SMEM_SPEC, SMEM_SPEC] + [vmem] * (len(every_mixed) + 4),
            out_shape=[half_planes],
            scratch_shapes=[pltpu.VMEM((planes * channels, JOINT), F32)],
            compiler_params=params(),
            name=f"backward_{half}",
        )(me, fx, *every_mixed, weight_row, target, forward, table)
        gathered.append(from_ring(back, "gx"))
    flat_parts = [a for half in gathered for a in half]
    grad_coeffs = pl.pallas_call(
        functools.partial(coeffs_kernel, count, HALVES),
        in_specs=[SMEM_SPEC, SMEM_SPEC] + [vmem] * len(flat_parts),
        out_shape=jax.ShapeDtypeStruct((channels, modes), F32),
        compiler_params=params(),
        name="grad_coeffs",
    )(me, fx, *flat_parts)

    width = channels // UPDATE_CHUNKS
    tiles = len(every_coeffs)
    outs = None
    for chunk in range(UPDATE_CHUNKS):
        grads = of_every_tile(grad_coeffs[chunk * width : (chunk + 1) * width])
        cube = pl.BlockSpec((UPDATE_BLOCK, width, modes), lambda i, chunk=chunk: (i, chunk, 0))
        anywhere = pl.BlockSpec(memory_space=pl.ANY)
        given = [*every_coeffs, *grads, spectral_t, one_t, two_t]
        specs = [pl.BlockSpec((UPDATE_BLOCK, modes), lambda i: (i, 0))] * tiles
        specs += [pl.BlockSpec((width, modes), lambda i: (0, 0))] * tiles + [cube] * 3
        aliases = {}
        if outs is not None:
            aliases = {len(given) + k: k for k in range(3)}
            given += outs
            specs += [anywhere] * 3
        outs = pl.pallas_call(
            functools.partial(update_kernel, tiles, outs is not None),
            grid=(channels // UPDATE_BLOCK,),
            in_specs=specs,
            out_specs=[cube] * 3,
            out_shape=[
                jax.ShapeDtypeStruct(spectral_t.shape, F32),
                jax.ShapeDtypeStruct(spectral_t.shape, BF16),
                jax.ShapeDtypeStruct(spectral_t.shape, BF16),
            ],
            input_output_aliases=aliases,
            compiler_params=params(dimension_semantics=("arbitrary",)),
            name=f"update_{chunk}",
        )(*given)
    new_spectral, new_one, new_two = (jnp.transpose(a, (2, 0, 1)) for a in outs)
    return new_flat.reshape(state.shape), new_spectral, new_one, new_two


def solution(mesh):
    in_specs = (
        P(("grp", "gy"), None, None, "gx", None),
        P("gx", None),
        P("gx", None),
        P(),
        P(),
        P("gx", None, None),
        P("gx", None, None),
        P("gx", None, None),
    )
    out_specs = (
        P(("grp", "gy"), None, None, "gx", None),
        P("gx", None, None),
        P("gx", None, None),
        P("gx", None, None),
    )
    return jax.shard_map(
        per_device, mesh=mesh, in_specs=in_specs, out_specs=out_specs, check_vma=False
    )
```

time: 564 us -> 169 us (0.30)
  waiting for transfers between devices: 395 us -> 29.2 us
  Pallas kernels: 0 us -> 67.6 us
  other arithmetic: 56.5 us -> 0 us
  matrix products: 39.2 us -> 0 us
  starting transfers between devices: 27 us -> 66 us
  between operations: 15.2 us -> 0.91 us
  local copies, waits for them, and re-layouts: 18.4 us -> 4.81 us
  blocking collectives: 10.4 us -> 0 us
    psum x1 -> x0, waiting for transfers between devices: 328 us -> none  [per_device(): gradient = lax.psum(local_grad, ('grp', 'gy'))]
    pallas_call x0 -> x12, Pallas kernels: none -> 67.6 us  [the longest x4 39.8 us: per_device(): pl.pallas_call(functools.partial(update_kernel, tiles, outs is not None),...]
    reduce_scatter x2 -> x0, waiting for transfers between devices: 54.5 us -> none  [coefficients(): lax.psum_scatter(partial_value, 'gx', scatter_dimension=0, tiled=True)]
    ppermute x5 -> x54, starting transfers between devices: 26.7 us -> 66 us  [the longest x30 52.7 us: from_ring(): lax.ppermute(array, axis, [(i, (i + b) % count) for i in range(count)])]
    dot_general x25 -> x0, matrix products: 39.2 us -> none  [the longest x2 12.9 us: to_basis(): jnp.einsum('tcxp,qp->tcxq', field_values, table_yz, preferred_element_typ...]
    convert_element_type x2 -> x0, other arithmetic: 31.7 us -> none  [the longest x1 31.6 us: adam_update(): second_moment.astype(jnp.bfloat16)]
    dot_general x2 -> x0, other arithmetic: 17.3 us -> none  [the longest x1 9.34 us: per_device(): jnp.einsum('mtc,mto->mco', coeffs, grad_coeffs, precision=HIGHEST)]
    ppermute x5 -> x54, waiting for transfers between devices: 12.1 us -> 29.2 us  [the longest x30 17.9 us: from_ring(): lax.ppermute(array, axis, [(i, (i + b) % count) for i in range(count)])]
  transfers between devices with their start and end apart: 8 -> 54, of which waited for: 7 -> 16; matrix products, arithmetic and copies ran while one was open for 2% -> 0% of each run, Pallas kernels for 0% -> 24%
where the time goes in v1:
time: 169 us; the launch traced here: 168 us
  Pallas kernels  67.6 us (40%)
  starting transfers between devices  66 us (39%)
  waiting for transfers between devices  29.2 us (17%)
  local copies, waits for them, and re-layouts  4.81 us (3%)
    ppermute x30, starting transfers between devices, from_ring(): lax.ppermute(array, axis, [(i, (i + b) % count) for i in range(count)])  52.7 us
    pallas_call x4, Pallas kernels, per_device(): pl.pallas_call(functools.partial(update_kernel, tiles, outs is not None),...  39.8 us
    ppermute x30, waiting for transfers between devices, from_ring(): lax.ppermute(array, axis, [(i, (i + b) % count) for i in range(count)])  17.9 us
    pallas_call x1, Pallas kernels, per_device(): pl.pallas_call(functools.partial(mix_kernel, count, HALVES), grid=(channe...  9.77 us
    pallas_call x2, Pallas kernels, per_device(): pl.pallas_call(functools.partial(backward_kernel, count, half), in_specs=...  9.08 us
    ppermute x2, waiting for transfers between devices, from_sides(): above = lax.ppermute(down, 'gx', [(i + 1, i) for i in range(count - 1)])  8.46 us
    ppermute x2, starting transfers between devices, from_sides(): below = lax.ppermute(up, 'gx', [(i, i + 1) for i in range(count - 1)])  6.77 us
    pallas_call x2, Pallas kernels, lift(): pl.pallas_call(functools.partial(lift_kernel, half, half == 0), out_shape...  5.27 us
  transfers between devices with their start and end apart: 54, of which 16 were waited for; matrix products, arithmetic and copies ran while one was open for 0% of the time, Pallas kernels for 24%

profile of v1, /device:TPU:0, one launch (start us, length us, event | category | flops | bytes accessed | tf_op | source)
XLA Modules:
  0.0 168.4 jit_solution(1420834953287107253)
XLA Ops:
  0.6 1.6 copy-done
  2.2 1.0 copy-done.3
  4.7 2.6 %lift_0.1 = (f32[2,64,256]{2,1,0:T(8,128)S(1)}, f32[32,256]{1,0:T(8,128)S(1)}, f32[32,256]{1,0:T(8,128)S(1)}) custom-call(f32[1000,128]{1,0:T(8,128)S(1)} %bitcast.11, f32[1,64]{1,0:T(1,128)S(1)} %bitcast.15, f32[64,128]{1,0:T(8,128)S(1)} %copy-done.7, bf16[4096,256]{1,0:T(8,128)(2,1)S(1)} %copy-done), custom_call_target="tpu_custom_call" | custom-call | tf_op jit(solution)/shard_map/lift_0/pallas_call | solution.py:483
  7.3 3.0 %collective-permute-start.4 = (f32[2,64,256]{2,1,0:T(8,128)S(1)}, f32[2,64,256]{2,1,0:T(8,128)S(1)}, u32[]{:S(2)}, u32[]{:S(2)}) collective-permute-start(f32[2,64,256]{2,1,0:T(8,128)S(1)} %get-tuple-element.32.refs_0_), channel_id=1, source_target_pairs={{0,2},{2,4},{4,6},{6,0},{1,3},{3,5},{5,7},{7,1},{8,10},{10,12},{12... | collective-permute-start | bytes 393224 | tf_op jit(solution)/shard_map/ppermute | solution.py:430
  10.3 1.5 collective-permute-start.5
  11.8 1.4 collective-permute-start.6
  13.2 2.6 %lift_1.1.refs_4_ = f32[2,64,256]{2,1,0:T(8,128)S(1)} custom-call(f32[1000,128]{1,0:T(8,128)S(1)} %bitcast.12, f32[1,64]{1,0:T(1,128)S(1)} %bitcast.16, f32[64,128]{1,0:T(8,128)S(1)} %copy-done.7, bf16[4096,256]{1,0:T(8,128)(2,1)S(1)} %copy-done), custom_call_target="tpu_custom_call" | custom-call | tf_op jit(solution)/shard_map/lift_1/pallas_call | solution.py:483
  17.0 1.9 %collective-permute-start.9 = (f32[2,64,256]{2,1,0:T(8,128)S(1)}, f32[2,64,256]{2,1,0:T(8,128)S(1)}, u32[]{:S(2)}, u32[]{:S(2)}) collective-permute-start(f32[2,64,256]{2,1,0:T(8,128)S(1)} %lift_1.1.refs_4_), channel_id=1, source_target_pairs={{0,6},{2,0},{4,2},{6,4},{1,7},{3,1},{5,3},{7,5},{8,14},{10,8},{12,... | collective-permute-start | bytes 393224 | tf_op jit(solution)/shard_map/ppermute | solution.py:430
  18.9 3.8 %collective-permute-done.7.refs_5_ = f32[2,64,256]{2,1,0:T(8,128)S(1)} collective-permute-done((f32[2,64,256]{2,1,0:T(8,128)S(1)}, f32[2,64,256]{2,1,0:T(8,128)S(1)}, u32[]{:S(2)}, u32[]{:S(2)}) %collective-permute-start.7) | collective-permute-done | bytes 131104 | tf_op jit(solution)/shard_map/ppermute | solution.py:430
  24.2 9.8 %mix.1 = (f32[64,1024]{1,0:T(8,128)S(1)}, bf16[64,1024]{1,0:T(8,128)(2,1)S(1)}) custom-call(s32[1]{0:T(128)} %bitcast.3.me_ref, f32[16,16]{1,0:T(8,128)S(1)} %copy-done.10, f32[2,64,256]{2,1,0:T(8,128)S(1)} %get-tuple-element.32.refs_0_, f32[2,64,256]{2,1,0:T(8,128)S(1)} %collective-permute-done.4.refs_1_, f32[2,64,256]{2,1,0:T(8,128)S(1)} %collective-permute-done.5.refs_2_, ...), custom_call_target="tpu_custom_call" | custom-call | tf_op jit(solution)/shard_map/mix/pallas_call | solution.py:505
  34.0 2.0 %collective-permute-start.17 = (bf16[64,1024]{1,0:T(8,128)(2,1)S(1)}, bf16[64,1024]{1,0:T(8,128)(2,1)S(1)}, u32[]{:S(2)}, u32[]{:S(2)}) collective-permute-start(bf16[64,1024]{1,0:T(8,128)(2,1)S(1)} %get-tuple-element.34.refs_0_), channel_id=1, source_target_pairs={{0,2},{2,4},{4,6},{6,0},{1,3},{3,5},{5,7},{7,1},{8,10},{10,12},{12... | collective-permute-start | bytes 393224 | tf_op jit(solution)/shard_map/ppermute | solution.py:430
  36.0 1.2 collective-permute-start.18
  37.2 1.3 collective-permute-start.19
  38.4 2.7 %collective-permute-start = (f32[32,256]{1,0:T(8,128)S(1)}, f32[32,256]{1,0:T(8,128)S(1)}, u32[]{:S(2)}, u32[]{:S(2)}) collective-permute-start(f32[32,256]{1,0:T(8,128)S(1)} %get-tuple-element.26), channel_id=1, source_target_pairs={{0,2},{2,4},{4,6},{1,3},{3,5},{5,7},{8,10},{10,12},{12,14},{9,11},... | collective-permute-start | bytes 98312 | tf_op jit(solution)/shard_map/ppermute | solution.py:448
  41.1 1.3 collective-permute-start.1
  42.7 4.2 %collective-permute-done.1.above_ref = f32[32,256]{1,0:T(8,128)S(1)} collective-permute-done((f32[32,256]{1,0:T(8,128)S(1)}, f32[32,256]{1,0:T(8,128)S(1)}, u32[]{:S(2)}, u32[]{:S(2)}) %collective-permute-start.1) | collective-permute-done | bytes 32800 | tf_op jit(solution)/shard_map/ppermute | solution.py:449
  47.8 4.1 %collective-permute-start.2 = (f32[32,256]{1,0:T(8,128)S(1)}, f32[32,256]{1,0:T(8,128)S(1)}, u32[]{:S(2)}, u32[]{:S(2)}) collective-permute-start(f32[32,256]{1,0:T(8,128)S(1)} %get-tuple-element.29), channel_id=1, source_target_pairs={{0,2},{2,4},{4,6},{1,3},{3,5},{5,7},{8,10},{10,12},{12,14},{9,11},... | collective-permute-start | bytes 98312 | tf_op jit(solution)/shard_map/ppermute | solution.py:448
  51.9 1.5 collective-permute-start.3
  53.5 4.2 %collective-permute-done.3.above_ref = f32[32,256]{1,0:T(8,128)S(1)} collective-permute-done((f32[32,256]{1,0:T(8,128)S(1)}, f32[32,256]{1,0:T(8,128)S(1)}, u32[]{:S(2)}, u32[]{:S(2)}) %collective-permute-start.3) | collective-permute-done | bytes 32800 | tf_op jit(solution)/shard_map/ppermute | solution.py:449
  57.7 1.7 %second_stage.1 = (f32[1000,128]{1,0:T(8,128)}, f32[64,256]{1,0:T(8,128)S(1)}) custom-call(f32[1000,128]{1,0:T(8,128)S(1)} %bitcast.14, f32[4,128,256]{2,1,0:T(8,128)S(1)} %get-tuple-element.28.mid_ref, f32[32,256]{1,0:T(8,128)S(1)} %collective-permute-done.2.below_ref, f32[32,256]{1,0:T(8,128)S(1)} %collective-permute-done.3.above_ref, ...), custom_call_target="tpu_custom_call" | custom-call | tf_op jit(solution)/shard_map/second_stage/pallas_call | solution.py:523
  59.5 4.5 %backward_1.1.refs_4_ = f32[2,64,256]{2,1,0:T(8,128)S(1)} custom-call(s32[1]{0:T(128)} %bitcast.3.me_ref, f32[16,16]{1,0:T(8,128)S(1)} %copy-done.10, bf16[64,1024]{1,0:T(8,128)(2,1)S(1)} %get-tuple-element.34.refs_0_, bf16[64,1024]{1,0:T(8,128)(2,1)S(1)} %collective-permute-done.17.refs_1_, bf16[64,1024]{1,0:T(8,128)(2,1)S(1)} %collective-permute-done.18.refs_2_, ...), custom_call_target="tpu_custom_call" | custom-call | tf_op jit(solution)/shard_map/backward_1/pallas_call | solution.py:538
  64.1 1.1 collective-permute-start.23
  65.1 1.9 %collective-permute-start.25 = (f32[2,64,256]{2,1,0:T(8,128)S(1)}, f32[2,64,256]{2,1,0:T(8,128)S(1)}, u32[]{:S(2)}, u32[]{:S(2)}) collective-permute-start(f32[2,64,256]{2,1,0:T(8,128)S(1)} %backward_1.1.refs_4_), channel_id=1, source_target_pairs={{0,6},{2,0},{4,2},{6,4},{1,7},{3,1},{5,3},{7,5},{8,14},{10,8},{12,... | collective-permute-start | bytes 393224 | tf_op jit(solution)/shard_map/ppermute | solution.py:430
  67.0 4.5 %backward_0.1.refs_0_ = f32[2,64,256]{2,1,0:T(8,128)S(1)} custom-call(s32[1]{0:T(128)} %bitcast.3.me_ref, f32[16,16]{1,0:T(8,128)S(1)} %copy-done.10, bf16[64,1024]{1,0:T(8,128)(2,1)S(1)} %get-tuple-element.34.refs_0_, bf16[64,1024]{1,0:T(8,128)(2,1)S(1)} %collective-permute-done.17.refs_1_, bf16[64,1024]{1,0:T(8,128)(2,1)S(1)} %collective-permute-done.18.refs_2_, ...), custom_call_target="tpu_custom_call" | custom-call | tf_op jit(solution)/shard_map/backward_0/pallas_call | solution.py:538
  72.2 1.6 collective-permute-start.21
  73.8 2.8 %collective-permute-start.22 = (f32[2,64,256]{2,1,0:T(8,128)S(1)}, f32[2,64,256]{2,1,0:T(8,128)S(1)}, u32[]{:S(2)}, u32[]{:S(2)}) collective-permute-start(f32[2,64,256]{2,1,0:T(8,128)S(1)} %backward_0.1.refs_0_), channel_id=1, source_target_pairs={{0,6},{2,0},{4,2},{6,4},{1,7},{3,1},{5,3},{7,5},{8,14},{10,8},{12,... | collective-permute-start | bytes 393224 | tf_op jit(solution)/shard_map/ppermute | solution.py:430
  76.6 1.6 collective-permute-start.10
  78.2 2.6 %collective-permute-start.11 = (f32[64,1024]{1,0:T(8,128)S(1)}, f32[64,1024]{1,0:T(8,128)S(1)}, u32[]{:S(2)}, u32[]{:S(2)}) collective-permute-start(f32[64,1024]{1,0:T(8,128)S(1)} %get-tuple-element.33.refs_0_), channel_id=1, source_target_pairs={{0,16},{8,24},{16,0},{24,8},{1,17},{9,25},{17,1},{25,9},{2,18},{10... | collective-permute-start | bytes 786440 | tf_op jit(solution)/shard_map/ppermute | solution.py:430
  80.8 1.3 collective-permute-start.12
  82.1 1.0 grad_coeffs.1
  83.9 3.0 %collective-permute-done.10.refs_1_ = f32[64,1024]{1,0:T(8,128)S(1)} collective-permute-done((f32[64,1024]{1,0:T(8,128)S(1)}, f32[64,1024]{1,0:T(8,128)S(1)}, u32[]{:S(2)}, u32[]{:S(2)}) %collective-permute-start.10) | collective-permute-done | bytes 262176 | tf_op jit(solution)/shard_map/ppermute | solution.py:430
  86.9 9.5 %collective-permute-start.48 = (f32[16,1024]{1,0:T(8,128)S(1)}, f32[16,1024]{1,0:T(8,128)S(1)}, u32[]{:S(2)}, u32[]{:S(2)}) collective-permute-start(f32[16,1024]{1,0:T(8,128)S(1)} %get-tuple-element.56.refs_8_), channel_id=1, source_target_pairs={{0,16},{8,24},{16,0},{24,8},{1,17},{9,25},{17,1},{25,9},{2,18},{10... | collective-permute-start | bytes 196616 | tf_op jit(solution)/shard_map/ppermute | solution.py:430
  96.5 5.1 %collective-permute-start.49 = (f32[16,1024]{1,0:T(8,128)S(1)}, f32[16,1024]{1,0:T(8,128)S(1)}, u32[]{:S(2)}, u32[]{:S(2)}) collective-permute-start(f32[16,1024]{1,0:T(8,128)S(1)} %get-tuple-element.56.refs_8_), channel_id=1, source_target_pairs={{0,24},{8,0},{16,8},{24,16},{1,25},{9,1},{17,9},{25,17},{2,26},{10... | collective-permute-start | bytes 196616 | tf_op jit(solution)/shard_map/ppermute | solution.py:430
  101.6 1.1 collective-permute-start.40
  102.9 2.5 %collective-permute-start.42 = (f32[16,1024]{1,0:T(8,128)S(1)}, f32[16,1024]{1,0:T(8,128)S(1)}, u32[]{:S(2)}, u32[]{:S(2)}) collective-permute-start(f32[16,1024]{1,0:T(8,128)S(1)} %get-tuple-element.57.refs_8_), channel_id=1, source_target_pairs={{0,24},{8,0},{16,8},{24,16},{1,25},{9,1},{17,9},{25,17},{2,26},{10... | collective-permute-start | bytes 196616 | tf_op jit(solution)/shard_map/ppermute | solution.py:430
  106.2 2.2 %collective-permute-done.40.refs_9_ = f32[16,1024]{1,0:T(8,128)S(1)} collective-permute-done((f32[16,1024]{1,0:T(8,128)S(1)}, f32[16,1024]{1,0:T(8,128)S(1)}, u32[]{:S(2)}, u32[]{:S(2)}) %collective-permute-start.40) | collective-permute-done | bytes 65568 | tf_op jit(solution)/shard_map/ppermute | solution.py:430
  108.4 2.6 %collective-permute-done.41.refs_10_ = f32[16,1024]{1,0:T(8,128)S(1)} collective-permute-done((f32[16,1024]{1,0:T(8,128)S(1)}, f32[16,1024]{1,0:T(8,128)S(1)}, u32[]{:S(2)}, u32[]{:S(2)}) %collective-permute-start.41) | collective-permute-done | bytes 65568 | tf_op jit(solution)/shard_map/ppermute | solution.py:430
  111.0 2.7 %collective-permute-start.35 = (f32[16,1024]{1,0:T(8,128)S(1)}, f32[16,1024]{1,0:T(8,128)S(1)}, u32[]{:S(2)}, u32[]{:S(2)}) collective-permute-start(f32[16,1024]{1,0:T(8,128)S(1)} %get-tuple-element.58.refs_8_), channel_id=1, source_target_pairs={{0,24},{8,0},{16,8},{24,16},{1,25},{9,1},{17,9},{25,17},{2,26},{10... | collective-permute-start | bytes 196616 | tf_op jit(solution)/shard_map/ppermute | solution.py:430
  113.7 1.9 %collective-permute-start.26 = (f32[16,1024]{1,0:T(8,128)S(1)}, f32[16,1024]{1,0:T(8,128)S(1)}, u32[]{:S(2)}, u32[]{:S(2)}) collective-permute-start(f32[16,1024]{1,0:T(8,128)S(1)} %get-tuple-element.59.refs_8_), channel_id=1, source_target_pairs={{0,8},{8,16},{16,24},{24,0},{1,9},{9,17},{17,25},{25,1},{2,10},{10... | collective-permute-start | bytes 196616 | tf_op jit(solution)/shard_map/ppermute | solution.py:430
  115.6 0.9 collective-permute-done.34.refs_10_
  116.4 1.6 collective-permute-start.28
  118.5 2.0 %collective-permute-done.26.refs_9_ = f32[16,1024]{1,0:T(8,128)S(1)} collective-permute-done((f32[16,1024]{1,0:T(8,128)S(1)}, f32[16,1024]{1,0:T(8,128)S(1)}, u32[]{:S(2)}, u32[]{:S(2)}) %collective-permute-start.26) | collective-permute-done | bytes 65568 | tf_op jit(solution)/shard_map/ppermute | solution.py:430
  120.5 2.3 %collective-permute-done.27.refs_10_ = f32[16,1024]{1,0:T(8,128)S(1)} collective-permute-done((f32[16,1024]{1,0:T(8,128)S(1)}, f32[16,1024]{1,0:T(8,128)S(1)}, u32[]{:S(2)}, u32[]{:S(2)}) %collective-permute-start.27) | collective-permute-done | bytes 65568 | tf_op jit(solution)/shard_map/ppermute | solution.py:430
  123.9 1.0 collective-permute-done.53.refs_15_
  128.6 9.9 %update_0.1 = (f32[64,64,1024]{2,1,0:T(8,128)}, bf16[64,64,1024]{2,1,0:T(8,128)(2,1)}, bf16[64,64,1024]{2,1,0:T(8,128)(2,1)}) custom-call(f32[64,1024]{1,0:T(8,128)S(1)} %get-tuple-element.33.refs_0_, f32[64,1024]{1,0:T(8,128)S(1)} %collective-permute-done.10.refs_1_, f32[64,1024]{1,0:T(8,128)S(1)} %collective-permute-done.11.refs_2_, ...), custom_call_target="tpu_custom_call" | custom-call | tf_op jit(solution)/shard_map/update_0/pallas_call | solution.py:571
  138.5 10.0 %update_1.1 = (f32[64,64,1024]{2,1,0:T(8,128)}, bf16[64,64,1024]{2,1,0:T(8,128)(2,1)}, bf16[64,64,1024]{2,1,0:T(8,128)(2,1)}) custom-call(f32[64,1024]{1,0:T(8,128)S(1)} %get-tuple-element.33.refs_0_, f32[64,1024]{1,0:T(8,128)S(1)} %collective-permute-done.10.refs_1_, ...), custom_call_target="tpu_custom_call", output_to_operand_aliasing={{0}: (19, {}), {1}: (20, {}), {2}: (21, {})} | custom-call | tf_op jit(solution)/shard_map/update_1/pallas_call | solution.py:571
  148.5 10.0 %update_2.1 = (f32[64,64,1024]{2,1,0:T(8,128)}, bf16[64,64,1024]{2,1,0:T(8,128)(2,1)}, bf16[64,64,1024]{2,1,0:T(8,128)(2,1)}) custom-call(f32[64,1024]{1,0:T(8,128)S(1)} %get-tuple-element.33.refs_0_, f32[64,1024]{1,0:T(8,128)S(1)} %collective-permute-done.10.refs_1_, ...), custom_call_target="tpu_custom_call", output_to_operand_aliasing={{0}: (19, {}), {1}: (20, {}), {2}: (21, {})} | custom-call | tf_op jit(solution)/shard_map/update_2/pallas_call | solution.py:571
  158.4 10.0 %update_3.1 = (f32[64,64,1024]{2,1,0:T(8,128)}, bf16[64,64,1024]{2,1,0:T(8,128)(2,1)}, bf16[64,64,1024]{2,1,0:T(8,128)(2,1)}) custom-call(f32[64,1024]{1,0:T(8,128)S(1)} %get-tuple-element.33.refs_0_, f32[64,1024]{1,0:T(8,128)S(1)} %collective-permute-done.10.refs_1_, ...), custom_call_target="tpu_custom_call", output_to_operand_aliasing={{0}: (19, {}), {1}: (20, {}), {2}: (21, {})} | custom-call | tf_op jit(solution)/shard_map/update_3/pallas_call | solution.py:571
  (103 shorter events, 12.8 us)
Async XLA Ops:
  7.3 9.7 %collective-permute-start.4 = (f32[2,64,256]{2,1,0:T(8,128)S(1)}, f32[2,64,256]{2,1,0:T(8,128)S(1)}, u32[]{:S(2)}, u32[]{:S(2)}) collective-permute-start(f32[2,64,256]{2,1,0:T(8,128)S(1)} %get-tuple-element.32.refs_0_), channel_id=1, source_target_pairs={{0,2},{2,4},{4,6},{6,0},{1,3},{3,5},{5,7},{7,1},{8,10},{10,12},{12... | collective-permute-start | bytes 393224 | tf_op jit(solution)/shard_map/ppermute | solution.py:430
  10.3 8.7 %collective-permute-start.5 = (f32[2,64,256]{2,1,0:T(8,128)S(1)}, f32[2,64,256]{2,1,0:T(8,128)S(1)}, u32[]{:S(2)}, u32[]{:S(2)}) collective-permute-start(f32[2,64,256]{2,1,0:T(8,128)S(1)} %get-tuple-element.32.refs_0_), channel_id=1, source_target_pairs={{0,4},{2,6},{4,0},{6,2},{1,5},{3,7},{5,1},{7,3},{8,12},{10,14},{12... | collective-permute-start | bytes 393224 | tf_op jit(solution)/shard_map/ppermute | solution.py:430
  11.8 7.1 %collective-permute-start.6 = (f32[2,64,256]{2,1,0:T(8,128)S(1)}, f32[2,64,256]{2,1,0:T(8,128)S(1)}, u32[]{:S(2)}, u32[]{:S(2)}) collective-permute-start(f32[2,64,256]{2,1,0:T(8,128)S(1)} %get-tuple-element.32.refs_0_), channel_id=1, source_target_pairs={{0,6},{2,0},{4,2},{6,4},{1,7},{3,1},{5,3},{7,5},{8,14},{10,8},{12,... | collective-permute-start | bytes 393224 | tf_op jit(solution)/shard_map/ppermute | solution.py:430
  15.9 6.9 %collective-permute-start.7 = (f32[2,64,256]{2,1,0:T(8,128)S(1)}, f32[2,64,256]{2,1,0:T(8,128)S(1)}, u32[]{:S(2)}, u32[]{:S(2)}) collective-permute-start(f32[2,64,256]{2,1,0:T(8,128)S(1)} %lift_1.1.refs_4_), channel_id=1, source_target_pairs={{0,2},{2,4},{4,6},{6,0},{1,3},{3,5},{5,7},{7,1},{8,10},{10,12},{12... | collective-permute-start | bytes 393224 | tf_op jit(solution)/shard_map/ppermute | solution.py:430
  16.5 6.9 %collective-permute-start.8 = (f32[2,64,256]{2,1,0:T(8,128)S(1)}, f32[2,64,256]{2,1,0:T(8,128)S(1)}, u32[]{:S(2)}, u32[]{:S(2)}) collective-permute-start(f32[2,64,256]{2,1,0:T(8,128)S(1)} %lift_1.1.refs_4_), channel_id=1, source_target_pairs={{0,4},{2,6},{4,0},{6,2},{1,5},{3,7},{5,1},{7,3},{8,12},{10,14},{12... | collective-permute-start | bytes 393224 | tf_op jit(solution)/shard_map/ppermute | solution.py:430
  17.0 6.5 %collective-permute-start.9 = (f32[2,64,256]{2,1,0:T(8,128)S(1)}, f32[2,64,256]{2,1,0:T(8,128)S(1)}, u32[]{:S(2)}, u32[]{:S(2)}) collective-permute-start(f32[2,64,256]{2,1,0:T(8,128)S(1)} %lift_1.1.refs_4_), channel_id=1, source_target_pairs={{0,6},{2,0},{4,2},{6,4},{1,7},{3,1},{5,3},{7,5},{8,14},{10,8},{12,... | collective-permute-start | bytes 393224 | tf_op jit(solution)/shard_map/ppermute | solution.py:430
  34.0 25.4 %collective-permute-start.17 = (bf16[64,1024]{1,0:T(8,128)(2,1)S(1)}, bf16[64,1024]{1,0:T(8,128)(2,1)S(1)}, u32[]{:S(2)}, u32[]{:S(2)}) collective-permute-start(bf16[64,1024]{1,0:T(8,128)(2,1)S(1)} %get-tuple-element.34.refs_0_), channel_id=1, source_target_pairs={{0,2},{2,4},{4,6},{6,0},{1,3},{3,5},{5,7},{7,1},{8,10},{10,12},{12... | collective-permute-start | bytes 393224 | tf_op jit(solution)/shard_map/ppermute | solution.py:430
  36.0 23.5 %collective-permute-start.18 = (bf16[64,1024]{1,0:T(8,128)(2,1)S(1)}, bf16[64,1024]{1,0:T(8,128)(2,1)S(1)}, u32[]{:S(2)}, u32[]{:S(2)}) collective-permute-start(bf16[64,1024]{1,0:T(8,128)(2,1)S(1)} %get-tuple-element.34.refs_0_), channel_id=1, source_target_pairs={{0,4},{2,6},{4,0},{6,2},{1,5},{3,7},{5,1},{7,3},{8,12},{10,14},{12... | collective-permute-start | bytes 393224 | tf_op jit(solution)/shard_map/ppermute | solution.py:430
  37.2 22.3 %collective-permute-start.19 = (bf16[64,1024]{1,0:T(8,128)(2,1)S(1)}, bf16[64,1024]{1,0:T(8,128)(2,1)S(1)}, u32[]{:S(2)}, u32[]{:S(2)}) collective-permute-start(bf16[64,1024]{1,0:T(8,128)(2,1)S(1)} %get-tuple-element.34.refs_0_), channel_id=1, source_target_pairs={{0,6},{2,0},{4,2},{6,4},{1,7},{3,1},{5,3},{7,5},{8,14},{10,8},{12,... | collective-permute-start | bytes 393224 | tf_op jit(solution)/shard_map/ppermute | solution.py:430
  38.4 4.2 %collective-permute-start = (f32[32,256]{1,0:T(8,128)S(1)}, f32[32,256]{1,0:T(8,128)S(1)}, u32[]{:S(2)}, u32[]{:S(2)}) collective-permute-start(f32[32,256]{1,0:T(8,128)S(1)} %get-tuple-element.26), channel_id=1, source_target_pairs={{0,2},{2,4},{4,6},{1,3},{3,5},{5,7},{8,10},{10,12},{12,14},{9,11},... | collective-permute-start | bytes 98312 | tf_op jit(solution)/shard_map/ppermute | solution.py:448
  41.1 5.8 %collective-permute-start.1 = (f32[32,256]{1,0:T(8,128)S(1)}, f32[32,256]{1,0:T(8,128)S(1)}, u32[]{:S(2)}, u32[]{:S(2)}) collective-permute-start(f32[32,256]{1,0:T(8,128)S(1)} %get-tuple-element.27), channel_id=1, source_target_pairs={{2,0},{4,2},{6,4},{3,1},{5,3},{7,5},{10,8},{12,10},{14,12},{11,9},... | collective-permute-start | bytes 98312 | tf_op jit(solution)/shard_map/ppermute | solution.py:449
  47.8 5.7 %collective-permute-start.2 = (f32[32,256]{1,0:T(8,128)S(1)}, f32[32,256]{1,0:T(8,128)S(1)}, u32[]{:S(2)}, u32[]{:S(2)}) collective-permute-start(f32[32,256]{1,0:T(8,128)S(1)} %get-tuple-element.29), channel_id=1, source_target_pairs={{0,2},{2,4},{4,6},{1,3},{3,5},{5,7},{8,10},{10,12},{12,14},{9,11},... | collective-permute-start | bytes 98312 | tf_op jit(solution)/shard_map/ppermute | solution.py:448
  51.9 5.8 %collective-permute-start.3 = (f32[32,256]{1,0:T(8,128)S(1)}, f32[32,256]{1,0:T(8,128)S(1)}, u32[]{:S(2)}, u32[]{:S(2)}) collective-permute-start(f32[32,256]{1,0:T(8,128)S(1)} %get-tuple-element.30), channel_id=1, source_target_pairs={{2,0},{4,2},{6,4},{3,1},{5,3},{7,5},{10,8},{12,10},{14,12},{11,9},... | collective-permute-start | bytes 98312 | tf_op jit(solution)/shard_map/ppermute | solution.py:449
  64.1 9.7 %collective-permute-start.23 = (f32[2,64,256]{2,1,0:T(8,128)S(1)}, f32[2,64,256]{2,1,0:T(8,128)S(1)}, u32[]{:S(2)}, u32[]{:S(2)}) collective-permute-start(f32[2,64,256]{2,1,0:T(8,128)S(1)} %backward_1.1.refs_4_), channel_id=1, source_target_pairs={{0,2},{2,4},{4,6},{6,0},{1,3},{3,5},{5,7},{7,1},{8,10},{10,12},{12... | collective-permute-start | bytes 393224 | tf_op jit(solution)/shard_map/ppermute | solution.py:430
  65.1 11.5 %collective-permute-start.24 = (f32[2,64,256]{2,1,0:T(8,128)S(1)}, f32[2,64,256]{2,1,0:T(8,128)S(1)}, u32[]{:S(2)}, u32[]{:S(2)}) collective-permute-start(f32[2,64,256]{2,1,0:T(8,128)S(1)} %backward_1.1.refs_4_), channel_id=1, source_target_pairs={{0,4},{2,6},{4,0},{6,2},{1,5},{3,7},{5,1},{7,3},{8,12},{10,14},{12... | collective-permute-start | bytes 393224 | tf_op jit(solution)/shard_map/ppermute | solution.py:430
  65.1 13.0 %collective-permute-start.25 = (f32[2,64,256]{2,1,0:T(8,128)S(1)}, f32[2,64,256]{2,1,0:T(8,128)S(1)}, u32[]{:S(2)}, u32[]{:S(2)}) collective-permute-start(f32[2,64,256]{2,1,0:T(8,128)S(1)} %backward_1.1.refs_4_), channel_id=1, source_target_pairs={{0,6},{2,0},{4,2},{6,4},{1,7},{3,1},{5,3},{7,5},{8,14},{10,8},{12,... | collective-permute-start | bytes 393224 | tf_op jit(solution)/shard_map/ppermute | solution.py:430
  71.6 9.2 %collective-permute-start.20 = (f32[2,64,256]{2,1,0:T(8,128)S(1)}, f32[2,64,256]{2,1,0:T(8,128)S(1)}, u32[]{:S(2)}, u32[]{:S(2)}) collective-permute-start(f32[2,64,256]{2,1,0:T(8,128)S(1)} %backward_0.1.refs_0_), channel_id=1, source_target_pairs={{0,2},{2,4},{4,6},{6,0},{1,3},{3,5},{5,7},{7,1},{8,10},{10,12},{12... | collective-permute-start | bytes 393224 | tf_op jit(solution)/shard_map/ppermute | solution.py:430
  72.2 9.9 %collective-permute-start.21 = (f32[2,64,256]{2,1,0:T(8,128)S(1)}, f32[2,64,256]{2,1,0:T(8,128)S(1)}, u32[]{:S(2)}, u32[]{:S(2)}) collective-permute-start(f32[2,64,256]{2,1,0:T(8,128)S(1)} %backward_0.1.refs_0_), channel_id=1, source_target_pairs={{0,4},{2,6},{4,0},{6,2},{1,5},{3,7},{5,1},{7,3},{8,12},{10,14},{12... | collective-permute-start | bytes 393224 | tf_op jit(solution)/shard_map/ppermute | solution.py:430
  73.8 8.3 %collective-permute-start.22 = (f32[2,64,256]{2,1,0:T(8,128)S(1)}, f32[2,64,256]{2,1,0:T(8,128)S(1)}, u32[]{:S(2)}, u32[]{:S(2)}) collective-permute-start(f32[2,64,256]{2,1,0:T(8,128)S(1)} %backward_0.1.refs_0_), channel_id=1, source_target_pairs={{0,6},{2,0},{4,2},{6,4},{1,7},{3,1},{5,3},{7,5},{8,14},{10,8},{12,... | collective-permute-start | bytes 393224 | tf_op jit(solution)/shard_map/ppermute | solution.py:430
  76.6 10.3 %collective-permute-start.10 = (f32[64,1024]{1,0:T(8,128)S(1)}, f32[64,1024]{1,0:T(8,128)S(1)}, u32[]{:S(2)}, u32[]{:S(2)}) collective-permute-start(f32[64,1024]{1,0:T(8,128)S(1)} %get-tuple-element.33.refs_0_), channel_id=1, source_target_pairs={{0,8},{8,16},{16,24},{24,0},{1,9},{9,17},{17,25},{25,1},{2,10},{10... | collective-permute-start | bytes 786440 | tf_op jit(solution)/shard_map/ppermute | solution.py:430
  78.2 18.3 %collective-permute-start.11 = (f32[64,1024]{1,0:T(8,128)S(1)}, f32[64,1024]{1,0:T(8,128)S(1)}, u32[]{:S(2)}, u32[]{:S(2)}) collective-permute-start(f32[64,1024]{1,0:T(8,128)S(1)} %get-tuple-element.33.refs_0_), channel_id=1, source_target_pairs={{0,16},{8,24},{16,0},{24,8},{1,17},{9,25},{17,1},{25,9},{2,18},{10... | collective-permute-start | bytes 786440 | tf_op jit(solution)/shard_map/ppermute | solution.py:430
  80.8 20.8 %collective-permute-start.12 = (f32[64,1024]{1,0:T(8,128)S(1)}, f32[64,1024]{1,0:T(8,128)S(1)}, u32[]{:S(2)}, u32[]{:S(2)}) collective-permute-start(f32[64,1024]{1,0:T(8,128)S(1)} %get-tuple-element.33.refs_0_), channel_id=1, source_target_pairs={{0,24},{8,0},{16,8},{24,16},{1,25},{9,1},{17,9},{25,17},{2,26},{10... | collective-permute-start | bytes 786440 | tf_op jit(solution)/shard_map/ppermute | solution.py:430
  82.1 19.4 %collective-permute-start.13 = (f32[64,1024]{1,0:T(8,128)S(1)}, f32[64,1024]{1,0:T(8,128)S(1)}, u32[]{:S(2)}, u32[]{:S(2)}) collective-permute-start(f32[64,1024]{1,0:T(8,128)S(1)} %get-tuple-element.33.refs_0_), channel_id=1, source_target_pairs={{0,1},{1,0},{2,3},{3,2},{4,5},{5,4},{6,7},{7,6},{8,9},{9,8},{10,11... | collective-permute-start | bytes 786440 | tf_op jit(solution)/shard_map/ppermute | solution.py:440
  83.2 19.5 %collective-permute-start.47 = (f32[16,1024]{1,0:T(8,128)S(1)}, f32[16,1024]{1,0:T(8,128)S(1)}, u32[]{:S(2)}, u32[]{:S(2)}) collective-permute-start(f32[16,1024]{1,0:T(8,128)S(1)} %get-tuple-element.56.refs_8_), channel_id=1, source_target_pairs={{0,8},{8,16},{16,24},{24,0},{1,9},{9,17},{17,25},{25,1},{2,10},{10... | collective-permute-start | bytes 196616 | tf_op jit(solution)/shard_map/ppermute | solution.py:430
  86.9 16.0 %collective-permute-start.48 = (f32[16,1024]{1,0:T(8,128)S(1)}, f32[16,1024]{1,0:T(8,128)S(1)}, u32[]{:S(2)}, u32[]{:S(2)}) collective-permute-start(f32[16,1024]{1,0:T(8,128)S(1)} %get-tuple-element.56.refs_8_), channel_id=1, source_target_pairs={{0,16},{8,24},{16,0},{24,8},{1,17},{9,25},{17,1},{25,9},{2,18},{10... | collective-permute-start | bytes 196616 | tf_op jit(solution)/shard_map/ppermute | solution.py:430
  96.5 9.0 %collective-permute-start.49 = (f32[16,1024]{1,0:T(8,128)S(1)}, f32[16,1024]{1,0:T(8,128)S(1)}, u32[]{:S(2)}, u32[]{:S(2)}) collective-permute-start(f32[16,1024]{1,0:T(8,128)S(1)} %get-tuple-element.56.refs_8_), channel_id=1, source_target_pairs={{0,24},{8,0},{16,8},{24,16},{1,25},{9,1},{17,9},{25,17},{2,26},{10... | collective-permute-start | bytes 196616 | tf_op jit(solution)/shard_map/ppermute | solution.py:430
  101.5 4.0 %collective-permute-start.50 = (f32[16,1024]{1,0:T(8,128)S(1)}, f32[16,1024]{1,0:T(8,128)S(1)}, u32[]{:S(2)}, u32[]{:S(2)}) collective-permute-start(f32[16,1024]{1,0:T(8,128)S(1)} %get-tuple-element.56.refs_8_), channel_id=1, source_target_pairs={{0,1},{1,0},{2,3},{3,2},{4,5},{5,4},{6,7},{7,6},{8,9},{9,8},{10,11... | collective-permute-start | bytes 196616 | tf_op jit(solution)/shard_map/ppermute | solution.py:440
  101.6 6.8 %collective-permute-start.40 = (f32[16,1024]{1,0:T(8,128)S(1)}, f32[16,1024]{1,0:T(8,128)S(1)}, u32[]{:S(2)}, u32[]{:S(2)}) collective-permute-start(f32[16,1024]{1,0:T(8,128)S(1)} %get-tuple-element.57.refs_8_), channel_id=1, source_target_pairs={{0,8},{8,16},{16,24},{24,0},{1,9},{9,17},{17,25},{25,1},{2,10},{10... | collective-permute-start | bytes 196616 | tf_op jit(solution)/shard_map/ppermute | solution.py:430
  102.7 8.3 %collective-permute-start.41 = (f32[16,1024]{1,0:T(8,128)S(1)}, f32[16,1024]{1,0:T(8,128)S(1)}, u32[]{:S(2)}, u32[]{:S(2)}) collective-permute-start(f32[16,1024]{1,0:T(8,128)S(1)} %get-tuple-element.57.refs_8_), channel_id=1, source_target_pairs={{0,16},{8,24},{16,0},{24,8},{1,17},{9,25},{17,1},{25,9},{2,18},{10... | collective-permute-start | bytes 196616 | tf_op jit(solution)/shard_map/ppermute | solution.py:430
  102.9 10.7 %collective-permute-start.42 = (f32[16,1024]{1,0:T(8,128)S(1)}, f32[16,1024]{1,0:T(8,128)S(1)}, u32[]{:S(2)}, u32[]{:S(2)}) collective-permute-start(f32[16,1024]{1,0:T(8,128)S(1)} %get-tuple-element.57.refs_8_), channel_id=1, source_target_pairs={{0,24},{8,0},{16,8},{24,16},{1,25},{9,1},{17,9},{25,17},{2,26},{10... | collective-permute-start | bytes 196616 | tf_op jit(solution)/shard_map/ppermute | solution.py:430
  105.5 8.2 %collective-permute-start.43 = (f32[16,1024]{1,0:T(8,128)S(1)}, f32[16,1024]{1,0:T(8,128)S(1)}, u32[]{:S(2)}, u32[]{:S(2)}) collective-permute-start(f32[16,1024]{1,0:T(8,128)S(1)} %get-tuple-element.57.refs_8_), channel_id=1, source_target_pairs={{0,1},{1,0},{2,3},{3,2},{4,5},{5,4},{6,7},{7,6},{8,9},{9,8},{10,11... | collective-permute-start | bytes 196616 | tf_op jit(solution)/shard_map/ppermute | solution.py:440
  105.5 10.0 %collective-permute-start.33 = (f32[16,1024]{1,0:T(8,128)S(1)}, f32[16,1024]{1,0:T(8,128)S(1)}, u32[]{:S(2)}, u32[]{:S(2)}) collective-permute-start(f32[16,1024]{1,0:T(8,128)S(1)} %get-tuple-element.58.refs_8_), channel_id=1, source_target_pairs={{0,8},{8,16},{16,24},{24,0},{1,9},{9,17},{17,25},{25,1},{2,10},{10... | collective-permute-start | bytes 196616 | tf_op jit(solution)/shard_map/ppermute | solution.py:430
  108.4 8.0 %collective-permute-start.34 = (f32[16,1024]{1,0:T(8,128)S(1)}, f32[16,1024]{1,0:T(8,128)S(1)}, u32[]{:S(2)}, u32[]{:S(2)}) collective-permute-start(f32[16,1024]{1,0:T(8,128)S(1)} %get-tuple-element.58.refs_8_), channel_id=1, source_target_pairs={{0,16},{8,24},{16,0},{24,8},{1,17},{9,25},{17,1},{25,9},{2,18},{10... | collective-permute-start | bytes 196616 | tf_op jit(solution)/shard_map/ppermute | solution.py:430
  111.0 7.0 %collective-permute-start.35 = (f32[16,1024]{1,0:T(8,128)S(1)}, f32[16,1024]{1,0:T(8,128)S(1)}, u32[]{:S(2)}, u32[]{:S(2)}) collective-permute-start(f32[16,1024]{1,0:T(8,128)S(1)} %get-tuple-element.58.refs_8_), channel_id=1, source_target_pairs={{0,24},{8,0},{16,8},{24,16},{1,25},{9,1},{17,9},{25,17},{2,26},{10... | collective-permute-start | bytes 196616 | tf_op jit(solution)/shard_map/ppermute | solution.py:430
  113.7 4.3 %collective-permute-start.36 = (f32[16,1024]{1,0:T(8,128)S(1)}, f32[16,1024]{1,0:T(8,128)S(1)}, u32[]{:S(2)}, u32[]{:S(2)}) collective-permute-start(f32[16,1024]{1,0:T(8,128)S(1)} %get-tuple-element.58.refs_8_), channel_id=1, source_target_pairs={{0,1},{1,0},{2,3},{3,2},{4,5},{5,4},{6,7},{7,6},{8,9},{9,8},{10,11... | collective-permute-start | bytes 196616 | tf_op jit(solution)/shard_map/ppermute | solution.py:440
  113.7 6.8 %collective-permute-start.26 = (f32[16,1024]{1,0:T(8,128)S(1)}, f32[16,1024]{1,0:T(8,128)S(1)}, u32[]{:S(2)}, u32[]{:S(2)}) collective-permute-start(f32[16,1024]{1,0:T(8,128)S(1)} %get-tuple-element.59.refs_8_), channel_id=1, source_target_pairs={{0,8},{8,16},{16,24},{24,0},{1,9},{9,17},{17,25},{25,1},{2,10},{10... | collective-permute-start | bytes 196616 | tf_op jit(solution)/shard_map/ppermute | solution.py:430
  115.5 7.3 %collective-permute-start.27 = (f32[16,1024]{1,0:T(8,128)S(1)}, f32[16,1024]{1,0:T(8,128)S(1)}, u32[]{:S(2)}, u32[]{:S(2)}) collective-permute-start(f32[16,1024]{1,0:T(8,128)S(1)} %get-tuple-element.59.refs_8_), channel_id=1, source_target_pairs={{0,16},{8,24},{16,0},{24,8},{1,17},{9,25},{17,1},{25,9},{2,18},{10... | collective-permute-start | bytes 196616 | tf_op jit(solution)/shard_map/ppermute | solution.py:430
  116.4 6.4 %collective-permute-start.28 = (f32[16,1024]{1,0:T(8,128)S(1)}, f32[16,1024]{1,0:T(8,128)S(1)}, u32[]{:S(2)}, u32[]{:S(2)}) collective-permute-start(f32[16,1024]{1,0:T(8,128)S(1)} %get-tuple-element.59.refs_8_), channel_id=1, source_target_pairs={{0,24},{8,0},{16,8},{24,16},{1,25},{9,1},{17,9},{25,17},{2,26},{10... | collective-permute-start | bytes 196616 | tf_op jit(solution)/shard_map/ppermute | solution.py:430
  118.0 5.4 %collective-permute-start.51 = (f32[16,1024]{1,0:T(8,128)S(1)}, f32[16,1024]{1,0:T(8,128)S(1)}, u32[]{:S(2)}, u32[]{:S(2)}) collective-permute-start(f32[16,1024]{1,0:T(8,128)S(1)} %collective-permute-done.47.refs_9_), channel_id=1, source_target_pairs={{0,1},{1,0},{2,3},{3,2},{4,5},{5,4},{6,7},{7,6},{8,9},{9,8},{10,11... | collective-permute-start | bytes 196616 | tf_op jit(solution)/shard_map/ppermute | solution.py:440
  118.0 5.4 %collective-permute-start.52 = (f32[16,1024]{1,0:T(8,128)S(1)}, f32[16,1024]{1,0:T(8,128)S(1)}, u32[]{:S(2)}, u32[]{:S(2)}) collective-permute-start(f32[16,1024]{1,0:T(8,128)S(1)} %collective-permute-done.48.refs_10_), channel_id=1, source_target_pairs={{0,1},{1,0},{2,3},{3,2},{4,5},{5,4},{6,7},{7,6},{8,9},{9,8},{10,11... | collective-permute-start | bytes 196616 | tf_op jit(solution)/shard_map/ppermute | solution.py:440
  120.5 7.4 %collective-permute-start.14 = (f32[64,1024]{1,0:T(8,128)S(1)}, f32[64,1024]{1,0:T(8,128)S(1)}, u32[]{:S(2)}, u32[]{:S(2)}) collective-permute-start(f32[64,1024]{1,0:T(8,128)S(1)} %collective-permute-done.10.refs_1_), channel_id=1, source_target_pairs={{0,1},{1,0},{2,3},{3,2},{4,5},{5,4},{6,7},{7,6},{8,9},{9,8},{10,11... | collective-permute-start | bytes 786440 | tf_op jit(solution)/shard_map/ppermute | solution.py:440
  122.9 5.2 %collective-permute-start.15 = (f32[64,1024]{1,0:T(8,128)S(1)}, f32[64,1024]{1,0:T(8,128)S(1)}, u32[]{:S(2)}, u32[]{:S(2)}) collective-permute-start(f32[64,1024]{1,0:T(8,128)S(1)} %collective-permute-done.11.refs_2_), channel_id=1, source_target_pairs={{0,1},{1,0},{2,3},{3,2},{4,5},{5,4},{6,7},{7,6},{8,9},{9,8},{10,11... | collective-permute-start | bytes 786440 | tf_op jit(solution)/shard_map/ppermute | solution.py:440
  122.9 5.5 %collective-permute-start.16 = (f32[64,1024]{1,0:T(8,128)S(1)}, f32[64,1024]{1,0:T(8,128)S(1)}, u32[]{:S(2)}, u32[]{:S(2)}) collective-permute-start(f32[64,1024]{1,0:T(8,128)S(1)} %collective-permute-done.12.refs_3_), channel_id=1, source_target_pairs={{0,1},{1,0},{2,3},{3,2},{4,5},{5,4},{6,7},{7,6},{8,9},{9,8},{10,11... | collective-permute-start | bytes 786440 | tf_op jit(solution)/shard_map/ppermute | solution.py:440
  127.4 21.1 %collective-permute-start.39 = (f32[16,1024]{1,0:T(8,128)S(1)}, f32[16,1024]{1,0:T(8,128)S(1)}, u32[]{:S(2)}, u32[]{:S(2)}) collective-permute-start(f32[16,1024]{1,0:T(8,128)S(1)} %collective-permute-done.35.refs_11_), channel_id=1, source_target_pairs={{0,1},{1,0},{2,3},{3,2},{4,5},{5,4},{6,7},{7,6},{8,9},{9,8},{10,11... | collective-permute-start | bytes 196616 | tf_op jit(solution)/shard_map/ppermute | solution.py:440
  127.5 30.9 %collective-permute-start.29 = (f32[16,1024]{1,0:T(8,128)S(1)}, f32[16,1024]{1,0:T(8,128)S(1)}, u32[]{:S(2)}, u32[]{:S(2)}) collective-permute-start(f32[16,1024]{1,0:T(8,128)S(1)} %get-tuple-element.59.refs_8_), channel_id=1, source_target_pairs={{0,1},{1,0},{2,3},{3,2},{4,5},{5,4},{6,7},{7,6},{8,9},{9,8},{10,11... | collective-permute-start | bytes 196616 | tf_op jit(solution)/shard_map/ppermute | solution.py:440
  127.9 30.5 %collective-permute-start.30 = (f32[16,1024]{1,0:T(8,128)S(1)}, f32[16,1024]{1,0:T(8,128)S(1)}, u32[]{:S(2)}, u32[]{:S(2)}) collective-permute-start(f32[16,1024]{1,0:T(8,128)S(1)} %collective-permute-done.26.refs_9_), channel_id=1, source_target_pairs={{0,1},{1,0},{2,3},{3,2},{4,5},{5,4},{6,7},{7,6},{8,9},{9,8},{10,11... | collective-permute-start | bytes 196616 | tf_op jit(solution)/shard_map/ppermute | solution.py:440
  128.1 30.4 %collective-permute-start.31 = (f32[16,1024]{1,0:T(8,128)S(1)}, f32[16,1024]{1,0:T(8,128)S(1)}, u32[]{:S(2)}, u32[]{:S(2)}) collective-permute-start(f32[16,1024]{1,0:T(8,128)S(1)} %collective-permute-done.27.refs_10_), channel_id=1, source_target_pairs={{0,1},{1,0},{2,3},{3,2},{4,5},{5,4},{6,7},{7,6},{8,9},{9,8},{10,11... | collective-permute-start | bytes 196616 | tf_op jit(solution)/shard_map/ppermute | solution.py:440
  128.4 30.0 %collective-permute-start.32 = (f32[16,1024]{1,0:T(8,128)S(1)}, f32[16,1024]{1,0:T(8,128)S(1)}, u32[]{:S(2)}, u32[]{:S(2)}) collective-permute-start(f32[16,1024]{1,0:T(8,128)S(1)} %collective-permute-done.28.refs_11_), channel_id=1, source_target_pairs={{0,1},{1,0},{2,3},{3,2},{4,5},{5,4},{6,7},{7,6},{8,9},{9,8},{10,11... | collective-permute-start | bytes 196616 | tf_op jit(solution)/shard_map/ppermute | solution.py:440
  (21 other events, 288.7 us)

commit v2 on v1

v2 whole, which is shorter than its diff:
```python
import functools
import math

import jax
import jax.numpy as jnp
import ml_dtypes
import numpy as np
from jax import lax
from jax.experimental import pallas as pl
from jax.experimental.pallas import tpu as pltpu
from jax.sharding import PartitionSpec as P

KM = 16
TY = 64
TZ = 64
MODES = KM * KM * KM
JOINT = KM * KM
EZ = TZ // 4
LANES = 128
NODES = 125
PLANES = 4
CELLS = 16

HIGHEST = lax.Precision.HIGHEST
F32 = jnp.float32
BF16 = jnp.bfloat16
TIME_STEP = 0.02
FACE_GAIN = 10.0
LOSS_SCALE = 1.0 / 2048.0
LEARN_RATE = 0.001
BETA_ONE = 0.9
BETA_TWO = 0.999
BIAS_ONE = 1.0 - BETA_ONE**10
BIAS_TWO = 1.0 - BETA_TWO**10
EPSILON = 1e-08
GAUSS_NORM = 1.0 / math.sqrt(2.0 * math.pi)
MIB = 1024 * 1024
VMEM_LIMIT = 8 * MIB
UPDATE_VMEM = 12 * MIB

TAIL_SCALE = 0.32
TAIL = (
    0.12766152875085093,
    0.12766094645791293,
    0.11462235951270612,
    0.08782909645624029,
    0.058653976831234717,
    -0.009377604773061265,
    0.065328090206421,
    -0.1467075324124934,
    0.09540730271922851,
    -0.021078179724135896,
)


def lagrange(nodes, column, target):
    value = 1.0
    for other in range(len(nodes)):
        if other != column:
            value = value * (target - nodes[other]) / (nodes[column] - nodes[other])
    return value


def lagrange_slope(nodes, column, target):
    total = 0.0
    for skipped in range(len(nodes)):
        if skipped != column:
            factor = 1.0 / (nodes[column] - nodes[skipped])
            for other in range(len(nodes)):
                if other != column and other != skipped:
                    factor = factor * (target - nodes[other]) / (nodes[column] - nodes[other])
            total = total + factor
    return total


def padded_to(matrix, shape):
    out = np.zeros(shape, np.float32)
    out[: matrix.shape[0], : matrix.shape[1]] = matrix
    return out


def solver_tables():
    nodes = [-1.0, -math.sqrt(3.0 / 7.0), 0.0, math.sqrt(3.0 / 7.0), 1.0]
    slopes = np.zeros((5, 5))
    interp = np.zeros((4, 5))
    for row in range(5):
        for column in range(5):
            slopes[row, column] = lagrange_slope(nodes, column, nodes[row])
    for sample in range(4):
        for column in range(5):
            interp[sample, column] = lagrange(nodes, column, -1.0 + (2.0 * sample + 1.0) / 4.0)
    slopes = slopes.astype(np.float32).astype(np.float64)
    interp = interp.astype(np.float32).astype(np.float64)
    eye = np.eye(5)
    along = (
        np.kron(slopes, np.eye(25)),
        np.kron(eye, np.kron(slopes, eye)),
        np.kron(np.eye(25), slopes),
    )
    square = [padded_to(-2.0 * m, (LANES, LANES)) for m in along]
    slopes_of = np.concatenate(square, axis=0)
    to_grid = padded_to(np.kron(interp, np.kron(interp, interp)), (64, LANES))
    faces = np.zeros((LANES, LANES), np.float32)
    index = np.arange(NODES)
    for direction, place in enumerate((index // 25, index // 5 % 5, index % 5)):
        faces[:NODES, 2 * direction] = np.where(place == 0, -FACE_GAIN, 0.0)
        faces[:NODES, 2 * direction + 1] = np.where(place == 4, FACE_GAIN, 0.0)
    return slopes_of, to_grid, faces


def fourier_table(length, kept):
    angles = np.arange(length) * (2.0 * math.pi / length)
    rows = []
    for k in range(kept // 2 + 1):
        factor = math.sqrt(1.0 / length) if k == 0 else math.sqrt(2.0 / length)
        rows.append(factor * np.cos(k * angles))
    for k in range(1, kept // 2):
        rows.append(math.sqrt(2.0 / length) * np.sin(k * angles))
    return np.stack(rows)


def rounded(table):
    return table.astype(np.float32).astype(ml_dtypes.bfloat16)


def joint_table():
    joined = rounded(np.kron(fourier_table(TY, KM), fourier_table(TZ, KM)))
    joined = joined.reshape(JOINT, TY // 4, 4, TZ // 4, 4)
    return np.ascontiguousarray(joined.transpose(0, 2, 4, 1, 3).reshape(JOINT, TY * TZ))


def params(limit=VMEM_LIMIT, **more):
    return pltpu.CompilerParams(vmem_limit_bytes=limit, **more)


SMALL_COST = pl.CostEstimate(flops=1000, bytes_accessed=1000, transcendentals=0)


def in_hbm(array):
    return pltpu.with_memory_space_constraint(array, pltpu.HBM)


def in_vmem(array):
    return pltpu.with_memory_space_constraint(array, pltpu.VMEM)


SMEM_SPEC = pl.BlockSpec(memory_space=pltpu.SMEM)
VMEM_SPEC = pl.BlockSpec(memory_space=pltpu.VMEM)
HBM_SPEC = pl.BlockSpec(memory_space=pltpu.HBM)
ANY_SPEC = pl.BlockSpec(memory_space=pl.ANY)


def column_of(row):
    n = row.shape[1]
    square = jnp.broadcast_to(row, (n, n))
    at_row = lax.broadcasted_iota(jnp.int32, (n, n), 0)
    at_lane = lax.broadcasted_iota(jnp.int32, (n, n), 1)
    return jnp.sum(jnp.where(at_row == at_lane, square, 0.0), axis=1, keepdims=True)


def normal_parts(x):
    bell = jnp.exp(-0.5 * x * x)
    t = 1.0 / (1.0 + TAIL_SCALE * jnp.abs(x))
    tail = jnp.full_like(t, TAIL[-1])
    for factor in TAIL[-2::-1]:
        tail = tail * t + factor
    tail = tail * t * bell
    return jnp.where(x < 0.0, tail, 1.0 - tail), bell


def read_field(ref, field):
    start = 2 * NODES * field
    halves = [ref[pl.ds(start + h, NODES, stride=2), :] for h in range(2)]
    both = jnp.concatenate(halves, axis=1)
    return jnp.concatenate([both, jnp.zeros((LANES - NODES, both.shape[1]), F32)], axis=0)


def x_faces(pressure, velocity, up_ref, down_ref, row):
    up_ref[row : row + 32] = pltpu.roll(pressure + velocity, 28, 0)[:32]
    down_ref[row : row + 32] = (velocity - pressure)[:32]


def grid_values(to_grid, pressure):
    return lax.dot(to_grid, pressure, precision=HIGHEST, preferred_element_type=F32)


def x_parts(pressure, velocity, below, above, faces):
    pad = jnp.zeros((LANES - 32, pressure.shape[1]), F32)
    from_low = jnp.concatenate([below, pad], axis=0)
    from_high = pltpu.roll(jnp.concatenate([above, pad], axis=0), 100, 0)
    low = faces[:, 0:1] * ((velocity + pressure) - from_low)
    high = faces[:, 1:2] * ((velocity - pressure) - from_high)
    return low + high, low - high


def local_rates(fields, sink, slopes, faces):
    pressure = fields[0]
    change = lax.dot(slopes, pressure, precision=HIGHEST, preferred_element_type=F32)
    across = jnp.concatenate([slopes[d * LANES : (d + 1) * LANES] for d in range(3)], axis=1)
    rate = lax.dot(
        across, jnp.concatenate(fields[1:], axis=0), precision=HIGHEST, preferred_element_type=F32
    )
    cells = pressure.shape[1]
    cell = lax.broadcasted_iota(jnp.int32, (1, cells), 1)
    depth = cell & (EZ - 1)
    velocity_rates = [change[:LANES]]
    for d in (1, 2):
        velocity = fields[1 + d]
        up = velocity + pressure
        down = velocity - pressure
        nodes, step = ((20, EZ), (4, 1))[d - 1]
        from_low = pltpu.roll(pltpu.roll(up, LANES - nodes, 0), step, 1)
        from_high = pltpu.roll(pltpu.roll(down, nodes, 0), cells - step, 1)
        first = cell < EZ if d == 1 else depth == 0
        last = cell >= cells - EZ if d == 1 else depth == EZ - 1
        low = faces[:, 2 * d : 2 * d + 1] * (up - jnp.where(first, 0.0, from_low))
        high = faces[:, 2 * d + 1 : 2 * d + 2] * (down - jnp.where(last, 0.0, from_high))
        rate = rate + (low + high)
        velocity_rates.append(change[d * LANES : (d + 1) * LANES] + (low - high))
    return [r - sink * q for r, q in zip([rate] + velocity_rates, fields)]


def first_stage(state_ref, mask_ref, damping_ref, slopes_ref, faces_ref, mid_ref, up_ref, down_ref):
    fields = [read_field(state_ref, f) for f in range(4)]
    sink = mask_ref[...].astype(F32) * damping_ref[...]
    rate = local_rates(fields, sink, slopes_ref[...], faces_ref[...])
    mid = [q + TIME_STEP * r for q, r in zip(fields, rate)]
    for f in range(4):
        mid_ref[f] = mid[f]
    x_faces(fields[0], fields[1], up_ref, down_ref, 0)
    x_faces(mid[0], mid[1], up_ref, down_ref, 32)


def lift_kernel(me_ref, *refs):
    del me_ref
    n = (len(refs) - 5) // 2
    given, (out_ref, mid_ref, up_ref, down_ref) = refs[:n], refs[n : n + 4]
    held, sems = refs[n + 4 : -1], refs[-1]
    state_ref, gain_ref, to_grid_ref, table_ref = held[:4]
    copies = [pltpu.make_async_copy(a, b, sems.at[k]) for k, (a, b) in enumerate(zip(given, held))]
    for copy in copies:
        copy.start()
    for copy in copies[:3]:
        copy.wait()
    grid = grid_values(to_grid_ref[...], read_field(state_ref, 0))
    grid = grid.astype(BF16).astype(F32)
    gain = column_of(gain_ref[...])
    cells = grid.shape[1]
    channels = gain.shape[0]
    for copy in copies[3:]:
        copy.wait()
    for pair in range(0, PLANES, 2):
        total = jnp.zeros((2 * channels, JOINT), F32)
        for j in range(CELLS):
            parts = []
            for k in (pair, pair + 1):
                at = k * CELLS + j
                scaled = gain * grid[at : at + 1, :]
                parts.append((scaled * normal_parts(scaled)[0]).astype(BF16))
            lifted = jnp.concatenate(parts, axis=0)
            total = total + jnp.dot(
                lifted, table_ref[j * cells : (j + 1) * cells, :], preferred_element_type=F32
            )
        out_ref[pair] = total[:channels]
        out_ref[pair + 1] = total[channels:]
    first_stage(state_ref, *held[4:], mid_ref, up_ref, down_ref)


def second_stage_kernel(
    state_ref, mid_ref, below_ref, above_ref, mask_ref, damping_ref, slopes_ref, faces_ref,
    to_grid_ref, after_ref, new_ref, target_ref,
):
    del after_ref
    faces = faces_ref[...]
    mid = [mid_ref[f] for f in range(4)]
    parts = x_parts(
        read_field(state_ref, 0), read_field(state_ref, 1), below_ref[:32], above_ref[:32], faces
    )
    mid[0] = mid[0] + TIME_STEP * parts[0]
    mid[1] = mid[1] + TIME_STEP * parts[1]
    sink = mask_ref[...].astype(F32) * damping_ref[...]
    rate = local_rates(mid, sink, slopes_ref[...], faces)
    parts = x_parts(mid[0], mid[1], below_ref[32:], above_ref[32:], faces)
    rate[0] = rate[0] + parts[0]
    rate[1] = rate[1] + parts[1]
    for f in range(4):
        new = 0.5 * (read_field(state_ref, f) + mid[f] + TIME_STEP * rate[f])
        for h in range(2):
            new_ref[pl.ds(2 * NODES * f + h, NODES, stride=2), :] = new[
                :NODES, h * LANES : (h + 1) * LANES
            ]
        if f == 0:
            target_ref[...] = grid_values(to_grid_ref[...], new).astype(BF16).astype(F32)


def owned(me, modes):
    if modes >= JOINT:
        return me * (modes // JOINT), modes // JOINT, None
    per = JOINT // modes
    return me // per, 1, pl.multiple_of(lax.rem(me, per) * modes, modes)


def sum_over_x(me_ref, fx_ref, gathered, halves, *out_refs, factor=1.0):
    me = me_ref[0]
    rows, modes = out_refs[0].shape
    first, count, offset = owned(me, modes)
    width = min(modes, JOINT)
    totals = [None] * count
    for slab, read in gathered(me):
        for h in range(halves):
            for k in range(PLANES // halves):
                block = read(h, k, offset, width)
                x = PLANES * slab + h * (PLANES // halves) + k
                for i in range(count):
                    term = fx_ref[first + i, x] * block
                    totals[i] = term if totals[i] is None else totals[i] + term
    for i in range(count):
        for k, out_ref in enumerate(out_refs):
            out_ref[:, i * width : (i + 1) * width] = factor * totals[i][k * rows : (k + 1) * rows]


def gathered_planes(refs, count, halves):
    def walk(me):
        per = len(refs) // halves
        if per == count:
            for b in range(count):
                slab = lax.rem(me + (count - b), count)

                def read(h, k, offset, width, b=b):
                    ref = refs[h * per + b]
                    return ref[k] if offset is None else ref[k, :, pl.ds(offset, width)]

                yield slab, read
        else:
            for b in range(count):

                def read(h, k, offset, width, b=b):
                    ref = refs[h]
                    return ref[b, k] if offset is None else ref[b, k, :, pl.ds(offset, width)]

                yield b, read

    return walk


def count_of_parts(refs, halves, count):
    return halves * count if refs[0].ndim == 3 else halves


def mix_kernel(count, me_ref, fx_ref, *refs):
    parts = refs[:-5]
    spectral_ref, _, _, coeffs_ref, mixed_ref = refs[-5:]
    sum_over_x(me_ref, fx_ref, gathered_planes(parts, count, 1), 1, coeffs_ref)
    channels, modes = coeffs_ref.shape

    @pl.loop(0, modes // LANES)
    def _(tile):
        at = pl.ds(pl.multiple_of(tile * LANES, LANES), LANES)
        total = coeffs_ref[0:1, at] * spectral_ref[0, :, at]
        for c in range(1, channels):
            total = total + coeffs_ref[c : c + 1, at] * spectral_ref[c, :, at]
        mixed_ref[:, at] = total.astype(BF16)


def coeffs_kernel(count, halves, me_ref, fx_ref, *refs):
    n = count_of_parts(refs, halves, count)
    parts = gathered_planes(refs[:n], count, halves)
    sum_over_x(me_ref, fx_ref, parts, halves, *refs[-UPDATE_CHUNKS:], factor=1.0 - BETA_ONE)


def backward_kernel(count, half, me_ref, fx_ref, *refs):
    parts = refs[:-8]
    weight_ref, target_ref, forward_ref, table_ref = refs[-8:-4]
    out_ref, along_ref = refs[-2:]
    me = me_ref[0]
    planes, channels = out_ref.shape[:2]
    modes = parts[0].shape[-1]
    width = min(modes, JOINT)
    along_ref[...] = jnp.zeros_like(along_ref)
    for b in range(count):
        if len(parts) == count:
            ref, slab = parts[b], lax.rem(me + (count - b), count)
        else:
            ref, slab = parts[0].at[b], b
        first, functions, offset = owned(slab, modes)
        for i in range(functions):
            block = ref[:, i * width : (i + 1) * width].astype(F32)
            for k in range(planes):
                x = PLANES * me + half * planes + k
                at = (pl.ds(k * channels, channels), slice(None) if offset is None else pl.ds(offset, width))
                along_ref[at] += fx_ref[first + i, x] * block
    along = along_ref[...]
    high = along.astype(BF16)
    rest = along - high.astype(F32)
    middle = rest.astype(BF16)
    low = (rest - middle.astype(F32)).astype(BF16)
    thirds = jnp.concatenate([high, middle, low], axis=0)
    weight = column_of(weight_ref[...])
    rows = planes * channels
    cells = target_ref.shape[1]
    total = jnp.zeros((rows, JOINT), F32)
    for j in range(CELLS):
        spread = jnp.dot(
            thirds, forward_ref[:, j * cells : (j + 1) * cells], preferred_element_type=F32
        )
        parts_of = []
        for k in range(planes):
            r = k * channels
            pre = (
                spread[2 * rows + r : 2 * rows + r + channels]
                + spread[rows + r : rows + r + channels]
            ) + spread[r : r + channels]
            phi, bell = normal_parts(pre)
            predicted = jnp.sum(pre * phi * weight, axis=0, keepdims=True)
            at = (half * planes + k) * CELLS + j
            misfit = 2.0 * LOSS_SCALE * (predicted - target_ref[at : at + 1, :])
            slope = phi + pre * bell * GAUSS_NORM
            parts_of.append((misfit * weight * slope).astype(BF16))
        total = total + jnp.dot(
            jnp.concatenate(parts_of, axis=0),
            table_ref[j * cells : (j + 1) * cells, :],
            preferred_element_type=F32,
        )
    for k in range(planes):
        out_ref[k] = total[k * channels : (k + 1) * channels]


def update_kernel(chunk, tiles, *refs):
    coeffs, grads = refs[:tiles], refs[tiles : 2 * tiles]
    spectral_ref, one_ref, two_ref = refs[2 * tiles : 2 * tiles + 3]
    new_ref, new_one_ref, new_two_ref, done_ref, rows_ref = refs[-5:]
    block, width, modes = new_ref.shape
    root = math.sqrt(BIAS_TWO)
    start = pl.program_id(0) * block
    done_ref[...] = jnp.zeros_like(done_ref)

    @pl.loop(0, modes // LANES)
    def _(tile):
        at = pl.ds(pl.multiple_of(tile * LANES, LANES), LANES)
        for t in range(len(grads)):
            for c in range(block):
                rows_ref[t, c] = jnp.broadcast_to(coeffs[t][c : c + 1, at], (8, LANES))
        for o in range(0, width, 16):
            held = [[g[o + k : o + k + 8, at] for k in (0, 8)] for g in grads]
            for c in range(block):
                rows = [rows_ref[t, c] for t in range(len(grads))]
                halves = []
                for k in range(2):
                    part = rows[0] * held[0][k]
                    for t in range(1, len(grads)):
                        part = part + rows[t] * held[t][k]
                    halves.append(part)
                gradient = jnp.concatenate(halves, axis=0)
                at_o = slice(o, o + 16)
                given = (start + c, slice(chunk * width + o, chunk * width + o + 16), at)
                first = BETA_ONE * one_ref[c, at_o, at].astype(F32) + gradient
                second = BETA_TWO * two_ref[c, at_o, at].astype(F32) + (
                    (1.0 - BETA_TWO) / (1.0 - BETA_ONE) ** 2
                ) * (gradient * gradient)
                denominator = second * lax.rsqrt(second) + EPSILON * root
                new_ref[c, at_o, at] = spectral_ref[given] - (LEARN_RATE / BIAS_ONE * root) * (
                    first / denominator
                )
                new_one_ref[c, at_o, at] = first.astype(BF16)
                new_two_ref[c, at_o, at] = second.astype(BF16)


def from_ring(array, axis):
    count = lax.axis_size(axis)
    if count > 8:
        return [lax.all_gather(array, axis)]
    return [array] + [
        lax.ppermute(array, axis, [(i, (i + b) % count) for i in range(count)])
        for b in range(1, count)
    ]


def load_kernel(n, *refs):
    given, held, sems = refs[:n], refs[n + 1 : 2 * n + 1], refs[-1]
    pieces = sems.shape[1]
    copies = []
    for k in range(n):
        step = given[k].shape[0] // pieces
        for p in range(pieces):
            at = pl.ds(p * step, step)
            copies.append(
                pltpu.make_async_copy(given[k].at[at], held[k].at[at], sems.at[k, p])
            )
    for copy in copies:
        copy.start()
    for copy in copies:
        copy.wait()


def loaded(arrays, after, limit):
    n = len(arrays)
    held = [pltpu.VMEM(a.shape, a.dtype) for a in arrays]
    return pl.pallas_call(
        functools.partial(load_kernel, n),
        in_specs=[ANY_SPEC] * (n + 1),
        out_specs=[VMEM_SPEC] * n,
        out_shape=held,
        scratch_shapes=[pltpu.SemaphoreType.DMA((n, 4))],
        compiler_params=params(limit),
        cost_estimate=SMALL_COST,
        name="load",
    )(*[in_hbm(a) for a in arrays], after)


def passed_kernel(*refs):
    del refs


def passed_after(arrays, after):
    n = len(arrays)
    return pl.pallas_call(
        passed_kernel,
        in_specs=[ANY_SPEC] * (n + 1),
        out_specs=[ANY_SPEC] * n,
        out_shape=[jax.ShapeDtypeStruct(a.shape, a.dtype) for a in arrays],
        input_output_aliases={k: k for k in range(n)},
        compiler_params=params(VMEM_LIMIT),
        name="passed",
    )(*arrays, after)


def of_every_core(behind):
    count = lax.axis_size("gy")
    arrays = list(behind)
    for b in range(1, count):
        arrays += [
            lax.ppermute(a, "gy", [(i, (i + b) % count) for i in range(count)]) for a in behind
        ]
    return arrays


def from_sides(up, down):
    count = lax.axis_size("gx")
    below = lax.ppermute(up, "gx", [(i, i + 1) for i in range(count - 1)])
    above = lax.ppermute(down, "gx", [(i + 1, i) for i in range(count - 1)])
    return below, above


HALVES = 2
MIX_BLOCK = 8
UPDATE_BLOCK = 8
UPDATE_CHUNKS = 2


def per_device(
    state, damping, absorb_mask, lift_gain, proj_weight, spectral, moment_one, moment_two
):
    count = lax.axis_size("gx")
    cells = state.shape[-1]
    channels = lift_gain.shape[0]
    modes = spectral.shape[0]
    planes = PLANES // HALVES
    slopes, to_grid, faces = (jnp.asarray(t) for t in solver_tables())
    joint = joint_table()
    forward = jnp.asarray(joint)
    table = jnp.asarray(np.ascontiguousarray(joint.T))
    fx = jnp.asarray(rounded(fourier_table(PLANES * count, KM)).astype(np.float32))
    me = lax.axis_index("gx").astype(jnp.int32).reshape(1)
    flat = state.reshape(-1, LANES)
    gain_row = lift_gain.reshape(1, channels)
    weight_row = proj_weight.reshape(1, channels)
    spectral_t, one_t, two_t = (
        jnp.transpose(a, (1, 2, 0)) for a in (spectral, moment_one, moment_two)
    )
    faces_out = jax.ShapeDtypeStruct((64, cells), F32)
    half_planes = jax.ShapeDtypeStruct((planes, channels, JOINT), F32)

    def shape_of(array):
        return jax.ShapeDtypeStruct(array.shape, array.dtype)

    given = (flat, gain_row, to_grid, table, absorb_mask, damping, slopes, faces)
    lifted, mid, up, down = pl.pallas_call(
        lift_kernel,
        in_specs=[SMEM_SPEC] + [ANY_SPEC] * len(given),
        out_specs=[VMEM_SPEC] * 4,
        out_shape=[
            jax.ShapeDtypeStruct((PLANES, channels, JOINT), F32),
            jax.ShapeDtypeStruct((4, LANES, cells), F32),
            faces_out,
            faces_out,
        ],
        scratch_shapes=[pltpu.VMEM(a.shape, a.dtype) for a in given]
        + [pltpu.SemaphoreType.DMA((len(given),))],
        compiler_params=params(VMEM_LIMIT),
        cost_estimate=SMALL_COST,
        name="lift",
    )(me, *[in_hbm(a) for a in given])
    gathered = from_ring(lifted, "gx")
    (spectral_held,) = loaded([spectral_t], mid, VMEM_LIMIT)
    below, above = from_sides(*passed_after([up, down], spectral_held))
    coeffs, mixed = pl.pallas_call(
        functools.partial(mix_kernel, count),
        in_specs=[SMEM_SPEC, SMEM_SPEC] + [VMEM_SPEC] * (len(gathered) + 1) + [ANY_SPEC] * 2,
        out_specs=[VMEM_SPEC] * 2,
        out_shape=[
            jax.ShapeDtypeStruct((channels, modes), F32),
            jax.ShapeDtypeStruct((channels, modes), BF16),
        ],
        compiler_params=params(),
        cost_estimate=SMALL_COST,
        name="mix",
    )(me, fx, *gathered, in_vmem(spectral_held), below, above)
    every_mixed = from_ring(mixed, "gx")
    behind = from_ring(coeffs, "grp")

    new_flat, target = pl.pallas_call(
        second_stage_kernel,
        in_specs=[VMEM_SPEC] * 9 + [ANY_SPEC],
        out_specs=[VMEM_SPEC] * 2,
        out_shape=[
            shape_of(flat),
            jax.ShapeDtypeStruct((PLANES * CELLS, cells), F32),
        ],
        compiler_params=params(),
        cost_estimate=SMALL_COST,
        name="second_stage",
    )(
        flat, mid, below, above, absorb_mask, damping, slopes, faces, to_grid, mixed,
    )

    gathered = []
    back = mixed
    for half in range(HALVES):
        back = pl.pallas_call(
            functools.partial(backward_kernel, count, half),
            in_specs=[SMEM_SPEC, SMEM_SPEC] + [VMEM_SPEC] * (len(every_mixed) + 4) + [ANY_SPEC] * 2,
            out_specs=VMEM_SPEC,
            out_shape=half_planes,
            scratch_shapes=[pltpu.VMEM((planes * channels, JOINT), F32)],
            compiler_params=params(),
            cost_estimate=SMALL_COST,
            name=f"backward_{half}",
        )(me, fx, *every_mixed, weight_row, target, forward, table, back, behind[half])
        gathered.append(from_ring(back, "gx"))
    flat_parts = [a for half in gathered for a in half]
    width = channels // UPDATE_CHUNKS
    grad_coeffs = pl.pallas_call(
        functools.partial(coeffs_kernel, count, HALVES),
        in_specs=[SMEM_SPEC, SMEM_SPEC] + [VMEM_SPEC] * len(flat_parts) + [ANY_SPEC] * len(behind),
        out_specs=[VMEM_SPEC] * UPDATE_CHUNKS,
        out_shape=[jax.ShapeDtypeStruct((width, modes), F32)] * UPDATE_CHUNKS,
        compiler_params=params(VMEM_LIMIT),
        cost_estimate=SMALL_COST,
        name="grad_coeffs",
    )(me, fx, *flat_parts, *behind)
    every_coeffs = of_every_core(behind)

    behind = [from_ring(grad_coeffs[0], "grp")]
    for chunk in range(1, UPDATE_CHUNKS):
        behind.append(from_ring(passed_after([grad_coeffs[chunk]], behind[-1][-1])[0], "grp"))
    tiles = len(every_coeffs)
    outs = None
    for chunk in range(UPDATE_CHUNKS):
        if outs is not None:
            behind[chunk] = passed_after(behind[chunk], outs[3])
        grads = of_every_core(behind[chunk])
        cube = pl.BlockSpec((UPDATE_BLOCK, width, modes), lambda i, chunk=chunk: (i, chunk, 0))
        given = [*every_coeffs, *grads]
        given += [in_vmem(spectral_held), in_hbm(one_t), in_hbm(two_t)]
        specs = [pl.BlockSpec((UPDATE_BLOCK, modes), lambda i: (i, 0))] * tiles
        specs += [VMEM_SPEC] * (tiles + 1) + [cube] * 2
        aliases = {}
        if outs is not None:
            aliases = {len(given) + k: k for k in range(3)}
            given += [in_hbm(a) for a in outs[:3]]
            specs += [ANY_SPEC] * 3
        outs = pl.pallas_call(
            functools.partial(update_kernel, chunk, tiles),
            grid=(channels // UPDATE_BLOCK,),
            in_specs=specs,
            out_specs=[cube] * 3 + [pl.BlockSpec((8, LANES), lambda i: (0, 0))],
            out_shape=[shape_of(a) for a in (spectral_t, one_t, two_t)]
            + [jax.ShapeDtypeStruct((8, LANES), F32)],
            scratch_shapes=[pltpu.VMEM((tiles, UPDATE_BLOCK, 8, LANES), F32)],
            input_output_aliases=aliases,
            compiler_params=params(UPDATE_VMEM, dimension_semantics=("arbitrary",)),
            cost_estimate=SMALL_COST,
            name=f"update_{chunk}",
        )(*given)
    new_spectral, new_one, new_two = (jnp.transpose(a, (2, 0, 1)) for a in outs[:3])
    return new_flat.reshape(state.shape), new_spectral, new_one, new_two


def solution(mesh):
    in_specs = (
        P(("grp", "gy"), None, None, "gx", None),
        P("gx", None),
        P("gx", None),
        P(),
        P(),
        P("gx", None, None),
        P("gx", None, None),
        P("gx", None, None),
    )
    out_specs = (
        P(("grp", "gy"), None, None, "gx", None),
        P("gx", None, None),
        P("gx", None, None),
        P("gx", None, None),
    )
    return jax.shard_map(
        per_device, mesh=mesh, in_specs=in_specs, out_specs=out_specs, check_vma=False
    )
```

time: 169 us -> 124 us (0.73)
  starting transfers between devices: 66 us -> 44.4 us
  waiting for transfers between devices: 29.2 us -> 17.8 us
  Pallas kernels: 67.6 us -> 60 us
  local copies, waits for them, and re-layouts: 4.81 us -> 0.07 us
    ppermute x30 -> x21, starting transfers between devices: 52.7 us -> 36.4 us  [from_ring(): lax.ppermute(array, axis, [(i, (i + b) % count) for i in range(count)])]
    pallas_call x9, Pallas kernels: 57.4 us -> 49.7 us  [the longest x2 30.9 us: per_device(): pl.pallas_call(functools.partial(update_kernel, chunk, tiles), grid=(chan...]
    ppermute x30 -> x21, waiting for transfers between devices: 17.9 us -> 11.9 us  [from_ring(): lax.ppermute(array, axis, [(i, (i + b) % count) for i in range(count)])]
    unnamed x30 -> x20, local copies, waits for them, and re-layouts: 4.79 us -> 0.07 us
    ppermute x2 -> x1, waiting for transfers between devices: 8.46 us -> 4.65 us  [from_sides(): above = lax.ppermute(down, 'gx', [(i + 1, i) for i in range(count - 1)])]
    ppermute x2 -> x1, starting transfers between devices: 6.77 us -> 4.3 us  [from_sides(): below = lax.ppermute(up, 'gx', [(i, i + 1) for i in range(count - 1)])]
    ppermute x20 -> x12, starting transfers between devices: 3.74 us -> 2.11 us  [of_every_core(): lax.ppermute(a, 'gy', [(i, (i + b) % count) for i in range(count)])]
  transfers between devices with their start and end apart: 54 -> 35, of which waited for: 16 -> 9; matrix products, arithmetic and copies ran while one was open for 0% -> 0% of each run, Pallas kernels for 24% -> 27%
where the time goes in v2:
time: 124 us; the launch traced here: 123 us
  Pallas kernels  60 us (48%)
  starting transfers between devices  44.4 us (36%)
  waiting for transfers between devices  17.8 us (14%)
    ppermute x21, starting transfers between devices, from_ring(): lax.ppermute(array, axis, [(i, (i + b) % count) for i in range(count)])  36.4 us
    pallas_call x2, Pallas kernels, per_device(): pl.pallas_call(functools.partial(update_kernel, chunk, tiles), grid=(chan...  30.9 us
    ppermute x21, waiting for transfers between devices, from_ring(): lax.ppermute(array, axis, [(i, (i + b) % count) for i in range(count)])  11.9 us
    pallas_call x2, Pallas kernels, per_device(): pl.pallas_call(functools.partial(backward_kernel, count, half), in_specs=...  9.2 us
    pallas_call x1, Pallas kernels, per_device(): pl.pallas_call(lift_kernel, in_specs=[SMEM_SPEC] + [ANY_SPEC] * len(given...  7.22 us
    pallas_call x1, Pallas kernels, loaded(): pl.pallas_call(functools.partial(load_kernel, n), in_specs=[ANY_SPEC] * (...  5.89 us
    ppermute x1, waiting for transfers between devices, from_sides(): above = lax.ppermute(down, 'gx', [(i + 1, i) for i in range(count - 1)])  4.65 us
    ppermute x1, starting transfers between devices, from_sides(): below = lax.ppermute(up, 'gx', [(i, i + 1) for i in range(count - 1)])  4.3 us
  transfers between devices with their start and end apart: 35, of which 9 were waited for; matrix products, arithmetic and copies ran while one was open for 0% of the time, Pallas kernels for 27%

profile of v2, /device:TPU:0, one launch (start us, length us, event | category | flops | bytes accessed | tf_op | source)
XLA Modules:
  0.0 123.3 jit_solution(3237851666930300404)
XLA Ops:
  0.6 7.2 %lift.1 = (f32[4,64,256]{2,1,0:T(8,128)S(1)}, f32[4,128,256]{2,1,0:T(8,128)S(1)}, f32[64,256]{1,0:T(8,128)S(1)}, f32[64,256]{1,0:T(8,128)S(1)}) custom-call(s32[1]{0:T(128)} %bitcast.1.me_ref, f32[1000,128]{1,0:T(8,128)} %bitcast.11, f32[1,64]{1,0:T(1,128)} %bitcast.23, f32[64,128]{1,0:T(8,128)} %constant.19.clone.refs_2_.to_grid_ref, ...), custom_call_target="tpu_custom_call" | custom-call | flops 1000 | bytes 1000 | tf_op jit(solution)/shard_map/lift/pallas_call | solution.py:577
  7.9 4.0 %collective-permute-start.4 = (f32[4,64,256]{2,1,0:T(8,128)S(1)}, f32[4,64,256]{2,1,0:T(8,128)S(1)}, u32[]{:S(2)}, u32[]{:S(2)}) collective-permute-start(f32[4,64,256]{2,1,0:T(8,128)S(1)} %get-tuple-element.32.refs_0_), channel_id=1, source_target_pairs={{0,6},{2,0},{4,2},{6,4},{1,7},{3,1},{5,3},{7,5},{8,14},{10,8},{12,... | collective-permute-start | bytes 786440 | tf_op jit(solution)/shard_map/ppermute | solution.py:473
  11.8 0.5 collective-permute-start.3
  12.3 0.6 collective-permute-start.2
  12.9 5.9 %load.1.refs_2_.refs_4_.refs_16_ = f32[64,64,1024]{2,1,0:T(8,128)S(1)} custom-call(f32[64,64,1024]{2,1,0:T(8,128)} %bitcast.19, f32[4,128,256]{2,1,0:T(8,128)S(1)} %get-tuple-element.27.refs_1_.mid_ref), custom_call_target="tpu_custom_call" | custom-call | flops 1000 | bytes 1000 | tf_op jit(solution)/shard_map/load/pallas_call | solution.py:498
  18.8 0.0 copy-start.5
  18.8 4.3 %collective-permute-start = (f32[64,256]{1,0:T(8,128)S(1)}, f32[64,256]{1,0:T(8,128)S(1)}, u32[]{:S(2)}, u32[]{:S(2)}) collective-permute-start(f32[64,256]{1,0:T(8,128)S(1)} %get-tuple-element.30), channel_id=1, source_target_pairs={{0,2},{2,4},{4,6},{1,3},{3,5},{5,7},{8,10},{10,12},{12,14},{9,11},... | collective-permute-start | bytes 196616 | tf_op jit(solution)/shard_map/ppermute | solution.py:539
  23.2 0.0 copy-start.4
  23.2 0.0 copy-start.6
  23.2 0.0 copy-start
  23.2 1.6 %collective-permute-start.1 = (f32[64,256]{1,0:T(8,128)S(1)}, f32[64,256]{1,0:T(8,128)S(1)}, u32[]{:S(2)}, u32[]{:S(2)}) collective-permute-start(f32[64,256]{1,0:T(8,128)S(1)} %get-tuple-element.31), channel_id=1, source_target_pairs={{2,0},{4,2},{6,4},{3,1},{5,3},{7,5},{10,8},{12,10},{14,12},{11,9},... | collective-permute-start | bytes 196616 | tf_op jit(solution)/shard_map/ppermute | solution.py:540
  24.8 0.2 collective-permute-done.refs_5_.below_ref
  25.0 4.6 %collective-permute-done.1.refs_6_.above_ref = f32[64,256]{1,0:T(8,128)S(1)} collective-permute-done((f32[64,256]{1,0:T(8,128)S(1)}, f32[64,256]{1,0:T(8,128)S(1)}, u32[]{:S(2)}, u32[]{:S(2)}) %collective-permute-start.1) | collective-permute-done | bytes 65568 | tf_op jit(solution)/shard_map/ppermute | solution.py:540
  29.7 3.8 %mix.1 = (f32[64,1024]{1,0:T(8,128)S(1)}, bf16[64,1024]{1,0:T(8,128)(2,1)S(1)}) custom-call(s32[1]{0:T(128)} %bitcast.1.me_ref, f32[16,16]{1,0:T(8,128)S(1)} %copy-done.5, f32[4,64,256]{2,1,0:T(8,128)S(1)} %get-tuple-element.32.refs_0_, f32[4,64,256]{2,1,0:T(8,128)S(1)} %collective-permute-done.2.refs_1_, f32[4,64,256]{2,1,0:T(8,128)S(1)} %collective-permute-done.3.refs_2_, ...), custom_call_target="tpu_custom_call" | custom-call | flops 1000 | bytes 1000 | tf_op jit(solution)/shard_map/mix/pallas_call | solution.py:596
  33.5 0.1 collective-permute-start.14
  33.6 2.4 %collective-permute-start.13 = (bf16[64,1024]{1,0:T(8,128)(2,1)S(1)}, bf16[64,1024]{1,0:T(8,128)(2,1)S(1)}, u32[]{:S(2)}, u32[]{:S(2)}) collective-permute-start(bf16[64,1024]{1,0:T(8,128)(2,1)S(1)} %get-tuple-element.33.after_ref.refs_0_.refs_8_), channel_id=1, source_target_pairs={{0,4},{2,6},{4,0},{6,2},{1,5},{3,7},{5,1},{7,3},{8,12},{10,14},{12... | collective-permute-start | bytes 393224 | tf_op jit(solution)/shard_map/ppermute | solution.py:473
  35.9 0.2 collective-permute-start.12
  36.1 1.6 %collective-permute-start.5 = (f32[64,1024]{1,0:T(8,128)S(1)}, f32[64,1024]{1,0:T(8,128)S(1)}, u32[]{:S(2)}, u32[]{:S(2)}) collective-permute-start(f32[64,1024]{1,0:T(8,128)S(1)} %get-tuple-element.35.refs_9_.refs_8_.refs_0_), channel_id=1, source_target_pairs={{0,8},{8,16},{16,24},{24,0},{1,9},{9,17},{17,25},{25,1},{2,10},{10... | collective-permute-start | bytes 786440 | tf_op jit(solution)/shard_map/ppermute | solution.py:473
  37.7 2.2 %collective-permute-start.7 = (f32[64,1024]{1,0:T(8,128)S(1)}, f32[64,1024]{1,0:T(8,128)S(1)}, u32[]{:S(2)}, u32[]{:S(2)}) collective-permute-start(f32[64,1024]{1,0:T(8,128)S(1)} %get-tuple-element.35.refs_9_.refs_8_.refs_0_), channel_id=1, source_target_pairs={{0,24},{8,0},{16,8},{24,16},{1,25},{9,1},{17,9},{25,17},{2,26},{10... | collective-permute-start | bytes 786440 | tf_op jit(solution)/shard_map/ppermute | solution.py:473
  40.0 1.9 %second_stage.1 = (f32[1000,128]{1,0:T(8,128)}, f32[64,256]{1,0:T(8,128)S(1)}) custom-call(f32[1000,128]{1,0:T(8,128)S(1)} %bitcast.12, f32[4,128,256]{2,1,0:T(8,128)S(1)} %get-tuple-element.27.refs_1_.mid_ref, f32[64,256]{1,0:T(8,128)S(1)} %collective-permute-done.refs_5_.below_ref, f32[64,256]{1,0:T(8,128)S(1)} %collective-permute-done.1.refs_6_.above_ref, ...), custom_call_target="tpu_custom_call" | custom-call | flops 1000 | bytes 1000 | tf_op jit(solution)/shard_map/second_stage/pallas_call | solution.py:611
  41.8 0.8 collective-permute-start.6
  42.7 4.6 %backward_0.1.refs_8_.refs_0_ = f32[2,64,256]{2,1,0:T(8,128)S(1)} custom-call(s32[1]{0:T(128)} %bitcast.1.me_ref, f32[16,16]{1,0:T(8,128)S(1)} %copy-done.5, bf16[64,1024]{1,0:T(8,128)(2,1)S(1)} %get-tuple-element.33.after_ref.refs_0_.refs_8_, bf16[64,1024]{1,0:T(8,128)(2,1)S(1)} %collective-permute-done.12.refs_1_, ...), custom_call_target="tpu_custom_call" | custom-call | flops 1000 | bytes 1000 | tf_op jit(solution)/shard_map/backward_0/pallas_call | solution.py:629
  47.3 2.8 %collective-permute-start.17 = (f32[2,64,256]{2,1,0:T(8,128)S(1)}, f32[2,64,256]{2,1,0:T(8,128)S(1)}, u32[]{:S(2)}, u32[]{:S(2)}) collective-permute-start(f32[2,64,256]{2,1,0:T(8,128)S(1)} %backward_0.1.refs_8_.refs_0_), channel_id=1, source_target_pairs={{0,6},{2,0},{4,2},{6,4},{1,7},{3,1},{5,3},{7,5},{8,14},{10,8},{12,... | collective-permute-start | bytes 393224 | tf_op jit(solution)/shard_map/ppermute | solution.py:473
  50.1 0.8 collective-permute-start.15
  50.9 4.6 %backward_1.1.refs_4_ = f32[2,64,256]{2,1,0:T(8,128)S(1)} custom-call(s32[1]{0:T(128)} %bitcast.1.me_ref, f32[16,16]{1,0:T(8,128)S(1)} %copy-done.5, bf16[64,1024]{1,0:T(8,128)(2,1)S(1)} %get-tuple-element.33.after_ref.refs_0_.refs_8_, bf16[64,1024]{1,0:T(8,128)(2,1)S(1)} %collective-permute-done.12.refs_1_, ...), custom_call_target="tpu_custom_call" | custom-call | flops 1000 | bytes 1000 | tf_op jit(solution)/shard_map/backward_1/pallas_call | solution.py:629
  55.5 2.2 %collective-permute-start.20 = (f32[2,64,256]{2,1,0:T(8,128)S(1)}, f32[2,64,256]{2,1,0:T(8,128)S(1)}, u32[]{:S(2)}, u32[]{:S(2)}) collective-permute-start(f32[2,64,256]{2,1,0:T(8,128)S(1)} %backward_1.1.refs_4_), channel_id=1, source_target_pairs={{0,6},{2,0},{4,2},{6,4},{1,7},{3,1},{5,3},{7,5},{8,14},{10,8},{12,... | collective-permute-start | bytes 393224 | tf_op jit(solution)/shard_map/ppermute | solution.py:473
  57.7 0.5 collective-permute-start.11
  58.2 2.0 %collective-permute-start.19 = (f32[2,64,256]{2,1,0:T(8,128)S(1)}, f32[2,64,256]{2,1,0:T(8,128)S(1)}, u32[]{:S(2)}, u32[]{:S(2)}) collective-permute-start(f32[2,64,256]{2,1,0:T(8,128)S(1)} %backward_1.1.refs_4_), channel_id=1, source_target_pairs={{0,4},{2,6},{4,0},{6,2},{1,5},{3,7},{5,1},{7,3},{8,12},{10,14},{12... | collective-permute-start | bytes 393224 | tf_op jit(solution)/shard_map/ppermute | solution.py:473
  60.2 1.4 %collective-permute-start.18 = (f32[2,64,256]{2,1,0:T(8,128)S(1)}, f32[2,64,256]{2,1,0:T(8,128)S(1)}, u32[]{:S(2)}, u32[]{:S(2)}) collective-permute-start(f32[2,64,256]{2,1,0:T(8,128)S(1)} %backward_1.1.refs_4_), channel_id=1, source_target_pairs={{0,2},{2,4},{4,6},{6,0},{1,3},{3,5},{5,7},{7,1},{8,10},{10,12},{12... | collective-permute-start | bytes 393224 | tf_op jit(solution)/shard_map/ppermute | solution.py:473
  61.6 5.2 %collective-permute-done.19.refs_6_ = f32[2,64,256]{2,1,0:T(8,128)S(1)} collective-permute-done((f32[2,64,256]{2,1,0:T(8,128)S(1)}, f32[2,64,256]{2,1,0:T(8,128)S(1)}, u32[]{:S(2)}, u32[]{:S(2)}) %collective-permute-start.19) | collective-permute-done | bytes 131104 | tf_op jit(solution)/shard_map/ppermute | solution.py:473
  66.8 1.0 grad_coeffs.1
  67.8 7.5 %collective-permute-start.26 = (f32[32,1024]{1,0:T(8,128)S(1)}, f32[32,1024]{1,0:T(8,128)S(1)}, u32[]{:S(2)}, u32[]{:S(2)}) collective-permute-start(f32[32,1024]{1,0:T(8,128)S(1)} %get-tuple-element.38.refs_8_), channel_id=1, source_target_pairs={{0,16},{8,24},{16,0},{24,8},{1,17},{9,25},{17,1},{25,9},{2,18},{10... | collective-permute-start | bytes 393224 | tf_op jit(solution)/shard_map/ppermute | solution.py:473
  75.3 3.8 %collective-permute-start.21 = (f32[32,1024]{1,0:T(8,128)S(1)}, f32[32,1024]{1,0:T(8,128)S(1)}, u32[]{:S(2)}, u32[]{:S(2)}) collective-permute-start(f32[32,1024]{1,0:T(8,128)S(1)} %get-tuple-element.38.refs_8_), channel_id=1, source_target_pairs={{0,24},{8,0},{16,8},{24,16},{1,25},{9,1},{17,9},{25,17},{2,26},{10... | collective-permute-start | bytes 393224 | tf_op jit(solution)/shard_map/ppermute | solution.py:473
  79.2 6.2 %collective-permute-done.26.refs_10_ = f32[32,1024]{1,0:T(8,128)S(1)} collective-permute-done((f32[32,1024]{1,0:T(8,128)S(1)}, f32[32,1024]{1,0:T(8,128)S(1)}, u32[]{:S(2)}, u32[]{:S(2)}) %collective-permute-start.26) | collective-permute-done | bytes 131104 | tf_op jit(solution)/shard_map/ppermute | solution.py:473
  85.3 0.5 collective-permute-start.28
  85.9 0.5 collective-permute-done.21.refs_1_.refs_11_
  86.4 2.4 %collective-permute-start.24 = (f32[32,1024]{1,0:T(8,128)S(1)}, f32[32,1024]{1,0:T(8,128)S(1)}, u32[]{:S(2)}, u32[]{:S(2)}) collective-permute-start(f32[32,1024]{1,0:T(8,128)S(1)} %passed.4.refs_0_), channel_id=1, source_target_pairs={{0,24},{8,0},{16,8},{24,16},{1,25},{9,1},{17,9},{25,17},{2,26},{10... | collective-permute-start | bytes 393224 | tf_op jit(solution)/shard_map/ppermute | solution.py:473
  88.8 1.3 %collective-permute-start.23 = (f32[32,1024]{1,0:T(8,128)S(1)}, f32[32,1024]{1,0:T(8,128)S(1)}, u32[]{:S(2)}, u32[]{:S(2)}) collective-permute-start(f32[32,1024]{1,0:T(8,128)S(1)} %passed.4.refs_0_), channel_id=1, source_target_pairs={{0,16},{8,24},{16,0},{24,8},{1,17},{9,25},{17,1},{25,9},{2,18},{10... | collective-permute-start | bytes 393224 | tf_op jit(solution)/shard_map/ppermute | solution.py:473
  90.1 15.5 %update_0.1 = (f32[64,64,1024]{2,1,0:T(8,128)}, bf16[64,64,1024]{2,1,0:T(8,128)(2,1)}, bf16[64,64,1024]{2,1,0:T(8,128)(2,1)}, f32[8,128]{1,0:T(8,128)S(1)}) custom-call(f32[64,1024]{1,0:T(8,128)S(1)} %get-tuple-element.35.refs_9_.refs_8_.refs_0_, f32[64,1024]{1,0:T(8,128)S(1)} %collective-permute-done.5.refs_9_.refs_1_, ...), custom_call_target="tpu_custom_call" | custom-call | flops 1000 | bytes 1000 | tf_op jit(solution)/shard_map/update_0/pallas_call | solution.py:672
  105.6 0.1 collective-permute-start.31
  105.7 0.5 collective-permute-start.32
  106.2 0.1 collective-permute-start.33
  106.2 0.4 collective-permute-start.34
  106.7 0.3 collective-permute-done.31.refs_12_
  107.0 0.2 collective-permute-done.32.refs_13_
  107.2 0.3 collective-permute-done.33.refs_14_
  107.5 0.2 collective-permute-done.34.refs_15_
  107.7 15.4 %update_1.1 = (f32[64,64,1024]{2,1,0:T(8,128)}, bf16[64,64,1024]{2,1,0:T(8,128)(2,1)}, bf16[64,64,1024]{2,1,0:T(8,128)(2,1)}, f32[8,128]{1,0:T(8,128)}) custom-call(f32[64,1024]{1,0:T(8,128)S(1)} %get-tuple-element.35.refs_9_.refs_8_.refs_0_, ...), custom_call_target="tpu_custom_call", output_to_operand_aliasing={{0}: (19, {}), {1}: (20, {}), {2}: (21, {})} | custom-call | flops 1000 | bytes 1000 | tf_op jit(solution)/shard_map/update_1/pallas_call | solution.py:672
  (54 shorter events, 0.1 us)
Async XLA Ops:
  7.9 21.8 %collective-permute-start.4 = (f32[4,64,256]{2,1,0:T(8,128)S(1)}, f32[4,64,256]{2,1,0:T(8,128)S(1)}, u32[]{:S(2)}, u32[]{:S(2)}) collective-permute-start(f32[4,64,256]{2,1,0:T(8,128)S(1)} %get-tuple-element.32.refs_0_), channel_id=1, source_target_pairs={{0,6},{2,0},{4,2},{6,4},{1,7},{3,1},{5,3},{7,5},{8,14},{10,8},{12,... | collective-permute-start | bytes 786440 | tf_op jit(solution)/shard_map/ppermute | solution.py:473
  11.8 17.9 %collective-permute-start.3 = (f32[4,64,256]{2,1,0:T(8,128)S(1)}, f32[4,64,256]{2,1,0:T(8,128)S(1)}, u32[]{:S(2)}, u32[]{:S(2)}) collective-permute-start(f32[4,64,256]{2,1,0:T(8,128)S(1)} %get-tuple-element.32.refs_0_), channel_id=1, source_target_pairs={{0,4},{2,6},{4,0},{6,2},{1,5},{3,7},{5,1},{7,3},{8,12},{10,14},{12... | collective-permute-start | bytes 786440 | tf_op jit(solution)/shard_map/ppermute | solution.py:473
  12.3 17.4 %collective-permute-start.2 = (f32[4,64,256]{2,1,0:T(8,128)S(1)}, f32[4,64,256]{2,1,0:T(8,128)S(1)}, u32[]{:S(2)}, u32[]{:S(2)}) collective-permute-start(f32[4,64,256]{2,1,0:T(8,128)S(1)} %get-tuple-element.32.refs_0_), channel_id=1, source_target_pairs={{0,2},{2,4},{4,6},{6,0},{1,3},{3,5},{5,7},{7,1},{8,10},{10,12},{12... | collective-permute-start | bytes 786440 | tf_op jit(solution)/shard_map/ppermute | solution.py:473
  18.8 10.9 %copy-start.5 = (f32[16,16]{1,0:T(8,128)S(1)}, f32[16,16]{1,0:T(8,128)}, u32[]{:S(2)}) copy-start(f32[16,16]{1,0:T(8,128)} %constant.23.clone.fx_ref) | copy-start | bytes 3076
  18.8 6.2 %collective-permute-start = (f32[64,256]{1,0:T(8,128)S(1)}, f32[64,256]{1,0:T(8,128)S(1)}, u32[]{:S(2)}, u32[]{:S(2)}) collective-permute-start(f32[64,256]{1,0:T(8,128)S(1)} %get-tuple-element.30), channel_id=1, source_target_pairs={{0,2},{2,4},{4,6},{1,3},{3,5},{5,7},{8,10},{10,12},{12,14},{9,11},... | collective-permute-start | bytes 196616 | tf_op jit(solution)/shard_map/ppermute | solution.py:539
  23.1 16.8 %copy-start.2 = (f32[1,4,125,1,256]{4,3,2,1,0:T(1,128)S(1)}, f32[1,4,125,1,256]{4,3,2,1,0:T(1,128)}, u32[]{:S(2)}) copy-start(f32[1,4,125,1,256]{4,3,2,1,0:T(1,128)} %param.14) | copy-start | bytes 1536004
  23.1 16.8 %copy-start.3 = (f32[384,128]{1,0:T(8,128)S(1)}, f32[384,128]{1,0:T(8,128)}, u32[]{:S(2)}) copy-start(f32[384,128]{1,0:T(8,128)} %constant.18.clone.refs_6_.slopes_ref) | copy-start | bytes 589828
  23.2 16.8 %copy-start.4 = (f32[128,128]{1,0:T(8,128)S(1)}, f32[128,128]{1,0:T(8,128)}, u32[]{:S(2)}) copy-start(f32[128,128]{1,0:T(8,128)} %constant.20.clone.refs_7_.faces_ref) | copy-start | bytes 196612
  23.2 16.8 %copy-start.6 = (f32[64,128]{1,0:T(8,128)S(1)}, f32[64,128]{1,0:T(8,128)}, u32[]{:S(2)}) copy-start(f32[64,128]{1,0:T(8,128)} %constant.19.clone.refs_2_.to_grid_ref) | copy-start | bytes 98308
  23.2 16.8 %copy-start.7 = (s32[1,256]{1,0:T(1,128)S(1)}, s32[1,256]{1,0:T(1,128)}, u32[]{:S(2)}) copy-start(s32[1,256]{1,0:T(1,128)} %mask_ref.1) | copy-start | bytes 3076
  23.2 16.7 %copy-start.8 = (f32[1,256]{1,0:T(1,128)S(1)}, f32[1,256]{1,0:T(1,128)}, u32[]{:S(2)}) copy-start(f32[1,256]{1,0:T(1,128)} %damping_ref.1) | copy-start | bytes 3076
  23.2 19.4 %copy-start = (bf16[4096,256]{1,0:T(8,128)(2,1)S(1)}, bf16[4096,256]{1,0:T(8,128)(2,1)}, u32[]{:S(2)}) copy-start(bf16[4096,256]{1,0:T(8,128)(2,1)} %constant.22.clone.refs_3_.refs_7_) | copy-start | bytes 6291460
  23.2 19.4 %copy-start.1 = (bf16[256,4096]{1,0:T(8,128)(2,1)S(1)}, bf16[256,4096]{1,0:T(8,128)(2,1)}, u32[]{:S(2)}) copy-start(bf16[256,4096]{1,0:T(8,128)(2,1)} %constant.21.clone.refs_6_) | copy-start | bytes 6291460
  23.2 19.4 %copy-start.9 = (f32[64]{0:T(128)S(1)}, f32[64]{0:T(128)}, u32[]{:S(2)}) copy-start(f32[64]{0:T(128)} %param.18) | copy-start | bytes 772
  23.2 6.4 %collective-permute-start.1 = (f32[64,256]{1,0:T(8,128)S(1)}, f32[64,256]{1,0:T(8,128)S(1)}, u32[]{:S(2)}, u32[]{:S(2)}) collective-permute-start(f32[64,256]{1,0:T(8,128)S(1)} %get-tuple-element.31), channel_id=1, source_target_pairs={{2,0},{4,2},{6,4},{3,1},{5,3},{7,5},{10,8},{12,10},{14,12},{11,9},... | collective-permute-start | bytes 196616 | tf_op jit(solution)/shard_map/ppermute | solution.py:540
  33.5 8.3 %collective-permute-start.14 = (bf16[64,1024]{1,0:T(8,128)(2,1)S(1)}, bf16[64,1024]{1,0:T(8,128)(2,1)S(1)}, u32[]{:S(2)}, u32[]{:S(2)}) collective-permute-start(bf16[64,1024]{1,0:T(8,128)(2,1)S(1)} %get-tuple-element.33.after_ref.refs_0_.refs_8_), channel_id=1, source_target_pairs={{0,6},{2,0},{4,2},{6,4},{1,7},{3,1},{5,3},{7,5},{8,14},{10,8},{12,... | collective-permute-start | bytes 393224 | tf_op jit(solution)/shard_map/ppermute | solution.py:473
  33.6 9.1 %collective-permute-start.13 = (bf16[64,1024]{1,0:T(8,128)(2,1)S(1)}, bf16[64,1024]{1,0:T(8,128)(2,1)S(1)}, u32[]{:S(2)}, u32[]{:S(2)}) collective-permute-start(bf16[64,1024]{1,0:T(8,128)(2,1)S(1)} %get-tuple-element.33.after_ref.refs_0_.refs_8_), channel_id=1, source_target_pairs={{0,4},{2,6},{4,0},{6,2},{1,5},{3,7},{5,1},{7,3},{8,12},{10,14},{12... | collective-permute-start | bytes 393224 | tf_op jit(solution)/shard_map/ppermute | solution.py:473
  35.9 6.7 %collective-permute-start.12 = (bf16[64,1024]{1,0:T(8,128)(2,1)S(1)}, bf16[64,1024]{1,0:T(8,128)(2,1)S(1)}, u32[]{:S(2)}, u32[]{:S(2)}) collective-permute-start(bf16[64,1024]{1,0:T(8,128)(2,1)S(1)} %get-tuple-element.33.after_ref.refs_0_.refs_8_), channel_id=1, source_target_pairs={{0,2},{2,4},{4,6},{6,0},{1,3},{3,5},{5,7},{7,1},{8,10},{10,12},{12... | collective-permute-start | bytes 393224 | tf_op jit(solution)/shard_map/ppermute | solution.py:473
  36.1 14.0 %collective-permute-start.5 = (f32[64,1024]{1,0:T(8,128)S(1)}, f32[64,1024]{1,0:T(8,128)S(1)}, u32[]{:S(2)}, u32[]{:S(2)}) collective-permute-start(f32[64,1024]{1,0:T(8,128)S(1)} %get-tuple-element.35.refs_9_.refs_8_.refs_0_), channel_id=1, source_target_pairs={{0,8},{8,16},{16,24},{24,0},{1,9},{9,17},{17,25},{25,1},{2,10},{10... | collective-permute-start | bytes 786440 | tf_op jit(solution)/shard_map/ppermute | solution.py:473
  37.7 20.0 %collective-permute-start.7 = (f32[64,1024]{1,0:T(8,128)S(1)}, f32[64,1024]{1,0:T(8,128)S(1)}, u32[]{:S(2)}, u32[]{:S(2)}) collective-permute-start(f32[64,1024]{1,0:T(8,128)S(1)} %get-tuple-element.35.refs_9_.refs_8_.refs_0_), channel_id=1, source_target_pairs={{0,24},{8,0},{16,8},{24,16},{1,25},{9,1},{17,9},{25,17},{2,26},{10... | collective-permute-start | bytes 786440 | tf_op jit(solution)/shard_map/ppermute | solution.py:473
  41.8 18.4 %collective-permute-start.6 = (f32[64,1024]{1,0:T(8,128)S(1)}, f32[64,1024]{1,0:T(8,128)S(1)}, u32[]{:S(2)}, u32[]{:S(2)}) collective-permute-start(f32[64,1024]{1,0:T(8,128)S(1)} %get-tuple-element.35.refs_9_.refs_8_.refs_0_), channel_id=1, source_target_pairs={{0,16},{8,24},{16,0},{24,8},{1,17},{9,25},{17,1},{25,9},{2,18},{10... | collective-permute-start | bytes 786440 | tf_op jit(solution)/shard_map/ppermute | solution.py:473
  47.3 8.2 %collective-permute-start.17 = (f32[2,64,256]{2,1,0:T(8,128)S(1)}, f32[2,64,256]{2,1,0:T(8,128)S(1)}, u32[]{:S(2)}, u32[]{:S(2)}) collective-permute-start(f32[2,64,256]{2,1,0:T(8,128)S(1)} %backward_0.1.refs_8_.refs_0_), channel_id=1, source_target_pairs={{0,6},{2,0},{4,2},{6,4},{1,7},{3,1},{5,3},{7,5},{8,14},{10,8},{12,... | collective-permute-start | bytes 393224 | tf_op jit(solution)/shard_map/ppermute | solution.py:473
  50.1 7.6 %collective-permute-start.16 = (f32[2,64,256]{2,1,0:T(8,128)S(1)}, f32[2,64,256]{2,1,0:T(8,128)S(1)}, u32[]{:S(2)}, u32[]{:S(2)}) collective-permute-start(f32[2,64,256]{2,1,0:T(8,128)S(1)} %backward_0.1.refs_8_.refs_0_), channel_id=1, source_target_pairs={{0,4},{2,6},{4,0},{6,2},{1,5},{3,7},{5,1},{7,3},{8,12},{10,14},{12... | collective-permute-start | bytes 393224 | tf_op jit(solution)/shard_map/ppermute | solution.py:473
  50.1 8.1 %collective-permute-start.15 = (f32[2,64,256]{2,1,0:T(8,128)S(1)}, f32[2,64,256]{2,1,0:T(8,128)S(1)}, u32[]{:S(2)}, u32[]{:S(2)}) collective-permute-start(f32[2,64,256]{2,1,0:T(8,128)S(1)} %backward_0.1.refs_8_.refs_0_), channel_id=1, source_target_pairs={{0,2},{2,4},{4,6},{6,0},{1,3},{3,5},{5,7},{7,1},{8,10},{10,12},{12... | collective-permute-start | bytes 393224 | tf_op jit(solution)/shard_map/ppermute | solution.py:473
  55.5 6.1 %collective-permute-start.20 = (f32[2,64,256]{2,1,0:T(8,128)S(1)}, f32[2,64,256]{2,1,0:T(8,128)S(1)}, u32[]{:S(2)}, u32[]{:S(2)}) collective-permute-start(f32[2,64,256]{2,1,0:T(8,128)S(1)} %backward_1.1.refs_4_), channel_id=1, source_target_pairs={{0,6},{2,0},{4,2},{6,4},{1,7},{3,1},{5,3},{7,5},{8,14},{10,8},{12,... | collective-permute-start | bytes 393224 | tf_op jit(solution)/shard_map/ppermute | solution.py:473
  57.7 17.7 %collective-permute-start.8 = (f32[64,1024]{1,0:T(8,128)S(1)}, f32[64,1024]{1,0:T(8,128)S(1)}, u32[]{:S(2)}, u32[]{:S(2)}) collective-permute-start(f32[64,1024]{1,0:T(8,128)S(1)} %get-tuple-element.35.refs_9_.refs_8_.refs_0_), channel_id=1, source_target_pairs={{0,1},{1,0},{2,3},{3,2},{4,5},{5,4},{6,7},{7,6},{8,9},{9,8},{10,11... | collective-permute-start | bytes 786440 | tf_op jit(solution)/shard_map/ppermute | solution.py:532
  57.7 17.6 %collective-permute-start.11 = (f32[64,1024]{1,0:T(8,128)S(1)}, f32[64,1024]{1,0:T(8,128)S(1)}, u32[]{:S(2)}, u32[]{:S(2)}) collective-permute-start(f32[64,1024]{1,0:T(8,128)S(1)} %collective-permute-done.7.refs_11_.refs_3_), channel_id=1, source_target_pairs={{0,1},{1,0},{2,3},{3,2},{4,5},{5,4},{6,7},{7,6},{8,9},{9,8},{10,11... | collective-permute-start | bytes 786440 | tf_op jit(solution)/shard_map/ppermute | solution.py:532
  58.2 8.6 %collective-permute-start.19 = (f32[2,64,256]{2,1,0:T(8,128)S(1)}, f32[2,64,256]{2,1,0:T(8,128)S(1)}, u32[]{:S(2)}, u32[]{:S(2)}) collective-permute-start(f32[2,64,256]{2,1,0:T(8,128)S(1)} %backward_1.1.refs_4_), channel_id=1, source_target_pairs={{0,4},{2,6},{4,0},{6,2},{1,5},{3,7},{5,1},{7,3},{8,12},{10,14},{12... | collective-permute-start | bytes 393224 | tf_op jit(solution)/shard_map/ppermute | solution.py:473
  60.2 6.5 %collective-permute-start.18 = (f32[2,64,256]{2,1,0:T(8,128)S(1)}, f32[2,64,256]{2,1,0:T(8,128)S(1)}, u32[]{:S(2)}, u32[]{:S(2)}) collective-permute-start(f32[2,64,256]{2,1,0:T(8,128)S(1)} %backward_1.1.refs_4_), channel_id=1, source_target_pairs={{0,2},{2,4},{4,6},{6,0},{1,3},{3,5},{5,7},{7,1},{8,10},{10,12},{12... | collective-permute-start | bytes 393224 | tf_op jit(solution)/shard_map/ppermute | solution.py:473
  61.6 17.6 %collective-permute-start.10 = (f32[64,1024]{1,0:T(8,128)S(1)}, f32[64,1024]{1,0:T(8,128)S(1)}, u32[]{:S(2)}, u32[]{:S(2)}) collective-permute-start(f32[64,1024]{1,0:T(8,128)S(1)} %collective-permute-done.6.refs_10_.refs_2_), channel_id=1, source_target_pairs={{0,1},{1,0},{2,3},{3,2},{4,5},{5,4},{6,7},{7,6},{8,9},{9,8},{10,11... | collective-permute-start | bytes 786440 | tf_op jit(solution)/shard_map/ppermute | solution.py:532
  66.8 19.6 %collective-permute-start.9 = (f32[64,1024]{1,0:T(8,128)S(1)}, f32[64,1024]{1,0:T(8,128)S(1)}, u32[]{:S(2)}, u32[]{:S(2)}) collective-permute-start(f32[64,1024]{1,0:T(8,128)S(1)} %collective-permute-done.5.refs_9_.refs_1_), channel_id=1, source_target_pairs={{0,1},{1,0},{2,3},{3,2},{4,5},{5,4},{6,7},{7,6},{8,9},{9,8},{10,11... | collective-permute-start | bytes 786440 | tf_op jit(solution)/shard_map/ppermute | solution.py:532
  67.8 17.5 %collective-permute-start.26 = (f32[32,1024]{1,0:T(8,128)S(1)}, f32[32,1024]{1,0:T(8,128)S(1)}, u32[]{:S(2)}, u32[]{:S(2)}) collective-permute-start(f32[32,1024]{1,0:T(8,128)S(1)} %get-tuple-element.38.refs_8_), channel_id=1, source_target_pairs={{0,16},{8,24},{16,0},{24,8},{1,17},{9,25},{17,1},{25,9},{2,18},{10... | collective-permute-start | bytes 393224 | tf_op jit(solution)/shard_map/ppermute | solution.py:473
  75.3 10.0 %collective-permute-start.25 = (f32[32,1024]{1,0:T(8,128)S(1)}, f32[32,1024]{1,0:T(8,128)S(1)}, u32[]{:S(2)}, u32[]{:S(2)}) collective-permute-start(f32[32,1024]{1,0:T(8,128)S(1)} %get-tuple-element.38.refs_8_), channel_id=1, source_target_pairs={{0,8},{8,16},{16,24},{24,0},{1,9},{9,17},{17,25},{25,1},{2,10},{10... | collective-permute-start | bytes 393224 | tf_op jit(solution)/shard_map/ppermute | solution.py:473
  75.3 11.0 %collective-permute-start.21 = (f32[32,1024]{1,0:T(8,128)S(1)}, f32[32,1024]{1,0:T(8,128)S(1)}, u32[]{:S(2)}, u32[]{:S(2)}) collective-permute-start(f32[32,1024]{1,0:T(8,128)S(1)} %get-tuple-element.38.refs_8_), channel_id=1, source_target_pairs={{0,24},{8,0},{16,8},{24,16},{1,25},{9,1},{17,9},{25,17},{2,26},{10... | collective-permute-start | bytes 393224 | tf_op jit(solution)/shard_map/ppermute | solution.py:473
  79.2 9.6 %collective-permute-start.27 = (f32[32,1024]{1,0:T(8,128)S(1)}, f32[32,1024]{1,0:T(8,128)S(1)}, u32[]{:S(2)}, u32[]{:S(2)}) collective-permute-start(f32[32,1024]{1,0:T(8,128)S(1)} %get-tuple-element.38.refs_8_), channel_id=1, source_target_pairs={{0,1},{1,0},{2,3},{3,2},{4,5},{5,4},{6,7},{7,6},{8,9},{9,8},{10,11... | collective-permute-start | bytes 393224 | tf_op jit(solution)/shard_map/ppermute | solution.py:532
  85.3 4.7 %collective-permute-start.29 = (f32[32,1024]{1,0:T(8,128)S(1)}, f32[32,1024]{1,0:T(8,128)S(1)}, u32[]{:S(2)}, u32[]{:S(2)}) collective-permute-start(f32[32,1024]{1,0:T(8,128)S(1)} %collective-permute-done.26.refs_10_), channel_id=1, source_target_pairs={{0,1},{1,0},{2,3},{3,2},{4,5},{5,4},{6,7},{7,6},{8,9},{9,8},{10,11... | collective-permute-start | bytes 393224 | tf_op jit(solution)/shard_map/ppermute | solution.py:532
  85.3 4.7 %collective-permute-start.28 = (f32[32,1024]{1,0:T(8,128)S(1)}, f32[32,1024]{1,0:T(8,128)S(1)}, u32[]{:S(2)}, u32[]{:S(2)}) collective-permute-start(f32[32,1024]{1,0:T(8,128)S(1)} %collective-permute-done.25.refs_9_), channel_id=1, source_target_pairs={{0,1},{1,0},{2,3},{3,2},{4,5},{5,4},{6,7},{7,6},{8,9},{9,8},{10,11... | collective-permute-start | bytes 393224 | tf_op jit(solution)/shard_map/ppermute | solution.py:532
  86.4 3.7 %collective-permute-start.30 = (f32[32,1024]{1,0:T(8,128)S(1)}, f32[32,1024]{1,0:T(8,128)S(1)}, u32[]{:S(2)}, u32[]{:S(2)}) collective-permute-start(f32[32,1024]{1,0:T(8,128)S(1)} %collective-permute-done.21.refs_1_.refs_11_), channel_id=1, source_target_pairs={{0,1},{1,0},{2,3},{3,2},{4,5},{5,4},{6,7},{7,6},{8,9},{9,8},{10,11... | collective-permute-start | bytes 393224 | tf_op jit(solution)/shard_map/ppermute | solution.py:532
  86.4 19.2 %collective-permute-start.24 = (f32[32,1024]{1,0:T(8,128)S(1)}, f32[32,1024]{1,0:T(8,128)S(1)}, u32[]{:S(2)}, u32[]{:S(2)}) collective-permute-start(f32[32,1024]{1,0:T(8,128)S(1)} %passed.4.refs_0_), channel_id=1, source_target_pairs={{0,24},{8,0},{16,8},{24,16},{1,25},{9,1},{17,9},{25,17},{2,26},{10... | collective-permute-start | bytes 393224 | tf_op jit(solution)/shard_map/ppermute | solution.py:473
  88.8 16.8 %collective-permute-start.23 = (f32[32,1024]{1,0:T(8,128)S(1)}, f32[32,1024]{1,0:T(8,128)S(1)}, u32[]{:S(2)}, u32[]{:S(2)}) collective-permute-start(f32[32,1024]{1,0:T(8,128)S(1)} %passed.4.refs_0_), channel_id=1, source_target_pairs={{0,16},{8,24},{16,0},{24,8},{1,17},{9,25},{17,1},{25,9},{2,18},{10... | collective-permute-start | bytes 393224 | tf_op jit(solution)/shard_map/ppermute | solution.py:473
  90.1 15.5 %collective-permute-start.22 = (f32[32,1024]{1,0:T(8,128)S(1)}, f32[32,1024]{1,0:T(8,128)S(1)}, u32[]{:S(2)}, u32[]{:S(2)}) collective-permute-start(f32[32,1024]{1,0:T(8,128)S(1)} %passed.4.refs_0_), channel_id=1, source_target_pairs={{0,8},{8,16},{16,24},{24,0},{1,9},{9,17},{17,25},{25,1},{2,10},{10... | collective-permute-start | bytes 393224 | tf_op jit(solution)/shard_map/ppermute | solution.py:473
  105.6 1.4 %collective-permute-start.31 = (f32[32,1024]{1,0:T(8,128)S(1)}, f32[32,1024]{1,0:T(8,128)S(1)}, u32[]{:S(2)}, u32[]{:S(2)}) collective-permute-start(f32[32,1024]{1,0:T(8,128)S(1)} %get-tuple-element.40.refs_8_), channel_id=1, source_target_pairs={{0,1},{1,0},{2,3},{3,2},{4,5},{5,4},{6,7},{7,6},{8,9},{9,8},{10,11... | collective-permute-start | bytes 393224 | tf_op jit(solution)/shard_map/ppermute | solution.py:532
  105.7 1.5 %collective-permute-start.32 = (f32[32,1024]{1,0:T(8,128)S(1)}, f32[32,1024]{1,0:T(8,128)S(1)}, u32[]{:S(2)}, u32[]{:S(2)}) collective-permute-start(f32[32,1024]{1,0:T(8,128)S(1)} %get-tuple-element.41.refs_9_), channel_id=1, source_target_pairs={{0,1},{1,0},{2,3},{3,2},{4,5},{5,4},{6,7},{7,6},{8,9},{9,8},{10,11... | collective-permute-start | bytes 393224 | tf_op jit(solution)/shard_map/ppermute | solution.py:532
  106.2 1.3 %collective-permute-start.33 = (f32[32,1024]{1,0:T(8,128)S(1)}, f32[32,1024]{1,0:T(8,128)S(1)}, u32[]{:S(2)}, u32[]{:S(2)}) collective-permute-start(f32[32,1024]{1,0:T(8,128)S(1)} %get-tuple-element.42.refs_10_), channel_id=1, source_target_pairs={{0,1},{1,0},{2,3},{3,2},{4,5},{5,4},{6,7},{7,6},{8,9},{9,8},{10,11... | collective-permute-start | bytes 393224 | tf_op jit(solution)/shard_map/ppermute | solution.py:532
  106.2 1.5 %collective-permute-start.34 = (f32[32,1024]{1,0:T(8,128)S(1)}, f32[32,1024]{1,0:T(8,128)S(1)}, u32[]{:S(2)}, u32[]{:S(2)}) collective-permute-start(f32[32,1024]{1,0:T(8,128)S(1)} %get-tuple-element.43.refs_11_), channel_id=1, source_target_pairs={{0,1},{1,0},{2,3},{3,2},{4,5},{5,4},{6,7},{7,6},{8,9},{9,8},{10,11... | collective-permute-start | bytes 393224 | tf_op jit(solution)/shard_map/ppermute | solution.py:532

commit v3 on v2

--- a/solution.py
+++ b/solution.py
@@ -36,7 +36,7 @@
 GAUSS_NORM = 1.0 / math.sqrt(2.0 * math.pi)
 MIB = 1024 * 1024
 VMEM_LIMIT = 8 * MIB
-UPDATE_VMEM = 12 * MIB
+UPDATE_VMEM = 8 * MIB
 
 TAIL_SCALE = 0.32
 TAIL = (
@@ -175,9 +175,8 @@
     return jnp.concatenate([both, jnp.zeros((LANES - NODES, both.shape[1]), F32)], axis=0)
 
 
-def x_faces(pressure, velocity, up_ref, down_ref, row):
-    up_ref[row : row + 32] = pltpu.roll(pressure + velocity, 28, 0)[:32]
-    down_ref[row : row + 32] = (velocity - pressure)[:32]
+def x_faces(pressure, velocity):
+    return pltpu.roll(pressure + velocity, 28, 0)[:32], (velocity - pressure)[:32]
 
 
 def grid_values(to_grid, pressure):
@@ -220,21 +219,20 @@
     return [r - sink * q for r, q in zip([rate] + velocity_rates, fields)]
 
 
-def first_stage(state_ref, mask_ref, damping_ref, slopes_ref, faces_ref, mid_ref, up_ref, down_ref):
+def first_stage(state_ref, mask_ref, damping_ref, slopes_ref, faces_ref, mid_ref):
     fields = [read_field(state_ref, f) for f in range(4)]
     sink = mask_ref[...].astype(F32) * damping_ref[...]
     rate = local_rates(fields, sink, slopes_ref[...], faces_ref[...])
     mid = [q + TIME_STEP * r for q, r in zip(fields, rate)]
     for f in range(4):
         mid_ref[f] = mid[f]
-    x_faces(fields[0], fields[1], up_ref, down_ref, 0)
-    x_faces(mid[0], mid[1], up_ref, down_ref, 32)
-
-
-def lift_kernel(me_ref, *refs):
-    del me_ref
+    messages = zip(x_faces(fields[0], fields[1]), x_faces(mid[0], mid[1]))
+    return [jnp.concatenate(stages, axis=0) for stages in messages]
+
+
+def lift_kernel(joined, me_ref, *refs):
     n = (len(refs) - 5) // 2
-    given, (out_ref, mid_ref, up_ref, down_ref) = refs[:n], refs[n : n + 4]
+    given, (out_ref, mid_ref, first_ref, second_ref) = refs[:n], refs[n : n + 4]
     held, sems = refs[n + 4 : -1], refs[-1]
     state_ref, gain_ref, to_grid_ref, table_ref = held[:4]
     copies = [pltpu.make_async_copy(a, b, sems.at[k]) for k, (a, b) in enumerate(zip(given, held))]
@@ -261,26 +259,42 @@
             total = total + jnp.dot(
                 lifted, table_ref[j * cells : (j + 1) * cells, :], preferred_element_type=F32
             )
-        out_ref[pair] = total[:channels]
-        out_ref[pair + 1] = total[channels:]
-    first_stage(state_ref, *held[4:], mid_ref, up_ref, down_ref)
+        for k in range(2):
+            for ref in (out_ref, first_ref, second_ref)[: 3 if joined else 1]:
+                ref[pair + k] = total[k * channels : (k + 1) * channels]
+    up, down = first_stage(state_ref, *held[4:], mid_ref)
+    if joined:
+        even = (me_ref[0] & 1) == 0
+        first_ref[PLANES] = jnp.where(even, up, down)
+        second_ref[PLANES] = jnp.where(even, down, up)
+    else:
+        first_ref[...] = up
+        second_ref[...] = down
 
 
 def second_stage_kernel(
-    state_ref, mid_ref, below_ref, above_ref, mask_ref, damping_ref, slopes_ref, faces_ref,
+    joined, me_ref, state_ref, mid_ref, first_ref, second_ref, mask_ref, damping_ref, slopes_ref, faces_ref,
     to_grid_ref, after_ref, new_ref, target_ref,
 ):
     del after_ref
+    if joined:
+        me = me_ref[0]
+        even = (me & 1) == 0
+        first, second = first_ref[PLANES], second_ref[PLANES]
+        below = jnp.where(me == 0, 0.0, jnp.where(even, second, first))
+        above = jnp.where(me == 3, 0.0, jnp.where(even, first, second))
+    else:
+        below, above = first_ref[...], second_ref[...]
     faces = faces_ref[...]
     mid = [mid_ref[f] for f in range(4)]
     parts = x_parts(
-        read_field(state_ref, 0), read_field(state_ref, 1), below_ref[:32], above_ref[:32], faces
+        read_field(state_ref, 0), read_field(state_ref, 1), below[:32], above[:32], faces
     )
     mid[0] = mid[0] + TIME_STEP * parts[0]
     mid[1] = mid[1] + TIME_STEP * parts[1]
     sink = mask_ref[...].astype(F32) * damping_ref[...]
     rate = local_rates(mid, sink, slopes_ref[...], faces)
-    parts = x_parts(mid[0], mid[1], below_ref[32:], above_ref[32:], faces)
+    parts = x_parts(mid[0], mid[1], below[32:], above[32:], faces)
     rate[0] = rate[0] + parts[0]
     rate[1] = rate[1] + parts[1]
     for f in range(4):
@@ -300,57 +314,40 @@
     return me // per, 1, pl.multiple_of(lax.rem(me, per) * modes, modes)
 
 
-def sum_over_x(me_ref, fx_ref, gathered, halves, *out_refs, factor=1.0):
+def sum_over_x(me_ref, fx_ref, gathered, *out_refs, factor=1.0):
     me = me_ref[0]
     rows, modes = out_refs[0].shape
-    first, count, offset = owned(me, modes)
+    first, functions, offset = owned(me, modes)
     width = min(modes, JOINT)
-    totals = [None] * count
+    totals = [None] * functions
     for slab, read in gathered(me):
-        for h in range(halves):
-            for k in range(PLANES // halves):
-                block = read(h, k, offset, width)
-                x = PLANES * slab + h * (PLANES // halves) + k
-                for i in range(count):
-                    term = fx_ref[first + i, x] * block
-                    totals[i] = term if totals[i] is None else totals[i] + term
-    for i in range(count):
+        for k in range(PLANES):
+            block = read(k, offset, width)
+            for i in range(functions):
+                term = fx_ref[first + i, PLANES * slab + k] * block
+                totals[i] = term if totals[i] is None else totals[i] + term
+    for i in range(functions):
+        total = totals[i] if factor == 1.0 else factor * totals[i]
         for k, out_ref in enumerate(out_refs):
-            out_ref[:, i * width : (i + 1) * width] = factor * totals[i][k * rows : (k + 1) * rows]
-
-
-def gathered_planes(refs, count, halves):
+            out_ref[:, i * width : (i + 1) * width] = total[k * rows : (k + 1) * rows]
+
+
+def gathered_planes(refs, count):
     def walk(me):
-        per = len(refs) // halves
-        if per == count:
-            for b in range(count):
-                slab = lax.rem(me + (count - b), count)
-
-                def read(h, k, offset, width, b=b):
-                    ref = refs[h * per + b]
-                    return ref[k] if offset is None else ref[k, :, pl.ds(offset, width)]
-
-                yield slab, read
-        else:
-            for b in range(count):
-
-                def read(h, k, offset, width, b=b):
-                    ref = refs[h]
-                    return ref[b, k] if offset is None else ref[b, k, :, pl.ds(offset, width)]
-
-                yield b, read
+        for b in range(count):
+            ref, slab = (refs[b], me ^ b) if len(refs) == count else (refs[0].at[b], b)
+
+            def read(k, offset, width, ref=ref):
+                return ref[k] if offset is None else ref[k, :, pl.ds(offset, width)]
+
+            yield slab, read
 
     return walk
 
 
-def count_of_parts(refs, halves, count):
-    return halves * count if refs[0].ndim == 3 else halves
-
-
-def mix_kernel(count, me_ref, fx_ref, *refs):
-    parts = refs[:-5]
-    spectral_ref, _, _, coeffs_ref, mixed_ref = refs[-5:]
-    sum_over_x(me_ref, fx_ref, gathered_planes(parts, count, 1), 1, coeffs_ref)
+def mix_kernel(count, n, me_ref, fx_ref, *refs):
+    spectral_ref, coeffs_ref, mixed_ref = refs[n], refs[-2], refs[-1]
+    sum_over_x(me_ref, fx_ref, gathered_planes(refs[:n], count), coeffs_ref)
     channels, modes = coeffs_ref.shape
 
     @pl.loop(0, modes // LANES)
@@ -362,76 +359,75 @@
         mixed_ref[:, at] = total.astype(BF16)
 
 
-def coeffs_kernel(count, halves, me_ref, fx_ref, *refs):
-    n = count_of_parts(refs, halves, count)
-    parts = gathered_planes(refs[:n], count, halves)
-    sum_over_x(me_ref, fx_ref, parts, halves, *refs[-UPDATE_CHUNKS:], factor=1.0 - BETA_ONE)
-
-
-def backward_kernel(count, half, me_ref, fx_ref, *refs):
-    parts = refs[:-8]
-    weight_ref, target_ref, forward_ref, table_ref = refs[-8:-4]
+def coeffs_kernel(count, n, me_ref, fx_ref, *refs):
+    parts = gathered_planes(refs[:n], count)
+    sum_over_x(me_ref, fx_ref, parts, *refs[-UPDATE_CHUNKS:], factor=1.0 - BETA_ONE)
+
+
+def backward_kernel(count, n, me_ref, fx_ref, *refs):
+    parts = refs[:n]
+    weight_ref, target_ref, forward_ref, table_ref = refs[n : n + 4]
     out_ref, along_ref = refs[-2:]
     me = me_ref[0]
-    planes, channels = out_ref.shape[:2]
+    channels = along_ref.shape[0] // PLANES
     modes = parts[0].shape[-1]
     width = min(modes, JOINT)
     along_ref[...] = jnp.zeros_like(along_ref)
     for b in range(count):
-        if len(parts) == count:
-            ref, slab = parts[b], lax.rem(me + (count - b), count)
-        else:
-            ref, slab = parts[0].at[b], b
+        ref, slab = (parts[b], me ^ b) if n == count else (parts[0].at[b], b)
         first, functions, offset = owned(slab, modes)
+        lanes = slice(None) if offset is None else pl.ds(offset, width)
         for i in range(functions):
             block = ref[:, i * width : (i + 1) * width].astype(F32)
-            for k in range(planes):
-                x = PLANES * me + half * planes + k
-                at = (pl.ds(k * channels, channels), slice(None) if offset is None else pl.ds(offset, width))
-                along_ref[at] += fx_ref[first + i, x] * block
-    along = along_ref[...]
-    high = along.astype(BF16)
-    rest = along - high.astype(F32)
-    middle = rest.astype(BF16)
-    low = (rest - middle.astype(F32)).astype(BF16)
-    thirds = jnp.concatenate([high, middle, low], axis=0)
+            for k in range(PLANES):
+                at = (pl.ds(k * channels, channels), lanes)
+                along_ref[at] += fx_ref[first + i, PLANES * me + k] * block
     weight = column_of(weight_ref[...])
-    rows = planes * channels
     cells = target_ref.shape[1]
-    total = jnp.zeros((rows, JOINT), F32)
-    for j in range(CELLS):
-        spread = jnp.dot(
-            thirds, forward_ref[:, j * cells : (j + 1) * cells], preferred_element_type=F32
-        )
-        parts_of = []
-        for k in range(planes):
-            r = k * channels
-            pre = (
-                spread[2 * rows + r : 2 * rows + r + channels]
-                + spread[rows + r : rows + r + channels]
-            ) + spread[r : r + channels]
-            phi, bell = normal_parts(pre)
-            predicted = jnp.sum(pre * phi * weight, axis=0, keepdims=True)
-            at = (half * planes + k) * CELLS + j
-            misfit = 2.0 * LOSS_SCALE * (predicted - target_ref[at : at + 1, :])
-            slope = phi + pre * bell * GAUSS_NORM
-            parts_of.append((misfit * weight * slope).astype(BF16))
-        total = total + jnp.dot(
-            jnp.concatenate(parts_of, axis=0),
-            table_ref[j * cells : (j + 1) * cells, :],
-            preferred_element_type=F32,
-        )
-    for k in range(planes):
-        out_ref[k] = total[k * channels : (k + 1) * channels]
-
-
-def update_kernel(chunk, tiles, *refs):
-    coeffs, grads = refs[:tiles], refs[tiles : 2 * tiles]
-    spectral_ref, one_ref, two_ref = refs[2 * tiles : 2 * tiles + 3]
+    rows = 2 * channels
+    for pair in range(0, PLANES, 2):
+        along = along_ref[pair * channels : pair * channels + rows]
+        high = along.astype(BF16)
+        rest = along - high.astype(F32)
+        middle = rest.astype(BF16)
+        low = (rest - middle.astype(F32)).astype(BF16)
+        thirds = jnp.concatenate([high, middle, low], axis=0)
+        total = jnp.zeros((rows, JOINT), F32)
+        for j in range(CELLS):
+            spread = jnp.dot(
+                thirds, forward_ref[:, j * cells : (j + 1) * cells], preferred_element_type=F32
+            )
+            grads = []
+            for k in range(2):
+                r = k * channels
+                pre = (
+                    spread[2 * rows + r : 2 * rows + r + channels]
+                    + spread[rows + r : rows + r + channels]
+                ) + spread[r : r + channels]
+                phi, bell = normal_parts(pre)
+                predicted = jnp.sum(pre * phi * weight, axis=0, keepdims=True)
+                at = (pair + k) * CELLS + j
+                misfit = 2.0 * LOSS_SCALE * (predicted - target_ref[at : at + 1, :])
+                slope = phi + pre * bell * GAUSS_NORM
+                grads.append((misfit * weight * slope).astype(BF16))
+            total = total + jnp.dot(
+                jnp.concatenate(grads, axis=0),
+                table_ref[j * cells : (j + 1) * cells, :],
+                preferred_element_type=F32,
+            )
+        for k in range(2):
+            out_ref[pair + k] = total[k * channels : (k + 1) * channels]
+
+
+def update_kernel(chunk, tiles, parts, *refs):
+    coeffs, given = refs[:tiles], refs[tiles : tiles + parts]
+    spectral_ref, moments_ref = refs[tiles + parts : tiles + parts + 2]
     new_ref, new_one_ref, new_two_ref, done_ref, rows_ref = refs[-5:]
     block, width, modes = new_ref.shape
+    grads = [g.at[pl.ds(r, width)] for g in given for r in range(0, g.shape[0], width)]
     root = math.sqrt(BIAS_TWO)
     start = pl.program_id(0) * block
+    channels = spectral_ref.shape[0]
     done_ref[...] = jnp.zeros_like(done_ref)
 
     @pl.loop(0, modes // LANES)
@@ -452,9 +448,12 @@
                     halves.append(part)
                 gradient = jnp.concatenate(halves, axis=0)
                 at_o = slice(o, o + 16)
-                given = (start + c, slice(chunk * width + o, chunk * width + o + 16), at)
-                first = BETA_ONE * one_ref[c, at_o, at].astype(F32) + gradient
-                second = BETA_TWO * two_ref[c, at_o, at].astype(F32) + (
+                across = (slice(chunk * width + o, chunk * width + o + 16), at)
+                given = (start + c, *across)
+                one = moments_ref[given].astype(F32)
+                two = moments_ref[(channels + start + c, *across)].astype(F32)
+                first = BETA_ONE * one + gradient
+                second = BETA_TWO * two + (
                     (1.0 - BETA_TWO) / (1.0 - BETA_ONE) ** 2
                 ) * (gradient * gradient)
                 denominator = second * lax.rsqrt(second) + EPSILON * root
@@ -465,26 +464,35 @@
                 new_two_ref[c, at_o, at] = second.astype(BF16)
 
 
-def from_ring(array, axis):
+def pairs_fit(count):
+    return count in (2, 4, 8)
+
+
+def from_all(array, axis):
     count = lax.axis_size(axis)
-    if count > 8:
+    if not pairs_fit(count):
         return [lax.all_gather(array, axis)]
-    return [array] + [
-        lax.ppermute(array, axis, [(i, (i + b) % count) for i in range(count)])
-        for b in range(1, count)
-    ]
+    return [array] + [exchanged(array, axis, b) for b in range(1, count)]
+
+
+def exchanged(array, axis, b):
+    return lax.ppermute(array, axis, [(i, i ^ b) for i in range(lax.axis_size(axis))])
 
 
 def load_kernel(n, *refs):
-    given, held, sems = refs[:n], refs[n + 1 : 2 * n + 1], refs[-1]
+    given, held_ref, sems = refs[:n], refs[n + 1], refs[-1]
     pieces = sems.shape[1]
+    rows = given[0].shape[0]
+    step = rows // pieces
     copies = []
     for k in range(n):
-        step = given[k].shape[0] // pieces
         for p in range(pieces):
-            at = pl.ds(p * step, step)
             copies.append(
-                pltpu.make_async_copy(given[k].at[at], held[k].at[at], sems.at[k, p])
+                pltpu.make_async_copy(
+                    given[k].at[pl.ds(p * step, step)],
+                    held_ref.at[pl.ds(k * rows + p * step, step)],
+                    sems.at[k, p],
+                )
             )
     for copy in copies:
         copy.start()
@@ -492,17 +500,17 @@
         copy.wait()
 
 
-def loaded(arrays, after, limit):
-    n = len(arrays)
-    held = [pltpu.VMEM(a.shape, a.dtype) for a in arrays]
+def loaded(arrays, after):
+    n, shape = len(arrays), arrays[0].shape
+    size = sum(a.size * a.dtype.itemsize for a in arrays)
     return pl.pallas_call(
         functools.partial(load_kernel, n),
         in_specs=[ANY_SPEC] * (n + 1),
-        out_specs=[VMEM_SPEC] * n,
-        out_shape=held,
+        out_specs=VMEM_SPEC,
+        out_shape=pltpu.VMEM((n * shape[0],) + shape[1:], arrays[0].dtype),
         scratch_shapes=[pltpu.SemaphoreType.DMA((n, 4))],
-        compiler_params=params(limit),
-        cost_estimate=SMALL_COST,
+        compiler_params=params(),
+        cost_estimate=pl.CostEstimate(flops=0, bytes_accessed=2 * size, transcendentals=0),
         name="load",
     )(*[in_hbm(a) for a in arrays], after)
 
@@ -511,26 +519,23 @@
     del refs
 
 
-def passed_after(arrays, after):
+def passed_after(arrays, *after):
     n = len(arrays)
     return pl.pallas_call(
         passed_kernel,
-        in_specs=[ANY_SPEC] * (n + 1),
+        in_specs=[ANY_SPEC] * (n + len(after)),
         out_specs=[ANY_SPEC] * n,
         out_shape=[jax.ShapeDtypeStruct(a.shape, a.dtype) for a in arrays],
         input_output_aliases={k: k for k in range(n)},
-        compiler_params=params(VMEM_LIMIT),
+        compiler_params=params(),
         name="passed",
-    )(*arrays, after)
+    )(*arrays, *after)
 
 
 def of_every_core(behind):
-    count = lax.axis_size("gy")
     arrays = list(behind)
-    for b in range(1, count):
-        arrays += [
-            lax.ppermute(a, "gy", [(i, (i + b) % count) for i in range(count)]) for a in behind
-        ]
+    for b in range(1, lax.axis_size("gy")):
+        arrays += [exchanged(a, "gy", b) for a in behind]
     return arrays
 
 
@@ -541,7 +546,6 @@
     return below, above
 
 
-HALVES = 2
 MIX_BLOCK = 8
 UPDATE_BLOCK = 8
 UPDATE_CHUNKS = 2
@@ -554,7 +558,6 @@
     cells = state.shape[-1]
     channels = lift_gain.shape[0]
     modes = spectral.shape[0]
-    planes = PLANES // HALVES
     slopes, to_grid, faces = (jnp.asarray(t) for t in solver_tables())
     joint = joint_table()
     forward = jnp.asarray(joint)
@@ -567,15 +570,17 @@
     spectral_t, one_t, two_t = (
         jnp.transpose(a, (1, 2, 0)) for a in (spectral, moment_one, moment_two)
     )
-    faces_out = jax.ShapeDtypeStruct((64, cells), F32)
-    half_planes = jax.ShapeDtypeStruct((planes, channels, JOINT), F32)
 
     def shape_of(array):
         return jax.ShapeDtypeStruct(array.shape, array.dtype)
 
     given = (flat, gain_row, to_grid, table, absorb_mask, damping, slopes, faces)
-    lifted, mid, up, down = pl.pallas_call(
-        lift_kernel,
+    joined = count == 4
+    faces_out = jax.ShapeDtypeStruct((64, cells), F32)
+    if joined:
+        faces_out = jax.ShapeDtypeStruct((PLANES + 1, channels, JOINT), F32)
+    lifted, mid, first, second = pl.pallas_call(
+        functools.partial(lift_kernel, joined),
         in_specs=[SMEM_SPEC] + [ANY_SPEC] * len(given),
         out_specs=[VMEM_SPEC] * 4,
         out_shape=[
@@ -590,12 +595,18 @@
         cost_estimate=SMALL_COST,
         name="lift",
     )(me, *[in_hbm(a) for a in given])
-    gathered = from_ring(lifted, "gx")
-    (spectral_held,) = loaded([spectral_t], mid, VMEM_LIMIT)
-    below, above = from_sides(*passed_after([up, down], spectral_held))
+    if joined:
+        sent = [first, lifted, second]
+        gathered = [lifted] + [exchanged(a, "gx", b) for b, a in enumerate(sent, 1)]
+        first, second = gathered[1], gathered[3]
+    else:
+        gathered = from_all(lifted, "gx")
+        first, second = from_sides(first, second)
+    spectral_held = loaded([spectral_t], mid)
+
     coeffs, mixed = pl.pallas_call(
-        functools.partial(mix_kernel, count),
-        in_specs=[SMEM_SPEC, SMEM_SPEC] + [VMEM_SPEC] * (len(gathered) + 1) + [ANY_SPEC] * 2,
+        functools.partial(mix_kernel, count, len(gathered)),
+        in_specs=[SMEM_SPEC, SMEM_SPEC] + [VMEM_SPEC] * (len(gathered) + 1),
         out_specs=[VMEM_SPEC] * 2,
         out_shape=[
             jax.ShapeDtypeStruct((channels, modes), F32),
@@ -604,13 +615,13 @@
         compiler_params=params(),
         cost_estimate=SMALL_COST,
         name="mix",
-    )(me, fx, *gathered, in_vmem(spectral_held), below, above)
-    every_mixed = from_ring(mixed, "gx")
-    behind = from_ring(coeffs, "grp")
+    )(me, fx, *gathered, in_vmem(spectral_held))
+    every_mixed = from_all(mixed, "gx")
+    behind = from_all(coeffs, "grp")
 
     new_flat, target = pl.pallas_call(
-        second_stage_kernel,
-        in_specs=[VMEM_SPEC] * 9 + [ANY_SPEC],
+        functools.partial(second_stage_kernel, joined),
+        in_specs=[SMEM_SPEC] + [VMEM_SPEC] * 9 + [ANY_SPEC],
         out_specs=[VMEM_SPEC] * 2,
         out_shape=[
             shape_of(flat),
@@ -620,39 +631,36 @@
         cost_estimate=SMALL_COST,
         name="second_stage",
     )(
-        flat, mid, below, above, absorb_mask, damping, slopes, faces, to_grid, mixed,
+        me, flat, mid, first, second, absorb_mask, damping, slopes, faces, to_grid, mixed,
     )
 
-    gathered = []
-    back = mixed
-    for half in range(HALVES):
-        back = pl.pallas_call(
-            functools.partial(backward_kernel, count, half),
-            in_specs=[SMEM_SPEC, SMEM_SPEC] + [VMEM_SPEC] * (len(every_mixed) + 4) + [ANY_SPEC] * 2,
-            out_specs=VMEM_SPEC,
-            out_shape=half_planes,
-            scratch_shapes=[pltpu.VMEM((planes * channels, JOINT), F32)],
-            compiler_params=params(),
-            cost_estimate=SMALL_COST,
-            name=f"backward_{half}",
-        )(me, fx, *every_mixed, weight_row, target, forward, table, back, behind[half])
-        gathered.append(from_ring(back, "gx"))
-    flat_parts = [a for half in gathered for a in half]
     width = channels // UPDATE_CHUNKS
+    back = pl.pallas_call(
+        functools.partial(backward_kernel, count, len(every_mixed)),
+        in_specs=[SMEM_SPEC, SMEM_SPEC] + [VMEM_SPEC] * (len(every_mixed) + 4),
+        out_specs=VMEM_SPEC,
+        out_shape=jax.ShapeDtypeStruct((PLANES, channels, JOINT), F32),
+        scratch_shapes=[pltpu.VMEM((PLANES * channels, JOINT), F32)],
+        compiler_params=params(),
+        cost_estimate=SMALL_COST,
+        name="backward",
+    )(me, fx, *every_mixed, weight_row, target, forward, table)
+    gathered = from_all(back, "gx")
+    moments_held = in_vmem(loaded([one_t, two_t], back))
     grad_coeffs = pl.pallas_call(
-        functools.partial(coeffs_kernel, count, HALVES),
-        in_specs=[SMEM_SPEC, SMEM_SPEC] + [VMEM_SPEC] * len(flat_parts) + [ANY_SPEC] * len(behind),
+        functools.partial(coeffs_kernel, count, len(gathered)),
+        in_specs=[SMEM_SPEC, SMEM_SPEC] + [VMEM_SPEC] * len(gathered) + [ANY_SPEC] * (len(behind) + 1),
         out_specs=[VMEM_SPEC] * UPDATE_CHUNKS,
         out_shape=[jax.ShapeDtypeStruct((width, modes), F32)] * UPDATE_CHUNKS,
-        compiler_params=params(VMEM_LIMIT),
+        compiler_params=params(),
         cost_estimate=SMALL_COST,
         name="grad_coeffs",
-    )(me, fx, *flat_parts, *behind)
+    )(me, fx, *gathered, *behind, moments_held)
     every_coeffs = of_every_core(behind)
-
-    behind = [from_ring(grad_coeffs[0], "grp")]
+    behind = [from_all(grad_coeffs[0], "grp")]
     for chunk in range(1, UPDATE_CHUNKS):
-        behind.append(from_ring(passed_after([grad_coeffs[chunk]], behind[-1][-1])[0], "grp"))
+        (waiting,) = passed_after([grad_coeffs[chunk]], *behind[-1], moments_held)
+        behind.append(from_all(waiting, "grp"))
     tiles = len(every_coeffs)
     outs = None
     for chunk in range(UPDATE_CHUNKS):
@@ -661,16 +669,16 @@
         grads = of_every_core(behind[chunk])
         cube = pl.BlockSpec((UPDATE_BLOCK, width, modes), lambda i, chunk=chunk: (i, chunk, 0))
         given = [*every_coeffs, *grads]
-        given += [in_vmem(spectral_held), in_hbm(one_t), in_hbm(two_t)]
+        given += [in_vmem(spectral_held), moments_held]
         specs = [pl.BlockSpec((UPDATE_BLOCK, modes), lambda i: (i, 0))] * tiles
-        specs += [VMEM_SPEC] * (tiles + 1) + [cube] * 2
+        specs += [VMEM_SPEC] * (len(grads) + 2)
         aliases = {}
         if outs is not None:
             aliases = {len(given) + k: k for k in range(3)}
             given += [in_hbm(a) for a in outs[:3]]
             specs += [ANY_SPEC] * 3
         outs = pl.pallas_call(
-            functools.partial(update_kernel, chunk, tiles),
+            functools.partial(update_kernel, chunk, tiles, len(grads)),
             grid=(channels // UPDATE_BLOCK,),
             in_specs=specs,
             out_specs=[cube] * 3 + [pl.BlockSpec((8, LANES), lambda i: (0, 0))],

time: 124 us -> 111 us (0.90)
  starting transfers between devices: 44.4 us -> 22.9 us
  waiting for transfers between devices: 17.8 us -> 28 us
    ppermute x35 -> x30, starting transfers between devices: 44.4 us -> 22.9 us  [exchanged(): lax.ppermute(array, axis, [(i, i ^ b) for i in range(lax.axis_size(axis))])]
    ppermute x35 -> x30, waiting for transfers between devices: 17.8 us -> 28 us  [exchanged(): lax.ppermute(array, axis, [(i, i ^ b) for i in range(lax.axis_size(axis))])]
    pallas_call x11 -> x9, Pallas kernels: 54.1 us -> 47.3 us  [the longest x2 25.2 us: per_device(): pl.pallas_call(functools.partial(update_kernel, chunk, tiles, len(grads))...]
    pallas_call x1 -> x2, Pallas kernels: 5.89 us -> 11.8 us  [loaded(): pl.pallas_call(functools.partial(load_kernel, n), in_specs=[ANY_SPEC] * (...]
  transfers between devices with their start and end apart: 35 -> 30, of which waited for: 9 -> 14; matrix products, arithmetic and copies ran while one was open for 0% -> 0% of each run, Pallas kernels for 27% -> 32%
where the time goes in v3:
time: 111 us
  Pallas kernels  59.1 us (53%)
  waiting for transfers between devices  28 us (25%)
  starting transfers between devices  22.9 us (21%)
    ppermute x30, waiting for transfers between devices, exchanged(): lax.ppermute(array, axis, [(i, i ^ b) for i in range(lax.axis_size(axis))])  28 us
    pallas_call x2, Pallas kernels, per_device(): pl.pallas_call(functools.partial(update_kernel, chunk, tiles, len(grads))...  25.2 us
    ppermute x30, starting transfers between devices, exchanged(): lax.ppermute(array, axis, [(i, i ^ b) for i in range(lax.axis_size(axis))])  22.9 us
    pallas_call x2, Pallas kernels, loaded(): pl.pallas_call(functools.partial(load_kernel, n), in_specs=[ANY_SPEC] * (...  11.8 us
    pallas_call x1, Pallas kernels, per_device(): pl.pallas_call(functools.partial(backward_kernel, count, len(every_mixed)...  8.03 us
    pallas_call x1, Pallas kernels, per_device(): pl.pallas_call(functools.partial(lift_kernel, joined), in_specs=[SMEM_SPE...  7.25 us
    pallas_call x1, Pallas kernels, per_device(): pl.pallas_call(functools.partial(mix_kernel, count, len(gathered)), in_sp...  3.99 us
  transfers between devices with their start and end apart: 30, of which 14 were waited for; matrix products, arithmetic and copies ran while one was open for 0% of the time, Pallas kernels for 32%

profile of v3, /device:TPU:0, one launch (start us, length us, event | category | flops | bytes accessed | tf_op | source)
XLA Modules:
  0.0 111.1 jit_solution(13024601479763146818)
XLA Ops:
  0.6 7.3 %lift.1 = (f32[4,64,256]{2,1,0:T(8,128)S(1)}, f32[4,128,256]{2,1,0:T(8,128)S(1)}, f32[5,64,256]{2,1,0:T(8,128)S(1)}, f32[5,64,256]{2,1,0:T(8,128)S(1)}) custom-call(s32[1]{0:T(128)} %bitcast.me_ref, f32[1000,128]{1,0:T(8,128)} %bitcast.15, f32[1,64]{1,0:T(1,128)} %bitcast.24, f32[64,128]{1,0:T(8,128)} %constant.19.clone.refs_2_.to_grid_ref, ...), custom_call_target="tpu_custom_call" | custom-call | flops 1000 | bytes 1000 | tf_op jit(solution)/shard_map/lift/pallas_call | solution.py:582
  7.9 3.0 %collective-permute-start = (f32[5,64,256]{2,1,0:T(8,128)S(1)}, f32[5,64,256]{2,1,0:T(8,128)S(1)}, u32[]{:S(2)}, u32[]{:S(2)}) collective-permute-start(f32[5,64,256]{2,1,0:T(8,128)S(1)} %get-tuple-element.26), channel_id=1, source_target_pairs={{0,2},{2,0},{4,6},{6,4},{1,3},{3,1},{5,7},{7,5},{8,10},{10,8},{12,... | collective-permute-start | bytes 983048 | tf_op jit(solution)/shard_map/ppermute | solution.py:479
  10.9 1.5 %collective-permute-start.1 = (f32[5,64,256]{2,1,0:T(8,128)S(1)}, f32[5,64,256]{2,1,0:T(8,128)S(1)}, u32[]{:S(2)}, u32[]{:S(2)}) collective-permute-start(f32[5,64,256]{2,1,0:T(8,128)S(1)} %get-tuple-element.27), channel_id=1, source_target_pairs={{0,6},{2,4},{4,2},{6,0},{1,7},{3,5},{5,3},{7,1},{8,14},{10,12},{12... | collective-permute-start | bytes 983048 | tf_op jit(solution)/shard_map/ppermute | solution.py:479
  12.4 0.1 collective-permute-start.2
  12.4 5.9 %load.2.refs_4_.refs_16_ = f32[64,64,1024]{2,1,0:T(8,128)S(1)} custom-call(f32[64,64,1024]{2,1,0:T(8,128)} %bitcast.18, f32[4,128,256]{2,1,0:T(8,128)S(1)} %get-tuple-element.25.refs_1_.mid_ref), custom_call_target="tpu_custom_call" | custom-call | bytes 33554432 | tf_op jit(solution)/shard_map/load/pallas_call | solution.py:506
  18.4 0.0 copy-start.5
  18.4 0.0 copy-start.6
  18.4 0.0 copy-start.1
  18.5 2.6 %collective-permute-done.2.refs_2_ = f32[4,64,256]{2,1,0:T(8,128)S(1)} collective-permute-done((f32[4,64,256]{2,1,0:T(8,128)S(1)}, f32[4,64,256]{2,1,0:T(8,128)S(1)}, u32[]{:S(2)}, u32[]{:S(2)}) %collective-permute-start.2) | collective-permute-done | bytes 262176 | tf_op jit(solution)/shard_map/ppermute | solution.py:479
  21.0 5.9 %collective-permute-done.1.refs_3_.second_ref = f32[5,64,256]{2,1,0:T(8,128)S(1)} collective-permute-done((f32[5,64,256]{2,1,0:T(8,128)S(1)}, f32[5,64,256]{2,1,0:T(8,128)S(1)}, u32[]{:S(2)}, u32[]{:S(2)}) %collective-permute-start.1) | collective-permute-done | bytes 327712 | tf_op jit(solution)/shard_map/ppermute | solution.py:479
  26.9 4.0 %mix.1 = (f32[64,1024]{1,0:T(8,128)S(1)}, bf16[64,1024]{1,0:T(8,128)(2,1)S(1)}) custom-call(s32[1]{0:T(128)} %bitcast.me_ref, f32[16,16]{1,0:T(8,128)S(1)} %copy-done.7, f32[4,64,256]{2,1,0:T(8,128)S(1)} %get-tuple-element.28.refs_0_, f32[5,64,256]{2,1,0:T(8,128)S(1)} %collective-permute-done.refs_1_.first_ref, ...), custom_call_target="tpu_custom_call" | custom-call | flops 1000 | bytes 1000 | tf_op jit(solution)/shard_map/mix/pallas_call | solution.py:607
  30.9 3.7 %collective-permute-start.5 = (f32[64,1024]{1,0:T(8,128)S(1)}, f32[64,1024]{1,0:T(8,128)S(1)}, u32[]{:S(2)}, u32[]{:S(2)}) collective-permute-start(f32[64,1024]{1,0:T(8,128)S(1)} %get-tuple-element.31.refs_4_.refs_0_), channel_id=1, source_target_pairs={{0,24},{8,16},{16,8},{24,0},{1,25},{9,17},{17,9},{25,1},{2,26},{10... | collective-permute-start | bytes 786440 | tf_op jit(solution)/shard_map/ppermute | solution.py:479
  34.6 1.4 %collective-permute-start.12 = (bf16[64,1024]{1,0:T(8,128)(2,1)S(1)}, bf16[64,1024]{1,0:T(8,128)(2,1)S(1)}, u32[]{:S(2)}, u32[]{:S(2)}) collective-permute-start(bf16[64,1024]{1,0:T(8,128)(2,1)S(1)} %get-tuple-element.29.after_ref.refs_0_), channel_id=1, source_target_pairs={{0,6},{2,4},{4,2},{6,0},{1,7},{3,5},{5,3},{7,1},{8,14},{10,12},{12... | collective-permute-start | bytes 393224 | tf_op jit(solution)/shard_map/ppermute | solution.py:479
  36.0 1.5 %collective-permute-start.11 = (bf16[64,1024]{1,0:T(8,128)(2,1)S(1)}, bf16[64,1024]{1,0:T(8,128)(2,1)S(1)}, u32[]{:S(2)}, u32[]{:S(2)}) collective-permute-start(bf16[64,1024]{1,0:T(8,128)(2,1)S(1)} %get-tuple-element.29.after_ref.refs_0_), channel_id=1, source_target_pairs={{0,4},{2,6},{4,0},{6,2},{1,5},{3,7},{5,1},{7,3},{8,12},{10,14},{12... | collective-permute-start | bytes 393224 | tf_op jit(solution)/shard_map/ppermute | solution.py:479
  37.5 0.5 collective-permute-start.10
  38.1 1.8 %second_stage.1 = (f32[1000,128]{1,0:T(8,128)}, f32[64,256]{1,0:T(8,128)S(1)}) custom-call(s32[1]{0:T(128)} %bitcast.me_ref, f32[1000,128]{1,0:T(8,128)S(1)} %bitcast.16, f32[4,128,256]{2,1,0:T(8,128)S(1)} %get-tuple-element.25.refs_1_.mid_ref, f32[5,64,256]{2,1,0:T(8,128)S(1)} %collective-permute-done.refs_1_.first_ref, ...), custom_call_target="tpu_custom_call" | custom-call | flops 1000 | bytes 1000 | tf_op jit(solution)/shard_map/second_stage/pallas_call | solution.py:622
  39.9 1.1 collective-permute-done.12.refs_3_
  41.0 1.3 %collective-permute-done.11.refs_2_ = bf16[64,1024]{1,0:T(8,128)(2,1)S(1)} collective-permute-done((bf16[64,1024]{1,0:T(8,128)(2,1)S(1)}, bf16[64,1024]{1,0:T(8,128)(2,1)S(1)}, u32[]{:S(2)}, u32[]{:S(2)}) %collective-permute-start.11) | collective-permute-done | bytes 131104 | tf_op jit(solution)/shard_map/ppermute | solution.py:479
  42.3 0.2 collective-permute-done.10.refs_1_
  42.5 8.0 %backward.1.refs_2_.refs_0_ = f32[4,64,256]{2,1,0:T(8,128)S(1)} custom-call(s32[1]{0:T(128)} %bitcast.me_ref, f32[16,16]{1,0:T(8,128)S(1)} %copy-done.7, bf16[64,1024]{1,0:T(8,128)(2,1)S(1)} %get-tuple-element.29.after_ref.refs_0_, bf16[64,1024]{1,0:T(8,128)(2,1)S(1)} %collective-permute-done.10.refs_1_, ...), custom_call_target="tpu_custom_call" | custom-call | flops 1000 | bytes 1000 | tf_op jit(solution)/shard_map/backward/pallas_call | solution.py:638
  50.5 1.4 %collective-permute-start.15 = (f32[4,64,256]{2,1,0:T(8,128)S(1)}, f32[4,64,256]{2,1,0:T(8,128)S(1)}, u32[]{:S(2)}, u32[]{:S(2)}) collective-permute-start(f32[4,64,256]{2,1,0:T(8,128)S(1)} %backward.1.refs_2_.refs_0_), channel_id=1, source_target_pairs={{0,6},{2,4},{4,2},{6,0},{1,7},{3,5},{5,3},{7,1},{8,14},{10,12},{12... | collective-permute-start | bytes 786440 | tf_op jit(solution)/shard_map/ppermute | solution.py:479
  52.0 0.7 collective-permute-start.14
  52.7 1.4 %collective-permute-start.13 = (f32[4,64,256]{2,1,0:T(8,128)S(1)}, f32[4,64,256]{2,1,0:T(8,128)S(1)}, u32[]{:S(2)}, u32[]{:S(2)}) collective-permute-start(f32[4,64,256]{2,1,0:T(8,128)S(1)} %backward.1.refs_2_.refs_0_), channel_id=1, source_target_pairs={{0,2},{2,0},{4,6},{6,4},{1,3},{3,1},{5,7},{7,5},{8,10},{10,8},{12,... | collective-permute-start | bytes 786440 | tf_op jit(solution)/shard_map/ppermute | solution.py:479
  54.1 1.9 %collective-permute-done.4.refs_6_.refs_2_ = f32[64,1024]{1,0:T(8,128)S(1)} collective-permute-done((f32[64,1024]{1,0:T(8,128)S(1)}, f32[64,1024]{1,0:T(8,128)S(1)}, u32[]{:S(2)}, u32[]{:S(2)}) %collective-permute-start.4) | collective-permute-done | bytes 262176 | tf_op jit(solution)/shard_map/ppermute | solution.py:479
  56.0 5.9 %load.3.refs_8_.refs_5_.refs_17_ = bf16[128,64,1024]{2,1,0:T(8,128)(2,1)S(1)} custom-call(bf16[64,64,1024]{2,1,0:T(8,128)(2,1)} %bitcast.22, bf16[64,64,1024]{2,1,0:T(8,128)(2,1)} %bitcast.23, f32[4,64,256]{2,1,0:T(8,128)S(1)} %backward.1.refs_2_.refs_0_), custom_call_target="tpu_custom_call" | custom-call | bytes 33554432 | tf_op jit(solution)/shard_map/load/pallas_call | solution.py:506
  61.9 1.7 %collective-permute-done.14.refs_2_ = f32[4,64,256]{2,1,0:T(8,128)S(1)} collective-permute-done((f32[4,64,256]{2,1,0:T(8,128)S(1)}, f32[4,64,256]{2,1,0:T(8,128)S(1)}, u32[]{:S(2)}, u32[]{:S(2)}) %collective-permute-start.14) | collective-permute-done | bytes 262176 | tf_op jit(solution)/shard_map/ppermute | solution.py:479
  63.7 1.0 grad_coeffs.1
  64.6 0.9 collective-permute-start.18
  65.6 0.2 collective-permute-start.9
  65.7 0.4 collective-permute-start.8
  66.1 0.2 collective-permute-start.7
  66.2 6.5 %collective-permute-done.18.refs_4_.refs_11_ = f32[32,1024]{1,0:T(8,128)S(1)} collective-permute-done((f32[32,1024]{1,0:T(8,128)S(1)}, f32[32,1024]{1,0:T(8,128)S(1)}, u32[]{:S(2)}, u32[]{:S(2)}) %collective-permute-start.18) | collective-permute-done | bytes 131104 | tf_op jit(solution)/shard_map/ppermute | solution.py:479
  72.7 4.5 %collective-permute-done.17.refs_3_.refs_10_ = f32[32,1024]{1,0:T(8,128)S(1)} collective-permute-done((f32[32,1024]{1,0:T(8,128)S(1)}, f32[32,1024]{1,0:T(8,128)S(1)}, u32[]{:S(2)}, u32[]{:S(2)}) %collective-permute-start.17) | collective-permute-done | bytes 131104 | tf_op jit(solution)/shard_map/ppermute | solution.py:479
  77.2 1.3 %collective-permute-done.16.refs_2_.refs_9_ = f32[32,1024]{1,0:T(8,128)S(1)} collective-permute-done((f32[32,1024]{1,0:T(8,128)S(1)}, f32[32,1024]{1,0:T(8,128)S(1)}, u32[]{:S(2)}, u32[]{:S(2)}) %collective-permute-start.16) | collective-permute-done | bytes 131104 | tf_op jit(solution)/shard_map/ppermute | solution.py:479
  78.6 2.5 %collective-permute-start.21 = (f32[32,1024]{1,0:T(8,128)S(1)}, f32[32,1024]{1,0:T(8,128)S(1)}, u32[]{:S(2)}, u32[]{:S(2)}) collective-permute-start(f32[32,1024]{1,0:T(8,128)S(1)} %passed.2.refs_0_), channel_id=1, source_target_pairs={{0,24},{8,16},{16,8},{24,0},{1,25},{9,17},{17,9},{25,1},{2,26},{10... | collective-permute-start | bytes 393224 | tf_op jit(solution)/shard_map/ppermute | solution.py:479
  81.1 0.2 collective-permute-start.24
  81.3 0.3 collective-permute-start.23
  81.6 2.0 %collective-permute-start.19 = (f32[32,1024]{1,0:T(8,128)S(1)}, f32[32,1024]{1,0:T(8,128)S(1)}, u32[]{:S(2)}, u32[]{:S(2)}) collective-permute-start(f32[32,1024]{1,0:T(8,128)S(1)} %passed.2.refs_0_), channel_id=1, source_target_pairs={{0,8},{8,0},{16,24},{24,16},{1,9},{9,1},{17,25},{25,17},{2,10},{10... | collective-permute-start | bytes 393224 | tf_op jit(solution)/shard_map/ppermute | solution.py:479
  83.6 12.6 %update_0.1 = (f32[64,64,1024]{2,1,0:T(8,128)}, bf16[64,64,1024]{2,1,0:T(8,128)(2,1)}, bf16[64,64,1024]{2,1,0:T(8,128)(2,1)}, f32[8,128]{1,0:T(8,128)S(1)}) custom-call(f32[64,1024]{1,0:T(8,128)S(1)} %get-tuple-element.31.refs_4_.refs_0_, f32[64,1024]{1,0:T(8,128)S(1)} %collective-permute-done.3.refs_5_.refs_1_, ...), custom_call_target="tpu_custom_call" | custom-call | flops 1000 | bytes 1000 | tf_op jit(solution)/shard_map/update_0/pallas_call | solution.py:680
  96.2 0.1 collective-permute-start.26
  96.3 0.5 collective-permute-start.27
  96.8 0.1 collective-permute-start.28
  96.9 0.4 collective-permute-start.29
  97.3 0.3 collective-permute-done.26.refs_12_
  97.6 0.2 collective-permute-done.27.refs_13_
  97.8 0.3 collective-permute-done.28.refs_14_
  98.2 0.2 collective-permute-done.29.refs_15_
  98.4 12.6 %update_1.1 = (f32[64,64,1024]{2,1,0:T(8,128)}, bf16[64,64,1024]{2,1,0:T(8,128)(2,1)}, bf16[64,64,1024]{2,1,0:T(8,128)(2,1)}, f32[8,128]{1,0:T(8,128)}) custom-call(f32[64,1024]{1,0:T(8,128)S(1)} %get-tuple-element.31.refs_4_.refs_0_, ...), custom_call_target="tpu_custom_call", output_to_operand_aliasing={{0}: (18, {}), {1}: (19, {}), {2}: (20, {})} | custom-call | flops 1000 | bytes 1000 | tf_op jit(solution)/shard_map/update_1/pallas_call | solution.py:680
  (63 shorter events, 0.2 us)
Async XLA Ops:
  7.9 13.1 %collective-permute-start = (f32[5,64,256]{2,1,0:T(8,128)S(1)}, f32[5,64,256]{2,1,0:T(8,128)S(1)}, u32[]{:S(2)}, u32[]{:S(2)}) collective-permute-start(f32[5,64,256]{2,1,0:T(8,128)S(1)} %get-tuple-element.26), channel_id=1, source_target_pairs={{0,2},{2,0},{4,6},{6,4},{1,3},{3,1},{5,7},{7,5},{8,10},{10,8},{12,... | collective-permute-start | bytes 983048 | tf_op jit(solution)/shard_map/ppermute | solution.py:479
  10.9 16.0 %collective-permute-start.1 = (f32[5,64,256]{2,1,0:T(8,128)S(1)}, f32[5,64,256]{2,1,0:T(8,128)S(1)}, u32[]{:S(2)}, u32[]{:S(2)}) collective-permute-start(f32[5,64,256]{2,1,0:T(8,128)S(1)} %get-tuple-element.27), channel_id=1, source_target_pairs={{0,6},{2,4},{4,2},{6,0},{1,7},{3,5},{5,3},{7,1},{8,14},{10,12},{12... | collective-permute-start | bytes 983048 | tf_op jit(solution)/shard_map/ppermute | solution.py:479
  12.4 8.6 %collective-permute-start.2 = (f32[4,64,256]{2,1,0:T(8,128)S(1)}, f32[4,64,256]{2,1,0:T(8,128)S(1)}, u32[]{:S(2)}, u32[]{:S(2)}) collective-permute-start(f32[4,64,256]{2,1,0:T(8,128)S(1)} %get-tuple-element.28.refs_0_), channel_id=1, source_target_pairs={{0,4},{2,6},{4,0},{6,2},{1,5},{3,7},{5,1},{7,3},{8,12},{10,14},{12... | collective-permute-start | bytes 786440 | tf_op jit(solution)/shard_map/ppermute | solution.py:479
  12.4 14.5 %copy-start.7 = (f32[16,16]{1,0:T(8,128)S(1)}, f32[16,16]{1,0:T(8,128)}, u32[]{:S(2)}) copy-start(f32[16,16]{1,0:T(8,128)} %constant.23.clone.fx_ref) | copy-start | bytes 3076
  18.3 12.5 %copy-start = (f32[64,64,1024]{2,1,0:T(8,128)}, f32[64,64,1024]{2,1,0:T(8,128)S(1)}, u32[]{:S(2)}) copy-start(f32[64,64,1024]{2,1,0:T(8,128)S(1)} %load.2.refs_4_.refs_16_) | copy-start | bytes 50331652
  18.4 19.7 %copy-start.3 = (f32[1,4,125,1,256]{4,3,2,1,0:T(1,128)S(1)}, f32[1,4,125,1,256]{4,3,2,1,0:T(1,128)}, u32[]{:S(2)}) copy-start(f32[1,4,125,1,256]{4,3,2,1,0:T(1,128)} %param.14) | copy-start | bytes 1536004
  18.4 19.7 %copy-start.4 = (f32[384,128]{1,0:T(8,128)S(1)}, f32[384,128]{1,0:T(8,128)}, u32[]{:S(2)}) copy-start(f32[384,128]{1,0:T(8,128)} %constant.18.clone.refs_6_.slopes_ref) | copy-start | bytes 589828
  18.4 19.7 %copy-start.5 = (f32[128,128]{1,0:T(8,128)S(1)}, f32[128,128]{1,0:T(8,128)}, u32[]{:S(2)}) copy-start(f32[128,128]{1,0:T(8,128)} %constant.20.clone.refs_7_.faces_ref) | copy-start | bytes 196612
  18.4 19.7 %copy-start.6 = (f32[64,128]{1,0:T(8,128)S(1)}, f32[64,128]{1,0:T(8,128)}, u32[]{:S(2)}) copy-start(f32[64,128]{1,0:T(8,128)} %constant.19.clone.refs_2_.to_grid_ref) | copy-start | bytes 98308
  18.4 19.7 %copy-start.8 = (s32[1,256]{1,0:T(1,128)S(1)}, s32[1,256]{1,0:T(1,128)}, u32[]{:S(2)}) copy-start(s32[1,256]{1,0:T(1,128)} %mask_ref.1) | copy-start | bytes 3076
  18.4 19.7 %copy-start.9 = (f32[1,256]{1,0:T(1,128)S(1)}, f32[1,256]{1,0:T(1,128)}, u32[]{:S(2)}) copy-start(f32[1,256]{1,0:T(1,128)} %damping_ref.1) | copy-start | bytes 3076
  18.4 24.1 %copy-start.1 = (bf16[4096,256]{1,0:T(8,128)(2,1)S(1)}, bf16[4096,256]{1,0:T(8,128)(2,1)}, u32[]{:S(2)}) copy-start(bf16[4096,256]{1,0:T(8,128)(2,1)} %constant.22.clone.refs_3_.refs_7_) | copy-start | bytes 6291460
  18.4 24.1 %copy-start.2 = (bf16[256,4096]{1,0:T(8,128)(2,1)S(1)}, bf16[256,4096]{1,0:T(8,128)(2,1)}, u32[]{:S(2)}) copy-start(bf16[256,4096]{1,0:T(8,128)(2,1)} %constant.21.clone.refs_6_) | copy-start | bytes 6291460
  18.5 24.0 %copy-start.10 = (f32[64]{0:T(128)S(1)}, f32[64]{0:T(128)}, u32[]{:S(2)}) copy-start(f32[64]{0:T(128)} %param.18) | copy-start | bytes 772
  30.9 21.8 %collective-permute-start.5 = (f32[64,1024]{1,0:T(8,128)S(1)}, f32[64,1024]{1,0:T(8,128)S(1)}, u32[]{:S(2)}, u32[]{:S(2)}) collective-permute-start(f32[64,1024]{1,0:T(8,128)S(1)} %get-tuple-element.31.refs_4_.refs_0_), channel_id=1, source_target_pairs={{0,24},{8,16},{16,8},{24,0},{1,25},{9,17},{17,9},{25,1},{2,26},{10... | collective-permute-start | bytes 786440 | tf_op jit(solution)/shard_map/ppermute | solution.py:479
  34.6 6.4 %collective-permute-start.12 = (bf16[64,1024]{1,0:T(8,128)(2,1)S(1)}, bf16[64,1024]{1,0:T(8,128)(2,1)S(1)}, u32[]{:S(2)}, u32[]{:S(2)}) collective-permute-start(bf16[64,1024]{1,0:T(8,128)(2,1)S(1)} %get-tuple-element.29.after_ref.refs_0_), channel_id=1, source_target_pairs={{0,6},{2,4},{4,2},{6,0},{1,7},{3,5},{5,3},{7,1},{8,14},{10,12},{12... | collective-permute-start | bytes 393224 | tf_op jit(solution)/shard_map/ppermute | solution.py:479
  36.0 6.3 %collective-permute-start.11 = (bf16[64,1024]{1,0:T(8,128)(2,1)S(1)}, bf16[64,1024]{1,0:T(8,128)(2,1)S(1)}, u32[]{:S(2)}, u32[]{:S(2)}) collective-permute-start(bf16[64,1024]{1,0:T(8,128)(2,1)S(1)} %get-tuple-element.29.after_ref.refs_0_), channel_id=1, source_target_pairs={{0,4},{2,6},{4,0},{6,2},{1,5},{3,7},{5,1},{7,3},{8,12},{10,14},{12... | collective-permute-start | bytes 393224 | tf_op jit(solution)/shard_map/ppermute | solution.py:479
  37.5 5.0 %collective-permute-start.10 = (bf16[64,1024]{1,0:T(8,128)(2,1)S(1)}, bf16[64,1024]{1,0:T(8,128)(2,1)S(1)}, u32[]{:S(2)}, u32[]{:S(2)}) collective-permute-start(bf16[64,1024]{1,0:T(8,128)(2,1)S(1)} %get-tuple-element.29.after_ref.refs_0_), channel_id=1, source_target_pairs={{0,2},{2,0},{4,6},{6,4},{1,3},{3,1},{5,7},{7,5},{8,10},{10,8},{12,... | collective-permute-start | bytes 393224 | tf_op jit(solution)/shard_map/ppermute | solution.py:479
  38.1 17.9 %collective-permute-start.4 = (f32[64,1024]{1,0:T(8,128)S(1)}, f32[64,1024]{1,0:T(8,128)S(1)}, u32[]{:S(2)}, u32[]{:S(2)}) collective-permute-start(f32[64,1024]{1,0:T(8,128)S(1)} %get-tuple-element.31.refs_4_.refs_0_), channel_id=1, source_target_pairs={{0,16},{8,24},{16,0},{24,8},{1,17},{9,25},{17,1},{25,9},{2,18},{10... | collective-permute-start | bytes 786440 | tf_op jit(solution)/shard_map/ppermute | solution.py:479
  41.0 20.9 %collective-permute-start.3 = (f32[64,1024]{1,0:T(8,128)S(1)}, f32[64,1024]{1,0:T(8,128)S(1)}, u32[]{:S(2)}, u32[]{:S(2)}) collective-permute-start(f32[64,1024]{1,0:T(8,128)S(1)} %get-tuple-element.31.refs_4_.refs_0_), channel_id=1, source_target_pairs={{0,8},{8,0},{16,24},{24,16},{1,9},{9,1},{17,25},{25,17},{2,10},{10... | collective-permute-start | bytes 786440 | tf_op jit(solution)/shard_map/ppermute | solution.py:479
  50.5 11.4 %collective-permute-start.15 = (f32[4,64,256]{2,1,0:T(8,128)S(1)}, f32[4,64,256]{2,1,0:T(8,128)S(1)}, u32[]{:S(2)}, u32[]{:S(2)}) collective-permute-start(f32[4,64,256]{2,1,0:T(8,128)S(1)} %backward.1.refs_2_.refs_0_), channel_id=1, source_target_pairs={{0,6},{2,4},{4,2},{6,0},{1,7},{3,5},{5,3},{7,1},{8,14},{10,12},{12... | collective-permute-start | bytes 786440 | tf_op jit(solution)/shard_map/ppermute | solution.py:479
  52.0 11.7 %collective-permute-start.14 = (f32[4,64,256]{2,1,0:T(8,128)S(1)}, f32[4,64,256]{2,1,0:T(8,128)S(1)}, u32[]{:S(2)}, u32[]{:S(2)}) collective-permute-start(f32[4,64,256]{2,1,0:T(8,128)S(1)} %backward.1.refs_2_.refs_0_), channel_id=1, source_target_pairs={{0,4},{2,6},{4,0},{6,2},{1,5},{3,7},{5,1},{7,3},{8,12},{10,14},{12... | collective-permute-start | bytes 786440 | tf_op jit(solution)/shard_map/ppermute | solution.py:479
  52.7 11.0 %collective-permute-start.13 = (f32[4,64,256]{2,1,0:T(8,128)S(1)}, f32[4,64,256]{2,1,0:T(8,128)S(1)}, u32[]{:S(2)}, u32[]{:S(2)}) collective-permute-start(f32[4,64,256]{2,1,0:T(8,128)S(1)} %backward.1.refs_2_.refs_0_), channel_id=1, source_target_pairs={{0,2},{2,0},{4,6},{6,4},{1,3},{3,1},{5,7},{7,5},{8,10},{10,8},{12,... | collective-permute-start | bytes 786440 | tf_op jit(solution)/shard_map/ppermute | solution.py:479
  56.0 10.3 %collective-permute-start.6 = (f32[64,1024]{1,0:T(8,128)S(1)}, f32[64,1024]{1,0:T(8,128)S(1)}, u32[]{:S(2)}, u32[]{:S(2)}) collective-permute-start(f32[64,1024]{1,0:T(8,128)S(1)} %get-tuple-element.31.refs_4_.refs_0_), channel_id=1, source_target_pairs={{0,1},{1,0},{2,3},{3,2},{4,5},{5,4},{6,7},{7,6},{8,9},{9,8},{10,11... | collective-permute-start | bytes 786440 | tf_op jit(solution)/shard_map/ppermute | solution.py:479
  63.7 19.9 %slice-start = ((s8[16777216]{0:T(1024)(128)(4,1)}), s8[4194304]{0:T(1024)(128)(4,1)S(1)}, s32[]{:S(2)}) async-start(s8[16777216]{0:T(1024)(128)(4,1)} %bitcast.11), calls=%async_computation | async-start | bytes 8388608
  63.7 19.9 %slice-start.1 = ((s8[16777216]{0:T(1024)(128)(4,1)}), s8[4194304]{0:T(1024)(128)(4,1)S(1)}, s32[]{:S(2)}) async-start(s8[16777216]{0:T(1024)(128)(4,1)} %bitcast.11), calls=%async_computation.1 | async-start | bytes 8388608
  63.7 19.9 %slice-start.2 = ((s8[16777216]{0:T(1024)(128)(4,1)}), s8[4194304]{0:T(1024)(128)(4,1)S(1)}, s32[]{:S(2)}) async-start(s8[16777216]{0:T(1024)(128)(4,1)} %bitcast.11), calls=%async_computation.2 | async-start | bytes 8388608
  64.6 8.1 %collective-permute-start.18 = (f32[32,1024]{1,0:T(8,128)S(1)}, f32[32,1024]{1,0:T(8,128)S(1)}, u32[]{:S(2)}, u32[]{:S(2)}) collective-permute-start(f32[32,1024]{1,0:T(8,128)S(1)} %get-tuple-element.34.refs_1_.refs_8_), channel_id=1, source_target_pairs={{0,24},{8,16},{16,8},{24,0},{1,25},{9,17},{17,9},{25,1},{2,26},{10... | collective-permute-start | bytes 393224 | tf_op jit(solution)/shard_map/ppermute | solution.py:479
  65.6 13.0 %collective-permute-start.9 = (f32[64,1024]{1,0:T(8,128)S(1)}, f32[64,1024]{1,0:T(8,128)S(1)}, u32[]{:S(2)}, u32[]{:S(2)}) collective-permute-start(f32[64,1024]{1,0:T(8,128)S(1)} %collective-permute-done.5.refs_7_.refs_3_), channel_id=1, source_target_pairs={{0,1},{1,0},{2,3},{3,2},{4,5},{5,4},{6,7},{7,6},{8,9},{9,8},{10,11... | collective-permute-start | bytes 786440 | tf_op jit(solution)/shard_map/ppermute | solution.py:479
  65.7 15.4 %collective-permute-start.8 = (f32[64,1024]{1,0:T(8,128)S(1)}, f32[64,1024]{1,0:T(8,128)S(1)}, u32[]{:S(2)}, u32[]{:S(2)}) collective-permute-start(f32[64,1024]{1,0:T(8,128)S(1)} %collective-permute-done.4.refs_6_.refs_2_), channel_id=1, source_target_pairs={{0,1},{1,0},{2,3},{3,2},{4,5},{5,4},{6,7},{7,6},{8,9},{9,8},{10,11... | collective-permute-start | bytes 786440 | tf_op jit(solution)/shard_map/ppermute | solution.py:479
  66.1 15.2 %collective-permute-start.7 = (f32[64,1024]{1,0:T(8,128)S(1)}, f32[64,1024]{1,0:T(8,128)S(1)}, u32[]{:S(2)}, u32[]{:S(2)}) collective-permute-start(f32[64,1024]{1,0:T(8,128)S(1)} %collective-permute-done.3.refs_5_.refs_1_), channel_id=1, source_target_pairs={{0,1},{1,0},{2,3},{3,2},{4,5},{5,4},{6,7},{7,6},{8,9},{9,8},{10,11... | collective-permute-start | bytes 786440 | tf_op jit(solution)/shard_map/ppermute | solution.py:479
  66.2 11.0 %collective-permute-start.17 = (f32[32,1024]{1,0:T(8,128)S(1)}, f32[32,1024]{1,0:T(8,128)S(1)}, u32[]{:S(2)}, u32[]{:S(2)}) collective-permute-start(f32[32,1024]{1,0:T(8,128)S(1)} %get-tuple-element.34.refs_1_.refs_8_), channel_id=1, source_target_pairs={{0,16},{8,24},{16,0},{24,8},{1,17},{9,25},{17,1},{25,9},{2,18},{10... | collective-permute-start | bytes 393224 | tf_op jit(solution)/shard_map/ppermute | solution.py:479
  72.7 5.8 %collective-permute-start.16 = (f32[32,1024]{1,0:T(8,128)S(1)}, f32[32,1024]{1,0:T(8,128)S(1)}, u32[]{:S(2)}, u32[]{:S(2)}) collective-permute-start(f32[32,1024]{1,0:T(8,128)S(1)} %get-tuple-element.34.refs_1_.refs_8_), channel_id=1, source_target_pairs={{0,8},{8,0},{16,24},{24,16},{1,9},{9,1},{17,25},{25,17},{2,10},{10... | collective-permute-start | bytes 393224 | tf_op jit(solution)/shard_map/ppermute | solution.py:479
  77.2 4.4 %collective-permute-start.22 = (f32[32,1024]{1,0:T(8,128)S(1)}, f32[32,1024]{1,0:T(8,128)S(1)}, u32[]{:S(2)}, u32[]{:S(2)}) collective-permute-start(f32[32,1024]{1,0:T(8,128)S(1)} %get-tuple-element.34.refs_1_.refs_8_), channel_id=1, source_target_pairs={{0,1},{1,0},{2,3},{3,2},{4,5},{5,4},{6,7},{7,6},{8,9},{9,8},{10,11... | collective-permute-start | bytes 393224 | tf_op jit(solution)/shard_map/ppermute | solution.py:479
  78.5 3.1 %collective-permute-start.25 = (f32[32,1024]{1,0:T(8,128)S(1)}, f32[32,1024]{1,0:T(8,128)S(1)}, u32[]{:S(2)}, u32[]{:S(2)}) collective-permute-start(f32[32,1024]{1,0:T(8,128)S(1)} %collective-permute-done.18.refs_4_.refs_11_), channel_id=1, source_target_pairs={{0,1},{1,0},{2,3},{3,2},{4,5},{5,4},{6,7},{7,6},{8,9},{9,8},{10,11... | collective-permute-start | bytes 393224 | tf_op jit(solution)/shard_map/ppermute | solution.py:479
  78.5 19.8 %slice-start.4 = ((s8[16777216]{0:T(1024)(128)(4,1)}), s8[4194304]{0:T(1024)(128)(4,1)S(1)}, s32[]{:S(2)}) async-start(s8[16777216]{0:T(1024)(128)(4,1)} %bitcast.13), calls=%async_computation.4 | async-start | bytes 8388608
  78.6 19.8 %slice-start.5 = ((s8[16777216]{0:T(1024)(128)(4,1)}), s8[4194304]{0:T(1024)(128)(4,1)S(1)}, s32[]{:S(2)}) async-start(s8[16777216]{0:T(1024)(128)(4,1)} %bitcast.13), calls=%async_computation.5 | async-start | bytes 8388608
  78.6 19.8 %slice-start.6 = ((s8[16777216]{0:T(1024)(128)(4,1)}), s8[4194304]{0:T(1024)(128)(4,1)S(1)}, s32[]{:S(2)}) async-start(s8[16777216]{0:T(1024)(128)(4,1)} %bitcast.13), calls=%async_computation.6 | async-start | bytes 8388608
  78.6 19.8 %slice-start.7 = ((s8[16777216]{0:T(1024)(128)(4,1)}), s8[4194304]{0:T(1024)(128)(4,1)S(1)}, s32[]{:S(2)}) async-start(s8[16777216]{0:T(1024)(128)(4,1)} %bitcast.13), calls=%async_computation.7 | async-start | bytes 8388608
  78.6 17.6 %collective-permute-start.21 = (f32[32,1024]{1,0:T(8,128)S(1)}, f32[32,1024]{1,0:T(8,128)S(1)}, u32[]{:S(2)}, u32[]{:S(2)}) collective-permute-start(f32[32,1024]{1,0:T(8,128)S(1)} %passed.2.refs_0_), channel_id=1, source_target_pairs={{0,24},{8,16},{16,8},{24,0},{1,25},{9,17},{17,9},{25,1},{2,26},{10... | collective-permute-start | bytes 393224 | tf_op jit(solution)/shard_map/ppermute | solution.py:479
  81.1 2.5 %collective-permute-start.24 = (f32[32,1024]{1,0:T(8,128)S(1)}, f32[32,1024]{1,0:T(8,128)S(1)}, u32[]{:S(2)}, u32[]{:S(2)}) collective-permute-start(f32[32,1024]{1,0:T(8,128)S(1)} %collective-permute-done.17.refs_3_.refs_10_), channel_id=1, source_target_pairs={{0,1},{1,0},{2,3},{3,2},{4,5},{5,4},{6,7},{7,6},{8,9},{9,8},{10,11... | collective-permute-start | bytes 393224 | tf_op jit(solution)/shard_map/ppermute | solution.py:479
  81.3 2.3 %collective-permute-start.23 = (f32[32,1024]{1,0:T(8,128)S(1)}, f32[32,1024]{1,0:T(8,128)S(1)}, u32[]{:S(2)}, u32[]{:S(2)}) collective-permute-start(f32[32,1024]{1,0:T(8,128)S(1)} %collective-permute-done.16.refs_2_.refs_9_), channel_id=1, source_target_pairs={{0,1},{1,0},{2,3},{3,2},{4,5},{5,4},{6,7},{7,6},{8,9},{9,8},{10,11... | collective-permute-start | bytes 393224 | tf_op jit(solution)/shard_map/ppermute | solution.py:479
  81.6 14.6 %collective-permute-start.20 = (f32[32,1024]{1,0:T(8,128)S(1)}, f32[32,1024]{1,0:T(8,128)S(1)}, u32[]{:S(2)}, u32[]{:S(2)}) collective-permute-start(f32[32,1024]{1,0:T(8,128)S(1)} %passed.2.refs_0_), channel_id=1, source_target_pairs={{0,16},{8,24},{16,0},{24,8},{1,17},{9,25},{17,1},{25,9},{2,18},{10... | collective-permute-start | bytes 393224 | tf_op jit(solution)/shard_map/ppermute | solution.py:479
  81.6 14.6 %collective-permute-start.19 = (f32[32,1024]{1,0:T(8,128)S(1)}, f32[32,1024]{1,0:T(8,128)S(1)}, u32[]{:S(2)}, u32[]{:S(2)}) collective-permute-start(f32[32,1024]{1,0:T(8,128)S(1)} %passed.2.refs_0_), channel_id=1, source_target_pairs={{0,8},{8,0},{16,24},{24,16},{1,9},{9,1},{17,25},{25,17},{2,10},{10... | collective-permute-start | bytes 393224 | tf_op jit(solution)/shard_map/ppermute | solution.py:479
  96.2 1.4 %collective-permute-start.26 = (f32[32,1024]{1,0:T(8,128)S(1)}, f32[32,1024]{1,0:T(8,128)S(1)}, u32[]{:S(2)}, u32[]{:S(2)}) collective-permute-start(f32[32,1024]{1,0:T(8,128)S(1)} %get-tuple-element.36.refs_8_), channel_id=1, source_target_pairs={{0,1},{1,0},{2,3},{3,2},{4,5},{5,4},{6,7},{7,6},{8,9},{9,8},{10,11... | collective-permute-start | bytes 393224 | tf_op jit(solution)/shard_map/ppermute | solution.py:479
  96.3 1.5 %collective-permute-start.27 = (f32[32,1024]{1,0:T(8,128)S(1)}, f32[32,1024]{1,0:T(8,128)S(1)}, u32[]{:S(2)}, u32[]{:S(2)}) collective-permute-start(f32[32,1024]{1,0:T(8,128)S(1)} %get-tuple-element.37.refs_9_), channel_id=1, source_target_pairs={{0,1},{1,0},{2,3},{3,2},{4,5},{5,4},{6,7},{7,6},{8,9},{9,8},{10,11... | collective-permute-start | bytes 393224 | tf_op jit(solution)/shard_map/ppermute | solution.py:479
  96.8 1.3 %collective-permute-start.28 = (f32[32,1024]{1,0:T(8,128)S(1)}, f32[32,1024]{1,0:T(8,128)S(1)}, u32[]{:S(2)}, u32[]{:S(2)}) collective-permute-start(f32[32,1024]{1,0:T(8,128)S(1)} %get-tuple-element.38.refs_10_), channel_id=1, source_target_pairs={{0,1},{1,0},{2,3},{3,2},{4,5},{5,4},{6,7},{7,6},{8,9},{9,8},{10,11... | collective-permute-start | bytes 393224 | tf_op jit(solution)/shard_map/ppermute | solution.py:479
  96.9 1.5 %collective-permute-start.29 = (f32[32,1024]{1,0:T(8,128)S(1)}, f32[32,1024]{1,0:T(8,128)S(1)}, u32[]{:S(2)}, u32[]{:S(2)}) collective-permute-start(f32[32,1024]{1,0:T(8,128)S(1)} %get-tuple-element.39.refs_11_), channel_id=1, source_target_pairs={{0,1},{1,0},{2,3},{3,2},{4,5},{5,4},{6,7},{7,6},{8,9},{9,8},{10,11... | collective-permute-start | bytes 393224 | tf_op jit(solution)/shard_map/ppermute | solution.py:479
  (1 other events, 5.1 us)

commit v4 on v3

--- a/solution.py
+++ b/solution.py
@@ -316,7 +316,8 @@
 
 def sum_over_x(me_ref, fx_ref, gathered, *out_refs, factor=1.0):
     me = me_ref[0]
-    rows, modes = out_refs[0].shape
+    lanes = out_refs[0].shape[1]
+    modes = lanes * len(out_refs)
     first, functions, offset = owned(me, modes)
     width = min(modes, JOINT)
     totals = [None] * functions
@@ -328,8 +329,8 @@
                 totals[i] = term if totals[i] is None else totals[i] + term
     for i in range(functions):
         total = totals[i] if factor == 1.0 else factor * totals[i]
-        for k, out_ref in enumerate(out_refs):
-            out_ref[:, i * width : (i + 1) * width] = total[k * rows : (k + 1) * rows]
+        start = i * width % lanes
+        out_refs[i * width // lanes][:, start : start + width] = total
 
 
 def gathered_planes(refs, count):
@@ -359,9 +360,9 @@
         mixed_ref[:, at] = total.astype(BF16)
 
 
-def coeffs_kernel(count, n, me_ref, fx_ref, *refs):
+def coeffs_kernel(count, n, chunks, me_ref, fx_ref, *refs):
     parts = gathered_planes(refs[:n], count)
-    sum_over_x(me_ref, fx_ref, parts, *refs[-UPDATE_CHUNKS:], factor=1.0 - BETA_ONE)
+    sum_over_x(me_ref, fx_ref, parts, *refs[-chunks:], factor=1.0 - BETA_ONE)
 
 
 def backward_kernel(count, n, me_ref, fx_ref, *refs):
@@ -419,24 +420,23 @@
             out_ref[pair + k] = total[k * channels : (k + 1) * channels]
 
 
-def update_kernel(chunk, tiles, parts, *refs):
-    coeffs, given = refs[:tiles], refs[tiles : tiles + parts]
-    spectral_ref, moments_ref = refs[tiles + parts : tiles + parts + 2]
+def update_kernel(chunk, tiles, *refs):
+    coeffs, grads = refs[:tiles], refs[tiles : 2 * tiles]
+    spectral_ref, moments_ref = refs[2 * tiles : 2 * tiles + 2]
     new_ref, new_one_ref, new_two_ref, done_ref, rows_ref = refs[-5:]
-    block, width, modes = new_ref.shape
-    grads = [g.at[pl.ds(r, width)] for g in given for r in range(0, g.shape[0], width)]
+    block, channels, width = new_ref.shape
     root = math.sqrt(BIAS_TWO)
     start = pl.program_id(0) * block
-    channels = spectral_ref.shape[0]
     done_ref[...] = jnp.zeros_like(done_ref)
 
-    @pl.loop(0, modes // LANES)
+    @pl.loop(0, width // LANES)
     def _(tile):
         at = pl.ds(pl.multiple_of(tile * LANES, LANES), LANES)
+        held_at = pl.ds(pl.multiple_of(chunk * width + tile * LANES, LANES), LANES)
         for t in range(len(grads)):
             for c in range(block):
                 rows_ref[t, c] = jnp.broadcast_to(coeffs[t][c : c + 1, at], (8, LANES))
-        for o in range(0, width, 16):
+        for o in range(0, channels, 16):
             held = [[g[o + k : o + k + 8, at] for k in (0, 8)] for g in grads]
             for c in range(block):
                 rows = [rows_ref[t, c] for t in range(len(grads))]
@@ -448,7 +448,7 @@
                     halves.append(part)
                 gradient = jnp.concatenate(halves, axis=0)
                 at_o = slice(o, o + 16)
-                across = (slice(chunk * width + o, chunk * width + o + 16), at)
+                across = (at_o, held_at)
                 given = (start + c, *across)
                 one = moments_ref[given].astype(F32)
                 two = moments_ref[(channels + start + c, *across)].astype(F32)
@@ -634,7 +634,8 @@
         me, flat, mid, first, second, absorb_mask, damping, slopes, faces, to_grid, mixed,
     )
 
-    width = channels // UPDATE_CHUNKS
+    chunks = UPDATE_CHUNKS if modes % (UPDATE_CHUNKS * JOINT) == 0 else 1
+    width = modes // chunks
     back = pl.pallas_call(
         functools.partial(backward_kernel, count, len(every_mixed)),
         in_specs=[SMEM_SPEC, SMEM_SPEC] + [VMEM_SPEC] * (len(every_mixed) + 4),
@@ -648,29 +649,29 @@
     gathered = from_all(back, "gx")
     moments_held = in_vmem(loaded([one_t, two_t], back))
     grad_coeffs = pl.pallas_call(
-        functools.partial(coeffs_kernel, count, len(gathered)),
+        functools.partial(coeffs_kernel, count, len(gathered), chunks),
         in_specs=[SMEM_SPEC, SMEM_SPEC] + [VMEM_SPEC] * len(gathered) + [ANY_SPEC] * (len(behind) + 1),
-        out_specs=[VMEM_SPEC] * UPDATE_CHUNKS,
-        out_shape=[jax.ShapeDtypeStruct((width, modes), F32)] * UPDATE_CHUNKS,
+        out_specs=[VMEM_SPEC] * chunks,
+        out_shape=[jax.ShapeDtypeStruct((channels, width), F32)] * chunks,
         compiler_params=params(),
         cost_estimate=SMALL_COST,
         name="grad_coeffs",
     )(me, fx, *gathered, *behind, moments_held)
     every_coeffs = of_every_core(behind)
     behind = [from_all(grad_coeffs[0], "grp")]
-    for chunk in range(1, UPDATE_CHUNKS):
+    for chunk in range(1, chunks):
         (waiting,) = passed_after([grad_coeffs[chunk]], *behind[-1], moments_held)
         behind.append(from_all(waiting, "grp"))
     tiles = len(every_coeffs)
     outs = None
-    for chunk in range(UPDATE_CHUNKS):
+    for chunk in range(chunks):
         if outs is not None:
             behind[chunk] = passed_after(behind[chunk], outs[3])
         grads = of_every_core(behind[chunk])
-        cube = pl.BlockSpec((UPDATE_BLOCK, width, modes), lambda i, chunk=chunk: (i, chunk, 0))
+        cube = pl.BlockSpec((UPDATE_BLOCK, channels, width), lambda i, chunk=chunk: (i, 0, chunk))
         given = [*every_coeffs, *grads]
         given += [in_vmem(spectral_held), moments_held]
-        specs = [pl.BlockSpec((UPDATE_BLOCK, modes), lambda i: (i, 0))] * tiles
+        specs = [pl.BlockSpec((UPDATE_BLOCK, width), lambda i, chunk=chunk: (i, chunk))] * tiles
         specs += [VMEM_SPEC] * (len(grads) + 2)
         aliases = {}
         if outs is not None:
@@ -678,7 +679,7 @@
             given += [in_hbm(a) for a in outs[:3]]
             specs += [ANY_SPEC] * 3
         outs = pl.pallas_call(
-            functools.partial(update_kernel, chunk, tiles, len(grads)),
+            functools.partial(update_kernel, chunk, tiles),
             grid=(channels // UPDATE_BLOCK,),
             in_specs=specs,
             out_specs=[cube] * 3 + [pl.BlockSpec((8, LANES), lambda i: (0, 0))],

time: 111 us -> 110 us (level)
  Pallas kernels: 59.1 us -> 57.5 us
    pallas_call x3, Pallas kernels: 26.2 us -> 24.6 us  [the longest x2 23.7 us: per_device(): pl.pallas_call(functools.partial(update_kernel, chunk, tiles), grid=(chan...]
  transfers between devices with their start and end apart: 30 -> 30, of which waited for: 14 -> 14; matrix products, arithmetic and copies ran while one was open for 0% -> 0% of each run, Pallas kernels for 32% -> 31%
where the time goes in v4:
time: 110 us
  Pallas kernels  57.5 us (52%)
  waiting for transfers between devices  28 us (25%)
  starting transfers between devices  22.9 us (21%)
    ppermute x30, waiting for transfers between devices, exchanged(): lax.ppermute(array, axis, [(i, i ^ b) for i in range(lax.axis_size(axis))])  28 us
    pallas_call x2, Pallas kernels, per_device(): pl.pallas_call(functools.partial(update_kernel, chunk, tiles), grid=(chan...  23.7 us
    ppermute x30, starting transfers between devices, exchanged(): lax.ppermute(array, axis, [(i, i ^ b) for i in range(lax.axis_size(axis))])  22.9 us
    pallas_call x2, Pallas kernels, loaded(): pl.pallas_call(functools.partial(load_kernel, n), in_specs=[ANY_SPEC] * (...  11.8 us
    pallas_call x1, Pallas kernels, per_device(): pl.pallas_call(functools.partial(backward_kernel, count, len(every_mixed)...  8.03 us
    pallas_call x1, Pallas kernels, per_device(): pl.pallas_call(functools.partial(lift_kernel, joined), in_specs=[SMEM_SPE...  7.25 us
    pallas_call x1, Pallas kernels, per_device(): pl.pallas_call(functools.partial(mix_kernel, count, len(gathered)), in_sp...  3.99 us
  transfers between devices with their start and end apart: 30, of which 14 were waited for; matrix products, arithmetic and copies ran while one was open for 0% of the time, Pallas kernels for 31%

profile of v4, /device:TPU:0, one launch (start us, length us, event | category | flops | bytes accessed | tf_op | source)
XLA Modules:
  0.0 109.6 jit_solution(14852955249403220877)
XLA Ops:
  0.6 7.3 %lift.1 = (f32[4,64,256]{2,1,0:T(8,128)S(1)}, f32[4,128,256]{2,1,0:T(8,128)S(1)}, f32[5,64,256]{2,1,0:T(8,128)S(1)}, f32[5,64,256]{2,1,0:T(8,128)S(1)}) custom-call(s32[1]{0:T(128)} %bitcast.me_ref, f32[1000,128]{1,0:T(8,128)} %bitcast.15, f32[1,64]{1,0:T(1,128)} %bitcast.24, f32[64,128]{1,0:T(8,128)} %constant.19.clone.refs_2_.to_grid_ref, ...), custom_call_target="tpu_custom_call" | custom-call | flops 1000 | bytes 1000 | tf_op jit(solution)/shard_map/lift/pallas_call | solution.py:582
  7.9 3.0 %collective-permute-start = (f32[5,64,256]{2,1,0:T(8,128)S(1)}, f32[5,64,256]{2,1,0:T(8,128)S(1)}, u32[]{:S(2)}, u32[]{:S(2)}) collective-permute-start(f32[5,64,256]{2,1,0:T(8,128)S(1)} %get-tuple-element.26), channel_id=1, source_target_pairs={{0,2},{2,0},{4,6},{6,4},{1,3},{3,1},{5,7},{7,5},{8,10},{10,8},{12,... | collective-permute-start | bytes 983048 | tf_op jit(solution)/shard_map/ppermute | solution.py:479
  10.9 1.5 %collective-permute-start.1 = (f32[5,64,256]{2,1,0:T(8,128)S(1)}, f32[5,64,256]{2,1,0:T(8,128)S(1)}, u32[]{:S(2)}, u32[]{:S(2)}) collective-permute-start(f32[5,64,256]{2,1,0:T(8,128)S(1)} %get-tuple-element.27), channel_id=1, source_target_pairs={{0,6},{2,4},{4,2},{6,0},{1,7},{3,5},{5,3},{7,1},{8,14},{10,12},{12... | collective-permute-start | bytes 983048 | tf_op jit(solution)/shard_map/ppermute | solution.py:479
  12.4 0.1 collective-permute-start.2
  12.4 5.9 %load.2.refs_4_.refs_16_ = f32[64,64,1024]{2,1,0:T(8,128)S(1)} custom-call(f32[64,64,1024]{2,1,0:T(8,128)} %bitcast.18, f32[4,128,256]{2,1,0:T(8,128)S(1)} %get-tuple-element.25.refs_1_.mid_ref), custom_call_target="tpu_custom_call" | custom-call | bytes 33554432 | tf_op jit(solution)/shard_map/load/pallas_call | solution.py:506
  18.4 0.0 copy-start.5
  18.4 0.0 copy-start.6
  18.4 0.0 copy-start.1
  18.5 2.6 %collective-permute-done.2.refs_2_ = f32[4,64,256]{2,1,0:T(8,128)S(1)} collective-permute-done((f32[4,64,256]{2,1,0:T(8,128)S(1)}, f32[4,64,256]{2,1,0:T(8,128)S(1)}, u32[]{:S(2)}, u32[]{:S(2)}) %collective-permute-start.2) | collective-permute-done | bytes 262176 | tf_op jit(solution)/shard_map/ppermute | solution.py:479
  21.0 5.9 %collective-permute-done.1.refs_3_.second_ref = f32[5,64,256]{2,1,0:T(8,128)S(1)} collective-permute-done((f32[5,64,256]{2,1,0:T(8,128)S(1)}, f32[5,64,256]{2,1,0:T(8,128)S(1)}, u32[]{:S(2)}, u32[]{:S(2)}) %collective-permute-start.1) | collective-permute-done | bytes 327712 | tf_op jit(solution)/shard_map/ppermute | solution.py:479
  26.9 4.0 %mix.1 = (f32[64,1024]{1,0:T(8,128)S(1)}, bf16[64,1024]{1,0:T(8,128)(2,1)S(1)}) custom-call(s32[1]{0:T(128)} %bitcast.me_ref, f32[16,16]{1,0:T(8,128)S(1)} %copy-done.7, f32[4,64,256]{2,1,0:T(8,128)S(1)} %get-tuple-element.28.refs_0_, f32[5,64,256]{2,1,0:T(8,128)S(1)} %collective-permute-done.refs_1_.first_ref, ...), custom_call_target="tpu_custom_call" | custom-call | flops 1000 | bytes 1000 | tf_op jit(solution)/shard_map/mix/pallas_call | solution.py:607
  30.9 3.7 %collective-permute-start.5 = (f32[64,1024]{1,0:T(8,128)S(1)}, f32[64,1024]{1,0:T(8,128)S(1)}, u32[]{:S(2)}, u32[]{:S(2)}) collective-permute-start(f32[64,1024]{1,0:T(8,128)S(1)} %get-tuple-element.31.refs_4_.refs_0_), channel_id=1, source_target_pairs={{0,24},{8,16},{16,8},{24,0},{1,25},{9,17},{17,9},{25,1},{2,26},{10... | collective-permute-start | bytes 786440 | tf_op jit(solution)/shard_map/ppermute | solution.py:479
  34.6 1.4 %collective-permute-start.12 = (bf16[64,1024]{1,0:T(8,128)(2,1)S(1)}, bf16[64,1024]{1,0:T(8,128)(2,1)S(1)}, u32[]{:S(2)}, u32[]{:S(2)}) collective-permute-start(bf16[64,1024]{1,0:T(8,128)(2,1)S(1)} %get-tuple-element.29.after_ref.refs_0_), channel_id=1, source_target_pairs={{0,6},{2,4},{4,2},{6,0},{1,7},{3,5},{5,3},{7,1},{8,14},{10,12},{12... | collective-permute-start | bytes 393224 | tf_op jit(solution)/shard_map/ppermute | solution.py:479
  36.0 1.5 %collective-permute-start.11 = (bf16[64,1024]{1,0:T(8,128)(2,1)S(1)}, bf16[64,1024]{1,0:T(8,128)(2,1)S(1)}, u32[]{:S(2)}, u32[]{:S(2)}) collective-permute-start(bf16[64,1024]{1,0:T(8,128)(2,1)S(1)} %get-tuple-element.29.after_ref.refs_0_), channel_id=1, source_target_pairs={{0,4},{2,6},{4,0},{6,2},{1,5},{3,7},{5,1},{7,3},{8,12},{10,14},{12... | collective-permute-start | bytes 393224 | tf_op jit(solution)/shard_map/ppermute | solution.py:479
  37.5 0.5 collective-permute-start.10
  38.1 1.8 %second_stage.1 = (f32[1000,128]{1,0:T(8,128)}, f32[64,256]{1,0:T(8,128)S(1)}) custom-call(s32[1]{0:T(128)} %bitcast.me_ref, f32[1000,128]{1,0:T(8,128)S(1)} %bitcast.16, f32[4,128,256]{2,1,0:T(8,128)S(1)} %get-tuple-element.25.refs_1_.mid_ref, f32[5,64,256]{2,1,0:T(8,128)S(1)} %collective-permute-done.refs_1_.first_ref, ...), custom_call_target="tpu_custom_call" | custom-call | flops 1000 | bytes 1000 | tf_op jit(solution)/shard_map/second_stage/pallas_call | solution.py:622
  39.9 1.1 collective-permute-done.12.refs_3_
  41.0 1.3 %collective-permute-done.11.refs_2_ = bf16[64,1024]{1,0:T(8,128)(2,1)S(1)} collective-permute-done((bf16[64,1024]{1,0:T(8,128)(2,1)S(1)}, bf16[64,1024]{1,0:T(8,128)(2,1)S(1)}, u32[]{:S(2)}, u32[]{:S(2)}) %collective-permute-start.11) | collective-permute-done | bytes 131104 | tf_op jit(solution)/shard_map/ppermute | solution.py:479
  42.3 0.2 collective-permute-done.10.refs_1_
  42.5 8.0 %backward.1.refs_2_.refs_0_ = f32[4,64,256]{2,1,0:T(8,128)S(1)} custom-call(s32[1]{0:T(128)} %bitcast.me_ref, f32[16,16]{1,0:T(8,128)S(1)} %copy-done.7, bf16[64,1024]{1,0:T(8,128)(2,1)S(1)} %get-tuple-element.29.after_ref.refs_0_, bf16[64,1024]{1,0:T(8,128)(2,1)S(1)} %collective-permute-done.10.refs_1_, ...), custom_call_target="tpu_custom_call" | custom-call | flops 1000 | bytes 1000 | tf_op jit(solution)/shard_map/backward/pallas_call | solution.py:639
  50.5 1.4 %collective-permute-start.15 = (f32[4,64,256]{2,1,0:T(8,128)S(1)}, f32[4,64,256]{2,1,0:T(8,128)S(1)}, u32[]{:S(2)}, u32[]{:S(2)}) collective-permute-start(f32[4,64,256]{2,1,0:T(8,128)S(1)} %backward.1.refs_2_.refs_0_), channel_id=1, source_target_pairs={{0,6},{2,4},{4,2},{6,0},{1,7},{3,5},{5,3},{7,1},{8,14},{10,12},{12... | collective-permute-start | bytes 786440 | tf_op jit(solution)/shard_map/ppermute | solution.py:479
  52.0 0.7 collective-permute-start.14
  52.7 1.4 %collective-permute-start.13 = (f32[4,64,256]{2,1,0:T(8,128)S(1)}, f32[4,64,256]{2,1,0:T(8,128)S(1)}, u32[]{:S(2)}, u32[]{:S(2)}) collective-permute-start(f32[4,64,256]{2,1,0:T(8,128)S(1)} %backward.1.refs_2_.refs_0_), channel_id=1, source_target_pairs={{0,2},{2,0},{4,6},{6,4},{1,3},{3,1},{5,7},{7,5},{8,10},{10,8},{12,... | collective-permute-start | bytes 786440 | tf_op jit(solution)/shard_map/ppermute | solution.py:479
  54.1 1.9 %collective-permute-done.4.refs_6_.refs_2_ = f32[64,1024]{1,0:T(8,128)S(1)} collective-permute-done((f32[64,1024]{1,0:T(8,128)S(1)}, f32[64,1024]{1,0:T(8,128)S(1)}, u32[]{:S(2)}, u32[]{:S(2)}) %collective-permute-start.4) | collective-permute-done | bytes 262176 | tf_op jit(solution)/shard_map/ppermute | solution.py:479
  56.0 5.9 %load.3.refs_8_.refs_5_.refs_17_ = bf16[128,64,1024]{2,1,0:T(8,128)(2,1)S(1)} custom-call(bf16[64,64,1024]{2,1,0:T(8,128)(2,1)} %bitcast.22, bf16[64,64,1024]{2,1,0:T(8,128)(2,1)} %bitcast.23, f32[4,64,256]{2,1,0:T(8,128)S(1)} %backward.1.refs_2_.refs_0_), custom_call_target="tpu_custom_call" | custom-call | bytes 33554432 | tf_op jit(solution)/shard_map/load/pallas_call | solution.py:506
  61.9 1.7 %collective-permute-done.14.refs_2_ = f32[4,64,256]{2,1,0:T(8,128)S(1)} collective-permute-done((f32[4,64,256]{2,1,0:T(8,128)S(1)}, f32[4,64,256]{2,1,0:T(8,128)S(1)}, u32[]{:S(2)}, u32[]{:S(2)}) %collective-permute-start.14) | collective-permute-done | bytes 262176 | tf_op jit(solution)/shard_map/ppermute | solution.py:479
  63.7 1.0 grad_coeffs.1
  64.6 0.9 collective-permute-start.18
  65.6 0.2 collective-permute-start.9
  65.7 0.4 collective-permute-start.8
  66.1 0.2 collective-permute-start.7
  66.2 6.5 %collective-permute-done.18.refs_4_.refs_11_ = f32[64,512]{1,0:T(8,128)S(1)} collective-permute-done((f32[64,512]{1,0:T(8,128)S(1)}, f32[64,512]{1,0:T(8,128)S(1)}, u32[]{:S(2)}, u32[]{:S(2)}) %collective-permute-start.18) | collective-permute-done | bytes 131104 | tf_op jit(solution)/shard_map/ppermute | solution.py:479
  72.7 4.5 %collective-permute-done.17.refs_3_.refs_10_ = f32[64,512]{1,0:T(8,128)S(1)} collective-permute-done((f32[64,512]{1,0:T(8,128)S(1)}, f32[64,512]{1,0:T(8,128)S(1)}, u32[]{:S(2)}, u32[]{:S(2)}) %collective-permute-start.17) | collective-permute-done | bytes 131104 | tf_op jit(solution)/shard_map/ppermute | solution.py:479
  77.2 1.3 %collective-permute-done.16.refs_2_.refs_9_ = f32[64,512]{1,0:T(8,128)S(1)} collective-permute-done((f32[64,512]{1,0:T(8,128)S(1)}, f32[64,512]{1,0:T(8,128)S(1)}, u32[]{:S(2)}, u32[]{:S(2)}) %collective-permute-start.16) | collective-permute-done | bytes 131104 | tf_op jit(solution)/shard_map/ppermute | solution.py:479
  78.6 2.5 %collective-permute-start.21 = (f32[64,512]{1,0:T(8,128)S(1)}, f32[64,512]{1,0:T(8,128)S(1)}, u32[]{:S(2)}, u32[]{:S(2)}) collective-permute-start(f32[64,512]{1,0:T(8,128)S(1)} %passed.2.refs_0_), channel_id=1, source_target_pairs={{0,24},{8,16},{16,8},{24,0},{1,25},{9,17},{17,9},{25,1},{2,26},{10... | collective-permute-start | bytes 393224 | tf_op jit(solution)/shard_map/ppermute | solution.py:479
  81.1 0.2 collective-permute-start.24
  81.3 0.3 collective-permute-start.23
  81.6 2.0 %collective-permute-start.19 = (f32[64,512]{1,0:T(8,128)S(1)}, f32[64,512]{1,0:T(8,128)S(1)}, u32[]{:S(2)}, u32[]{:S(2)}) collective-permute-start(f32[64,512]{1,0:T(8,128)S(1)} %passed.2.refs_0_), channel_id=1, source_target_pairs={{0,8},{8,0},{16,24},{24,16},{1,9},{9,1},{17,25},{25,17},{2,10},{10... | collective-permute-start | bytes 393224 | tf_op jit(solution)/shard_map/ppermute | solution.py:479
  83.6 11.7 %update_0.1 = (f32[64,64,1024]{2,1,0:T(8,128)}, bf16[64,64,1024]{2,1,0:T(8,128)(2,1)}, bf16[64,64,1024]{2,1,0:T(8,128)(2,1)}, f32[8,128]{1,0:T(8,128)S(1)}) custom-call(f32[64,1024]{1,0:T(8,128)S(1)} %get-tuple-element.31.refs_4_.refs_0_, f32[64,1024]{1,0:T(8,128)S(1)} %collective-permute-done.3.refs_5_.refs_1_, ...), custom_call_target="tpu_custom_call" | custom-call | flops 1000 | bytes 1000 | tf_op jit(solution)/shard_map/update_0/pallas_call | solution.py:681
  95.4 0.1 collective-permute-start.26
  95.5 0.5 collective-permute-start.27
  96.0 0.1 collective-permute-start.28
  96.1 0.4 collective-permute-start.29
  96.5 0.3 collective-permute-done.26.refs_12_
  96.8 0.2 collective-permute-done.27.refs_13_
  97.0 0.3 collective-permute-done.28.refs_14_
  97.3 0.2 collective-permute-done.29.refs_15_
  97.5 11.9 %update_1.1 = (f32[64,64,1024]{2,1,0:T(8,128)}, bf16[64,64,1024]{2,1,0:T(8,128)(2,1)}, bf16[64,64,1024]{2,1,0:T(8,128)(2,1)}, f32[8,128]{1,0:T(8,128)}) custom-call(f32[64,1024]{1,0:T(8,128)S(1)} %get-tuple-element.31.refs_4_.refs_0_, ...), custom_call_target="tpu_custom_call", output_to_operand_aliasing={{0}: (18, {}), {1}: (19, {}), {2}: (20, {})} | custom-call | flops 1000 | bytes 1000 | tf_op jit(solution)/shard_map/update_1/pallas_call | solution.py:681
  (63 shorter events, 0.2 us)
Async XLA Ops:
  7.9 13.1 %collective-permute-start = (f32[5,64,256]{2,1,0:T(8,128)S(1)}, f32[5,64,256]{2,1,0:T(8,128)S(1)}, u32[]{:S(2)}, u32[]{:S(2)}) collective-permute-start(f32[5,64,256]{2,1,0:T(8,128)S(1)} %get-tuple-element.26), channel_id=1, source_target_pairs={{0,2},{2,0},{4,6},{6,4},{1,3},{3,1},{5,7},{7,5},{8,10},{10,8},{12,... | collective-permute-start | bytes 983048 | tf_op jit(solution)/shard_map/ppermute | solution.py:479
  10.9 16.0 %collective-permute-start.1 = (f32[5,64,256]{2,1,0:T(8,128)S(1)}, f32[5,64,256]{2,1,0:T(8,128)S(1)}, u32[]{:S(2)}, u32[]{:S(2)}) collective-permute-start(f32[5,64,256]{2,1,0:T(8,128)S(1)} %get-tuple-element.27), channel_id=1, source_target_pairs={{0,6},{2,4},{4,2},{6,0},{1,7},{3,5},{5,3},{7,1},{8,14},{10,12},{12... | collective-permute-start | bytes 983048 | tf_op jit(solution)/shard_map/ppermute | solution.py:479
  12.4 8.6 %collective-permute-start.2 = (f32[4,64,256]{2,1,0:T(8,128)S(1)}, f32[4,64,256]{2,1,0:T(8,128)S(1)}, u32[]{:S(2)}, u32[]{:S(2)}) collective-permute-start(f32[4,64,256]{2,1,0:T(8,128)S(1)} %get-tuple-element.28.refs_0_), channel_id=1, source_target_pairs={{0,4},{2,6},{4,0},{6,2},{1,5},{3,7},{5,1},{7,3},{8,12},{10,14},{12... | collective-permute-start | bytes 786440 | tf_op jit(solution)/shard_map/ppermute | solution.py:479
  12.4 14.5 %copy-start.7 = (f32[16,16]{1,0:T(8,128)S(1)}, f32[16,16]{1,0:T(8,128)}, u32[]{:S(2)}) copy-start(f32[16,16]{1,0:T(8,128)} %constant.23.clone.fx_ref) | copy-start | bytes 3076
  18.3 12.5 %copy-start = (f32[64,64,1024]{2,1,0:T(8,128)}, f32[64,64,1024]{2,1,0:T(8,128)S(1)}, u32[]{:S(2)}) copy-start(f32[64,64,1024]{2,1,0:T(8,128)S(1)} %load.2.refs_4_.refs_16_) | copy-start | bytes 50331652
  18.4 19.7 %copy-start.3 = (f32[1,4,125,1,256]{4,3,2,1,0:T(1,128)S(1)}, f32[1,4,125,1,256]{4,3,2,1,0:T(1,128)}, u32[]{:S(2)}) copy-start(f32[1,4,125,1,256]{4,3,2,1,0:T(1,128)} %param.14) | copy-start | bytes 1536004
  18.4 19.7 %copy-start.4 = (f32[384,128]{1,0:T(8,128)S(1)}, f32[384,128]{1,0:T(8,128)}, u32[]{:S(2)}) copy-start(f32[384,128]{1,0:T(8,128)} %constant.18.clone.refs_6_.slopes_ref) | copy-start | bytes 589828
  18.4 19.7 %copy-start.5 = (f32[128,128]{1,0:T(8,128)S(1)}, f32[128,128]{1,0:T(8,128)}, u32[]{:S(2)}) copy-start(f32[128,128]{1,0:T(8,128)} %constant.20.clone.refs_7_.faces_ref) | copy-start | bytes 196612
  18.4 19.7 %copy-start.6 = (f32[64,128]{1,0:T(8,128)S(1)}, f32[64,128]{1,0:T(8,128)}, u32[]{:S(2)}) copy-start(f32[64,128]{1,0:T(8,128)} %constant.19.clone.refs_2_.to_grid_ref) | copy-start | bytes 98308
  18.4 19.7 %copy-start.8 = (s32[1,256]{1,0:T(1,128)S(1)}, s32[1,256]{1,0:T(1,128)}, u32[]{:S(2)}) copy-start(s32[1,256]{1,0:T(1,128)} %mask_ref.1) | copy-start | bytes 3076
  18.4 19.7 %copy-start.9 = (f32[1,256]{1,0:T(1,128)S(1)}, f32[1,256]{1,0:T(1,128)}, u32[]{:S(2)}) copy-start(f32[1,256]{1,0:T(1,128)} %damping_ref.1) | copy-start | bytes 3076
  18.4 24.1 %copy-start.1 = (bf16[4096,256]{1,0:T(8,128)(2,1)S(1)}, bf16[4096,256]{1,0:T(8,128)(2,1)}, u32[]{:S(2)}) copy-start(bf16[4096,256]{1,0:T(8,128)(2,1)} %constant.22.clone.refs_3_.refs_7_) | copy-start | bytes 6291460
  18.4 24.1 %copy-start.2 = (bf16[256,4096]{1,0:T(8,128)(2,1)S(1)}, bf16[256,4096]{1,0:T(8,128)(2,1)}, u32[]{:S(2)}) copy-start(bf16[256,4096]{1,0:T(8,128)(2,1)} %constant.21.clone.refs_6_) | copy-start | bytes 6291460
  18.5 24.0 %copy-start.10 = (f32[64]{0:T(128)S(1)}, f32[64]{0:T(128)}, u32[]{:S(2)}) copy-start(f32[64]{0:T(128)} %param.18) | copy-start | bytes 772
  30.9 21.8 %collective-permute-start.5 = (f32[64,1024]{1,0:T(8,128)S(1)}, f32[64,1024]{1,0:T(8,128)S(1)}, u32[]{:S(2)}, u32[]{:S(2)}) collective-permute-start(f32[64,1024]{1,0:T(8,128)S(1)} %get-tuple-element.31.refs_4_.refs_0_), channel_id=1, source_target_pairs={{0,24},{8,16},{16,8},{24,0},{1,25},{9,17},{17,9},{25,1},{2,26},{10... | collective-permute-start | bytes 786440 | tf_op jit(solution)/shard_map/ppermute | solution.py:479
  34.6 6.4 %collective-permute-start.12 = (bf16[64,1024]{1,0:T(8,128)(2,1)S(1)}, bf16[64,1024]{1,0:T(8,128)(2,1)S(1)}, u32[]{:S(2)}, u32[]{:S(2)}) collective-permute-start(bf16[64,1024]{1,0:T(8,128)(2,1)S(1)} %get-tuple-element.29.after_ref.refs_0_), channel_id=1, source_target_pairs={{0,6},{2,4},{4,2},{6,0},{1,7},{3,5},{5,3},{7,1},{8,14},{10,12},{12... | collective-permute-start | bytes 393224 | tf_op jit(solution)/shard_map/ppermute | solution.py:479
  36.0 6.3 %collective-permute-start.11 = (bf16[64,1024]{1,0:T(8,128)(2,1)S(1)}, bf16[64,1024]{1,0:T(8,128)(2,1)S(1)}, u32[]{:S(2)}, u32[]{:S(2)}) collective-permute-start(bf16[64,1024]{1,0:T(8,128)(2,1)S(1)} %get-tuple-element.29.after_ref.refs_0_), channel_id=1, source_target_pairs={{0,4},{2,6},{4,0},{6,2},{1,5},{3,7},{5,1},{7,3},{8,12},{10,14},{12... | collective-permute-start | bytes 393224 | tf_op jit(solution)/shard_map/ppermute | solution.py:479
  37.5 5.0 %collective-permute-start.10 = (bf16[64,1024]{1,0:T(8,128)(2,1)S(1)}, bf16[64,1024]{1,0:T(8,128)(2,1)S(1)}, u32[]{:S(2)}, u32[]{:S(2)}) collective-permute-start(bf16[64,1024]{1,0:T(8,128)(2,1)S(1)} %get-tuple-element.29.after_ref.refs_0_), channel_id=1, source_target_pairs={{0,2},{2,0},{4,6},{6,4},{1,3},{3,1},{5,7},{7,5},{8,10},{10,8},{12,... | collective-permute-start | bytes 393224 | tf_op jit(solution)/shard_map/ppermute | solution.py:479
  38.1 17.9 %collective-permute-start.4 = (f32[64,1024]{1,0:T(8,128)S(1)}, f32[64,1024]{1,0:T(8,128)S(1)}, u32[]{:S(2)}, u32[]{:S(2)}) collective-permute-start(f32[64,1024]{1,0:T(8,128)S(1)} %get-tuple-element.31.refs_4_.refs_0_), channel_id=1, source_target_pairs={{0,16},{8,24},{16,0},{24,8},{1,17},{9,25},{17,1},{25,9},{2,18},{10... | collective-permute-start | bytes 786440 | tf_op jit(solution)/shard_map/ppermute | solution.py:479
  41.0 20.9 %collective-permute-start.3 = (f32[64,1024]{1,0:T(8,128)S(1)}, f32[64,1024]{1,0:T(8,128)S(1)}, u32[]{:S(2)}, u32[]{:S(2)}) collective-permute-start(f32[64,1024]{1,0:T(8,128)S(1)} %get-tuple-element.31.refs_4_.refs_0_), channel_id=1, source_target_pairs={{0,8},{8,0},{16,24},{24,16},{1,9},{9,1},{17,25},{25,17},{2,10},{10... | collective-permute-start | bytes 786440 | tf_op jit(solution)/shard_map/ppermute | solution.py:479
  50.5 11.4 %collective-permute-start.15 = (f32[4,64,256]{2,1,0:T(8,128)S(1)}, f32[4,64,256]{2,1,0:T(8,128)S(1)}, u32[]{:S(2)}, u32[]{:S(2)}) collective-permute-start(f32[4,64,256]{2,1,0:T(8,128)S(1)} %backward.1.refs_2_.refs_0_), channel_id=1, source_target_pairs={{0,6},{2,4},{4,2},{6,0},{1,7},{3,5},{5,3},{7,1},{8,14},{10,12},{12... | collective-permute-start | bytes 786440 | tf_op jit(solution)/shard_map/ppermute | solution.py:479
  52.0 11.7 %collective-permute-start.14 = (f32[4,64,256]{2,1,0:T(8,128)S(1)}, f32[4,64,256]{2,1,0:T(8,128)S(1)}, u32[]{:S(2)}, u32[]{:S(2)}) collective-permute-start(f32[4,64,256]{2,1,0:T(8,128)S(1)} %backward.1.refs_2_.refs_0_), channel_id=1, source_target_pairs={{0,4},{2,6},{4,0},{6,2},{1,5},{3,7},{5,1},{7,3},{8,12},{10,14},{12... | collective-permute-start | bytes 786440 | tf_op jit(solution)/shard_map/ppermute | solution.py:479
  52.7 11.0 %collective-permute-start.13 = (f32[4,64,256]{2,1,0:T(8,128)S(1)}, f32[4,64,256]{2,1,0:T(8,128)S(1)}, u32[]{:S(2)}, u32[]{:S(2)}) collective-permute-start(f32[4,64,256]{2,1,0:T(8,128)S(1)} %backward.1.refs_2_.refs_0_), channel_id=1, source_target_pairs={{0,2},{2,0},{4,6},{6,4},{1,3},{3,1},{5,7},{7,5},{8,10},{10,8},{12,... | collective-permute-start | bytes 786440 | tf_op jit(solution)/shard_map/ppermute | solution.py:479
  56.0 10.3 %collective-permute-start.6 = (f32[64,1024]{1,0:T(8,128)S(1)}, f32[64,1024]{1,0:T(8,128)S(1)}, u32[]{:S(2)}, u32[]{:S(2)}) collective-permute-start(f32[64,1024]{1,0:T(8,128)S(1)} %get-tuple-element.31.refs_4_.refs_0_), channel_id=1, source_target_pairs={{0,1},{1,0},{2,3},{3,2},{4,5},{5,4},{6,7},{7,6},{8,9},{9,8},{10,11... | collective-permute-start | bytes 786440 | tf_op jit(solution)/shard_map/ppermute | solution.py:479
  63.7 19.9 %slice-start = ((s8[16777216]{0:T(1024)(128)(4,1)}), s8[4194304]{0:T(1024)(128)(4,1)S(1)}, s32[]{:S(2)}) async-start(s8[16777216]{0:T(1024)(128)(4,1)} %bitcast.11), calls=%async_computation | async-start | bytes 8388608
  63.7 19.9 %slice-start.1 = ((s8[16777216]{0:T(1024)(128)(4,1)}), s8[4194304]{0:T(1024)(128)(4,1)S(1)}, s32[]{:S(2)}) async-start(s8[16777216]{0:T(1024)(128)(4,1)} %bitcast.11), calls=%async_computation.1 | async-start | bytes 8388608
  63.7 19.9 %slice-start.2 = ((s8[16777216]{0:T(1024)(128)(4,1)}), s8[4194304]{0:T(1024)(128)(4,1)S(1)}, s32[]{:S(2)}) async-start(s8[16777216]{0:T(1024)(128)(4,1)} %bitcast.11), calls=%async_computation.2 | async-start | bytes 8388608
  64.6 8.1 %collective-permute-start.18 = (f32[64,512]{1,0:T(8,128)S(1)}, f32[64,512]{1,0:T(8,128)S(1)}, u32[]{:S(2)}, u32[]{:S(2)}) collective-permute-start(f32[64,512]{1,0:T(8,128)S(1)} %get-tuple-element.34.refs_1_.refs_8_), channel_id=1, source_target_pairs={{0,24},{8,16},{16,8},{24,0},{1,25},{9,17},{17,9},{25,1},{2,26},{10... | collective-permute-start | bytes 393224 | tf_op jit(solution)/shard_map/ppermute | solution.py:479
  65.6 13.0 %collective-permute-start.9 = (f32[64,1024]{1,0:T(8,128)S(1)}, f32[64,1024]{1,0:T(8,128)S(1)}, u32[]{:S(2)}, u32[]{:S(2)}) collective-permute-start(f32[64,1024]{1,0:T(8,128)S(1)} %collective-permute-done.5.refs_7_.refs_3_), channel_id=1, source_target_pairs={{0,1},{1,0},{2,3},{3,2},{4,5},{5,4},{6,7},{7,6},{8,9},{9,8},{10,11... | collective-permute-start | bytes 786440 | tf_op jit(solution)/shard_map/ppermute | solution.py:479
  65.7 15.4 %collective-permute-start.8 = (f32[64,1024]{1,0:T(8,128)S(1)}, f32[64,1024]{1,0:T(8,128)S(1)}, u32[]{:S(2)}, u32[]{:S(2)}) collective-permute-start(f32[64,1024]{1,0:T(8,128)S(1)} %collective-permute-done.4.refs_6_.refs_2_), channel_id=1, source_target_pairs={{0,1},{1,0},{2,3},{3,2},{4,5},{5,4},{6,7},{7,6},{8,9},{9,8},{10,11... | collective-permute-start | bytes 786440 | tf_op jit(solution)/shard_map/ppermute | solution.py:479
  66.1 15.2 %collective-permute-start.7 = (f32[64,1024]{1,0:T(8,128)S(1)}, f32[64,1024]{1,0:T(8,128)S(1)}, u32[]{:S(2)}, u32[]{:S(2)}) collective-permute-start(f32[64,1024]{1,0:T(8,128)S(1)} %collective-permute-done.3.refs_5_.refs_1_), channel_id=1, source_target_pairs={{0,1},{1,0},{2,3},{3,2},{4,5},{5,4},{6,7},{7,6},{8,9},{9,8},{10,11... | collective-permute-start | bytes 786440 | tf_op jit(solution)/shard_map/ppermute | solution.py:479
  66.2 11.0 %collective-permute-start.17 = (f32[64,512]{1,0:T(8,128)S(1)}, f32[64,512]{1,0:T(8,128)S(1)}, u32[]{:S(2)}, u32[]{:S(2)}) collective-permute-start(f32[64,512]{1,0:T(8,128)S(1)} %get-tuple-element.34.refs_1_.refs_8_), channel_id=1, source_target_pairs={{0,16},{8,24},{16,0},{24,8},{1,17},{9,25},{17,1},{25,9},{2,18},{10... | collective-permute-start | bytes 393224 | tf_op jit(solution)/shard_map/ppermute | solution.py:479
  72.7 5.8 %collective-permute-start.16 = (f32[64,512]{1,0:T(8,128)S(1)}, f32[64,512]{1,0:T(8,128)S(1)}, u32[]{:S(2)}, u32[]{:S(2)}) collective-permute-start(f32[64,512]{1,0:T(8,128)S(1)} %get-tuple-element.34.refs_1_.refs_8_), channel_id=1, source_target_pairs={{0,8},{8,0},{16,24},{24,16},{1,9},{9,1},{17,25},{25,17},{2,10},{10... | collective-permute-start | bytes 393224 | tf_op jit(solution)/shard_map/ppermute | solution.py:479
  77.2 4.4 %collective-permute-start.22 = (f32[64,512]{1,0:T(8,128)S(1)}, f32[64,512]{1,0:T(8,128)S(1)}, u32[]{:S(2)}, u32[]{:S(2)}) collective-permute-start(f32[64,512]{1,0:T(8,128)S(1)} %get-tuple-element.34.refs_1_.refs_8_), channel_id=1, source_target_pairs={{0,1},{1,0},{2,3},{3,2},{4,5},{5,4},{6,7},{7,6},{8,9},{9,8},{10,11... | collective-permute-start | bytes 393224 | tf_op jit(solution)/shard_map/ppermute | solution.py:479
  78.5 3.1 %collective-permute-start.25 = (f32[64,512]{1,0:T(8,128)S(1)}, f32[64,512]{1,0:T(8,128)S(1)}, u32[]{:S(2)}, u32[]{:S(2)}) collective-permute-start(f32[64,512]{1,0:T(8,128)S(1)} %collective-permute-done.18.refs_4_.refs_11_), channel_id=1, source_target_pairs={{0,1},{1,0},{2,3},{3,2},{4,5},{5,4},{6,7},{7,6},{8,9},{9,8},{10,11... | collective-permute-start | bytes 393224 | tf_op jit(solution)/shard_map/ppermute | solution.py:479
  78.5 19.0 %slice-start.4 = ((s8[16777216]{0:T(1024)(128)(4,1)}), s8[4194304]{0:T(1024)(128)(4,1)S(1)}, s32[]{:S(2)}) async-start(s8[16777216]{0:T(1024)(128)(4,1)} %bitcast.13), calls=%async_computation.4 | async-start | bytes 8388608
  78.6 19.0 %slice-start.5 = ((s8[16777216]{0:T(1024)(128)(4,1)}), s8[4194304]{0:T(1024)(128)(4,1)S(1)}, s32[]{:S(2)}) async-start(s8[16777216]{0:T(1024)(128)(4,1)} %bitcast.13), calls=%async_computation.5 | async-start | bytes 8388608
  78.6 19.0 %slice-start.6 = ((s8[16777216]{0:T(1024)(128)(4,1)}), s8[4194304]{0:T(1024)(128)(4,1)S(1)}, s32[]{:S(2)}) async-start(s8[16777216]{0:T(1024)(128)(4,1)} %bitcast.13), calls=%async_computation.6 | async-start | bytes 8388608
  78.6 18.9 %slice-start.7 = ((s8[16777216]{0:T(1024)(128)(4,1)}), s8[4194304]{0:T(1024)(128)(4,1)S(1)}, s32[]{:S(2)}) async-start(s8[16777216]{0:T(1024)(128)(4,1)} %bitcast.13), calls=%async_computation.7 | async-start | bytes 8388608
  78.6 16.8 %collective-permute-start.21 = (f32[64,512]{1,0:T(8,128)S(1)}, f32[64,512]{1,0:T(8,128)S(1)}, u32[]{:S(2)}, u32[]{:S(2)}) collective-permute-start(f32[64,512]{1,0:T(8,128)S(1)} %passed.2.refs_0_), channel_id=1, source_target_pairs={{0,24},{8,16},{16,8},{24,0},{1,25},{9,17},{17,9},{25,1},{2,26},{10... | collective-permute-start | bytes 393224 | tf_op jit(solution)/shard_map/ppermute | solution.py:479
  81.1 2.5 %collective-permute-start.24 = (f32[64,512]{1,0:T(8,128)S(1)}, f32[64,512]{1,0:T(8,128)S(1)}, u32[]{:S(2)}, u32[]{:S(2)}) collective-permute-start(f32[64,512]{1,0:T(8,128)S(1)} %collective-permute-done.17.refs_3_.refs_10_), channel_id=1, source_target_pairs={{0,1},{1,0},{2,3},{3,2},{4,5},{5,4},{6,7},{7,6},{8,9},{9,8},{10,11... | collective-permute-start | bytes 393224 | tf_op jit(solution)/shard_map/ppermute | solution.py:479
  81.3 2.3 %collective-permute-start.23 = (f32[64,512]{1,0:T(8,128)S(1)}, f32[64,512]{1,0:T(8,128)S(1)}, u32[]{:S(2)}, u32[]{:S(2)}) collective-permute-start(f32[64,512]{1,0:T(8,128)S(1)} %collective-permute-done.16.refs_2_.refs_9_), channel_id=1, source_target_pairs={{0,1},{1,0},{2,3},{3,2},{4,5},{5,4},{6,7},{7,6},{8,9},{9,8},{10,11... | collective-permute-start | bytes 393224 | tf_op jit(solution)/shard_map/ppermute | solution.py:479
  81.6 13.8 %collective-permute-start.20 = (f32[64,512]{1,0:T(8,128)S(1)}, f32[64,512]{1,0:T(8,128)S(1)}, u32[]{:S(2)}, u32[]{:S(2)}) collective-permute-start(f32[64,512]{1,0:T(8,128)S(1)} %passed.2.refs_0_), channel_id=1, source_target_pairs={{0,16},{8,24},{16,0},{24,8},{1,17},{9,25},{17,1},{25,9},{2,18},{10... | collective-permute-start | bytes 393224 | tf_op jit(solution)/shard_map/ppermute | solution.py:479
  81.6 13.8 %collective-permute-start.19 = (f32[64,512]{1,0:T(8,128)S(1)}, f32[64,512]{1,0:T(8,128)S(1)}, u32[]{:S(2)}, u32[]{:S(2)}) collective-permute-start(f32[64,512]{1,0:T(8,128)S(1)} %passed.2.refs_0_), channel_id=1, source_target_pairs={{0,8},{8,0},{16,24},{24,16},{1,9},{9,1},{17,25},{25,17},{2,10},{10... | collective-permute-start | bytes 393224 | tf_op jit(solution)/shard_map/ppermute | solution.py:479
  95.4 1.4 %collective-permute-start.26 = (f32[64,512]{1,0:T(8,128)S(1)}, f32[64,512]{1,0:T(8,128)S(1)}, u32[]{:S(2)}, u32[]{:S(2)}) collective-permute-start(f32[64,512]{1,0:T(8,128)S(1)} %get-tuple-element.36.refs_8_), channel_id=1, source_target_pairs={{0,1},{1,0},{2,3},{3,2},{4,5},{5,4},{6,7},{7,6},{8,9},{9,8},{10,11... | collective-permute-start | bytes 393224 | tf_op jit(solution)/shard_map/ppermute | solution.py:479
  95.5 1.5 %collective-permute-start.27 = (f32[64,512]{1,0:T(8,128)S(1)}, f32[64,512]{1,0:T(8,128)S(1)}, u32[]{:S(2)}, u32[]{:S(2)}) collective-permute-start(f32[64,512]{1,0:T(8,128)S(1)} %get-tuple-element.37.refs_9_), channel_id=1, source_target_pairs={{0,1},{1,0},{2,3},{3,2},{4,5},{5,4},{6,7},{7,6},{8,9},{9,8},{10,11... | collective-permute-start | bytes 393224 | tf_op jit(solution)/shard_map/ppermute | solution.py:479
  96.0 1.3 %collective-permute-start.28 = (f32[64,512]{1,0:T(8,128)S(1)}, f32[64,512]{1,0:T(8,128)S(1)}, u32[]{:S(2)}, u32[]{:S(2)}) collective-permute-start(f32[64,512]{1,0:T(8,128)S(1)} %get-tuple-element.38.refs_10_), channel_id=1, source_target_pairs={{0,1},{1,0},{2,3},{3,2},{4,5},{5,4},{6,7},{7,6},{8,9},{9,8},{10,11... | collective-permute-start | bytes 393224 | tf_op jit(solution)/shard_map/ppermute | solution.py:479
  96.1 1.5 %collective-permute-start.29 = (f32[64,512]{1,0:T(8,128)S(1)}, f32[64,512]{1,0:T(8,128)S(1)}, u32[]{:S(2)}, u32[]{:S(2)}) collective-permute-start(f32[64,512]{1,0:T(8,128)S(1)} %get-tuple-element.39.refs_11_), channel_id=1, source_target_pairs={{0,1},{1,0},{2,3},{3,2},{4,5},{5,4},{6,7},{7,6},{8,9},{9,8},{10,11... | collective-permute-start | bytes 393224 | tf_op jit(solution)/shard_map/ppermute | solution.py:479
  (1 other events, 5.1 us)

commit v5 on v4

--- a/solution.py
+++ b/solution.py
@@ -234,19 +234,20 @@
     n = (len(refs) - 5) // 2
     given, (out_ref, mid_ref, first_ref, second_ref) = refs[:n], refs[n : n + 4]
     held, sems = refs[n + 4 : -1], refs[-1]
-    state_ref, gain_ref, to_grid_ref, table_ref = held[:4]
+    state_ref, gain_ref, to_grid_ref = held[:3]
+    table_ref = held[-1]
     copies = [pltpu.make_async_copy(a, b, sems.at[k]) for k, (a, b) in enumerate(zip(given, held))]
     for copy in copies:
         copy.start()
-    for copy in copies[:3]:
+    for copy in copies[:-1]:
         copy.wait()
+    up, down = first_stage(state_ref, *held[3:-1], mid_ref)
     grid = grid_values(to_grid_ref[...], read_field(state_ref, 0))
     grid = grid.astype(BF16).astype(F32)
     gain = column_of(gain_ref[...])
     cells = grid.shape[1]
     channels = gain.shape[0]
-    for copy in copies[3:]:
-        copy.wait()
+    copies[-1].wait()
     for pair in range(0, PLANES, 2):
         total = jnp.zeros((2 * channels, JOINT), F32)
         for j in range(CELLS):
@@ -262,7 +263,6 @@
         for k in range(2):
             for ref in (out_ref, first_ref, second_ref)[: 3 if joined else 1]:
                 ref[pair + k] = total[k * channels : (k + 1) * channels]
-    up, down = first_stage(state_ref, *held[4:], mid_ref)
     if joined:
         even = (me_ref[0] & 1) == 0
         first_ref[PLANES] = jnp.where(even, up, down)
@@ -574,7 +574,7 @@
     def shape_of(array):
         return jax.ShapeDtypeStruct(array.shape, array.dtype)
 
-    given = (flat, gain_row, to_grid, table, absorb_mask, damping, slopes, faces)
+    given = (flat, gain_row, to_grid, absorb_mask, damping, slopes, faces, table)
     joined = count == 4
     faces_out = jax.ShapeDtypeStruct((64, cells), F32)
     if joined:

time: 110 us -> 109 us (level)
  transfers between devices with their start and end apart: 30 -> 30, of which waited for: 14 -> 14; matrix products, arithmetic and copies ran while one was open for 0% -> 0% of each run, Pallas kernels for 31% -> 32%
where the time goes in v5:
time: 109 us
  Pallas kernels  57 us (52%)
  waiting for transfers between devices  27.8 us (26%)
  starting transfers between devices  22.9 us (21%)
  between operations  1.09 us (1%)
    ppermute x30, waiting for transfers between devices, exchanged(): lax.ppermute(array, axis, [(i, i ^ b) for i in range(lax.axis_size(axis))])  27.8 us
    pallas_call x2, Pallas kernels, per_device(): pl.pallas_call(functools.partial(update_kernel, chunk, tiles), grid=(chan...  23.7 us
    ppermute x30, starting transfers between devices, exchanged(): lax.ppermute(array, axis, [(i, i ^ b) for i in range(lax.axis_size(axis))])  22.9 us
    pallas_call x2, Pallas kernels, loaded(): pl.pallas_call(functools.partial(load_kernel, n), in_specs=[ANY_SPEC] * (...  11.8 us
    pallas_call x1, Pallas kernels, per_device(): pl.pallas_call(functools.partial(backward_kernel, count, len(every_mixed)...  8.03 us
    pallas_call x1, Pallas kernels, per_device(): pl.pallas_call(functools.partial(lift_kernel, joined), in_specs=[SMEM_SPE...  6.72 us
    pallas_call x1, Pallas kernels, per_device(): pl.pallas_call(functools.partial(mix_kernel, count, len(gathered)), in_sp...  3.99 us
  transfers between devices with their start and end apart: 30, of which 14 were waited for; matrix products, arithmetic and copies ran while one was open for 0% of the time, Pallas kernels for 32%

profile of v5, /device:TPU:0, one launch (start us, length us, event | category | flops | bytes accessed | tf_op | source)
XLA Modules:
  0.0 109.0 jit_solution(2144877907629047891)
XLA Ops:
  0.6 6.7 %lift.1 = (f32[4,64,256]{2,1,0:T(8,128)S(1)}, f32[4,128,256]{2,1,0:T(8,128)S(1)}, f32[5,64,256]{2,1,0:T(8,128)S(1)}, f32[5,64,256]{2,1,0:T(8,128)S(1)}) custom-call(s32[1]{0:T(128)} %bitcast.me_ref, f32[1000,128]{1,0:T(8,128)} %bitcast.15, f32[1,64]{1,0:T(1,128)} %bitcast.24, f32[64,128]{1,0:T(8,128)} %constant.19.clone.refs_2_.to_grid_ref, ...), custom_call_target="tpu_custom_call" | custom-call | flops 1000 | bytes 1000 | tf_op jit(solution)/shard_map/lift/pallas_call | solution.py:582
  7.4 3.0 %collective-permute-start = (f32[5,64,256]{2,1,0:T(8,128)S(1)}, f32[5,64,256]{2,1,0:T(8,128)S(1)}, u32[]{:S(2)}, u32[]{:S(2)}) collective-permute-start(f32[5,64,256]{2,1,0:T(8,128)S(1)} %get-tuple-element.26), channel_id=1, source_target_pairs={{0,2},{2,0},{4,6},{6,4},{1,3},{3,1},{5,7},{7,5},{8,10},{10,8},{12,... | collective-permute-start | bytes 983048 | tf_op jit(solution)/shard_map/ppermute | solution.py:479
  10.4 1.5 %collective-permute-start.1 = (f32[5,64,256]{2,1,0:T(8,128)S(1)}, f32[5,64,256]{2,1,0:T(8,128)S(1)}, u32[]{:S(2)}, u32[]{:S(2)}) collective-permute-start(f32[5,64,256]{2,1,0:T(8,128)S(1)} %get-tuple-element.27), channel_id=1, source_target_pairs={{0,6},{2,4},{4,2},{6,0},{1,7},{3,5},{5,3},{7,1},{8,14},{10,12},{12... | collective-permute-start | bytes 983048 | tf_op jit(solution)/shard_map/ppermute | solution.py:479
  11.9 0.1 collective-permute-start.2
  11.9 5.9 %load.2.refs_4_.refs_16_ = f32[64,64,1024]{2,1,0:T(8,128)S(1)} custom-call(f32[64,64,1024]{2,1,0:T(8,128)} %bitcast.18, f32[4,128,256]{2,1,0:T(8,128)S(1)} %get-tuple-element.25.refs_1_.mid_ref), custom_call_target="tpu_custom_call" | custom-call | bytes 33554432 | tf_op jit(solution)/shard_map/load/pallas_call | solution.py:506
  17.8 0.0 copy-start.4
  17.8 0.0 copy-start.5
  17.9 0.0 copy-start.6
  17.9 2.6 %collective-permute-done.2.refs_2_ = f32[4,64,256]{2,1,0:T(8,128)S(1)} collective-permute-done((f32[4,64,256]{2,1,0:T(8,128)S(1)}, f32[4,64,256]{2,1,0:T(8,128)S(1)}, u32[]{:S(2)}, u32[]{:S(2)}) %collective-permute-start.2) | collective-permute-done | bytes 262176 | tf_op jit(solution)/shard_map/ppermute | solution.py:479
  20.5 5.9 %collective-permute-done.1.refs_3_.second_ref = f32[5,64,256]{2,1,0:T(8,128)S(1)} collective-permute-done((f32[5,64,256]{2,1,0:T(8,128)S(1)}, f32[5,64,256]{2,1,0:T(8,128)S(1)}, u32[]{:S(2)}, u32[]{:S(2)}) %collective-permute-start.1) | collective-permute-done | bytes 327712 | tf_op jit(solution)/shard_map/ppermute | solution.py:479
  26.4 4.0 %mix.1 = (f32[64,1024]{1,0:T(8,128)S(1)}, bf16[64,1024]{1,0:T(8,128)(2,1)S(1)}) custom-call(s32[1]{0:T(128)} %bitcast.me_ref, f32[16,16]{1,0:T(8,128)S(1)} %copy-done.7, f32[4,64,256]{2,1,0:T(8,128)S(1)} %get-tuple-element.28.refs_0_, f32[5,64,256]{2,1,0:T(8,128)S(1)} %collective-permute-done.refs_1_.first_ref, ...), custom_call_target="tpu_custom_call" | custom-call | flops 1000 | bytes 1000 | tf_op jit(solution)/shard_map/mix/pallas_call | solution.py:607
  30.4 3.7 %collective-permute-start.5 = (f32[64,1024]{1,0:T(8,128)S(1)}, f32[64,1024]{1,0:T(8,128)S(1)}, u32[]{:S(2)}, u32[]{:S(2)}) collective-permute-start(f32[64,1024]{1,0:T(8,128)S(1)} %get-tuple-element.31.refs_4_.refs_0_), channel_id=1, source_target_pairs={{0,24},{8,16},{16,8},{24,0},{1,25},{9,17},{17,9},{25,1},{2,26},{10... | collective-permute-start | bytes 786440 | tf_op jit(solution)/shard_map/ppermute | solution.py:479
  34.0 1.4 %collective-permute-start.12 = (bf16[64,1024]{1,0:T(8,128)(2,1)S(1)}, bf16[64,1024]{1,0:T(8,128)(2,1)S(1)}, u32[]{:S(2)}, u32[]{:S(2)}) collective-permute-start(bf16[64,1024]{1,0:T(8,128)(2,1)S(1)} %get-tuple-element.29.after_ref.refs_0_), channel_id=1, source_target_pairs={{0,6},{2,4},{4,2},{6,0},{1,7},{3,5},{5,3},{7,1},{8,14},{10,12},{12... | collective-permute-start | bytes 393224 | tf_op jit(solution)/shard_map/ppermute | solution.py:479
  35.5 1.5 %collective-permute-start.11 = (bf16[64,1024]{1,0:T(8,128)(2,1)S(1)}, bf16[64,1024]{1,0:T(8,128)(2,1)S(1)}, u32[]{:S(2)}, u32[]{:S(2)}) collective-permute-start(bf16[64,1024]{1,0:T(8,128)(2,1)S(1)} %get-tuple-element.29.after_ref.refs_0_), channel_id=1, source_target_pairs={{0,4},{2,6},{4,0},{6,2},{1,5},{3,7},{5,1},{7,3},{8,12},{10,14},{12... | collective-permute-start | bytes 393224 | tf_op jit(solution)/shard_map/ppermute | solution.py:479
  37.0 0.5 collective-permute-start.10
  37.6 1.8 %second_stage.1 = (f32[1000,128]{1,0:T(8,128)}, f32[64,256]{1,0:T(8,128)S(1)}) custom-call(s32[1]{0:T(128)} %bitcast.me_ref, f32[1000,128]{1,0:T(8,128)S(1)} %bitcast.16, f32[4,128,256]{2,1,0:T(8,128)S(1)} %get-tuple-element.25.refs_1_.mid_ref, f32[5,64,256]{2,1,0:T(8,128)S(1)} %collective-permute-done.refs_1_.first_ref, ...), custom_call_target="tpu_custom_call" | custom-call | flops 1000 | bytes 1000 | tf_op jit(solution)/shard_map/second_stage/pallas_call | solution.py:622
  39.4 1.1 collective-permute-done.12.refs_3_
  40.5 1.3 %collective-permute-done.11.refs_2_ = bf16[64,1024]{1,0:T(8,128)(2,1)S(1)} collective-permute-done((bf16[64,1024]{1,0:T(8,128)(2,1)S(1)}, bf16[64,1024]{1,0:T(8,128)(2,1)S(1)}, u32[]{:S(2)}, u32[]{:S(2)}) %collective-permute-start.11) | collective-permute-done | bytes 131104 | tf_op jit(solution)/shard_map/ppermute | solution.py:479
  41.8 0.2 collective-permute-done.10.refs_1_
  42.0 8.0 %backward.1.refs_2_.refs_0_ = f32[4,64,256]{2,1,0:T(8,128)S(1)} custom-call(s32[1]{0:T(128)} %bitcast.me_ref, f32[16,16]{1,0:T(8,128)S(1)} %copy-done.7, bf16[64,1024]{1,0:T(8,128)(2,1)S(1)} %get-tuple-element.29.after_ref.refs_0_, bf16[64,1024]{1,0:T(8,128)(2,1)S(1)} %collective-permute-done.10.refs_1_, ...), custom_call_target="tpu_custom_call" | custom-call | flops 1000 | bytes 1000 | tf_op jit(solution)/shard_map/backward/pallas_call | solution.py:639
  50.0 1.4 %collective-permute-start.15 = (f32[4,64,256]{2,1,0:T(8,128)S(1)}, f32[4,64,256]{2,1,0:T(8,128)S(1)}, u32[]{:S(2)}, u32[]{:S(2)}) collective-permute-start(f32[4,64,256]{2,1,0:T(8,128)S(1)} %backward.1.refs_2_.refs_0_), channel_id=1, source_target_pairs={{0,6},{2,4},{4,2},{6,0},{1,7},{3,5},{5,3},{7,1},{8,14},{10,12},{12... | collective-permute-start | bytes 786440 | tf_op jit(solution)/shard_map/ppermute | solution.py:479
  51.4 0.7 collective-permute-start.14
  52.1 1.4 %collective-permute-start.13 = (f32[4,64,256]{2,1,0:T(8,128)S(1)}, f32[4,64,256]{2,1,0:T(8,128)S(1)}, u32[]{:S(2)}, u32[]{:S(2)}) collective-permute-start(f32[4,64,256]{2,1,0:T(8,128)S(1)} %backward.1.refs_2_.refs_0_), channel_id=1, source_target_pairs={{0,2},{2,0},{4,6},{6,4},{1,3},{3,1},{5,7},{7,5},{8,10},{10,8},{12,... | collective-permute-start | bytes 786440 | tf_op jit(solution)/shard_map/ppermute | solution.py:479
  53.6 1.8 %collective-permute-done.4.refs_6_.refs_2_ = f32[64,1024]{1,0:T(8,128)S(1)} collective-permute-done((f32[64,1024]{1,0:T(8,128)S(1)}, f32[64,1024]{1,0:T(8,128)S(1)}, u32[]{:S(2)}, u32[]{:S(2)}) %collective-permute-start.4) | collective-permute-done | bytes 262176 | tf_op jit(solution)/shard_map/ppermute | solution.py:479
  55.4 5.9 %load.3.refs_8_.refs_5_.refs_17_ = bf16[128,64,1024]{2,1,0:T(8,128)(2,1)S(1)} custom-call(bf16[64,64,1024]{2,1,0:T(8,128)(2,1)} %bitcast.22, bf16[64,64,1024]{2,1,0:T(8,128)(2,1)} %bitcast.23, f32[4,64,256]{2,1,0:T(8,128)S(1)} %backward.1.refs_2_.refs_0_), custom_call_target="tpu_custom_call" | custom-call | bytes 33554432 | tf_op jit(solution)/shard_map/load/pallas_call | solution.py:506
  61.4 1.7 %collective-permute-done.14.refs_2_ = f32[4,64,256]{2,1,0:T(8,128)S(1)} collective-permute-done((f32[4,64,256]{2,1,0:T(8,128)S(1)}, f32[4,64,256]{2,1,0:T(8,128)S(1)}, u32[]{:S(2)}, u32[]{:S(2)}) %collective-permute-start.14) | collective-permute-done | bytes 262176 | tf_op jit(solution)/shard_map/ppermute | solution.py:479
  63.1 1.0 grad_coeffs.1
  64.1 1.0 collective-permute-start.18
  65.0 0.1 collective-permute-start.9
  65.2 0.4 collective-permute-start.8
  65.5 0.1 collective-permute-start.7
  65.7 6.4 %collective-permute-done.18.refs_4_.refs_11_ = f32[64,512]{1,0:T(8,128)S(1)} collective-permute-done((f32[64,512]{1,0:T(8,128)S(1)}, f32[64,512]{1,0:T(8,128)S(1)}, u32[]{:S(2)}, u32[]{:S(2)}) %collective-permute-start.18) | collective-permute-done | bytes 131104 | tf_op jit(solution)/shard_map/ppermute | solution.py:479
  72.1 4.5 %collective-permute-done.17.refs_3_.refs_10_ = f32[64,512]{1,0:T(8,128)S(1)} collective-permute-done((f32[64,512]{1,0:T(8,128)S(1)}, f32[64,512]{1,0:T(8,128)S(1)}, u32[]{:S(2)}, u32[]{:S(2)}) %collective-permute-start.17) | collective-permute-done | bytes 131104 | tf_op jit(solution)/shard_map/ppermute | solution.py:479
  76.6 1.3 %collective-permute-done.16.refs_2_.refs_9_ = f32[64,512]{1,0:T(8,128)S(1)} collective-permute-done((f32[64,512]{1,0:T(8,128)S(1)}, f32[64,512]{1,0:T(8,128)S(1)}, u32[]{:S(2)}, u32[]{:S(2)}) %collective-permute-start.16) | collective-permute-done | bytes 131104 | tf_op jit(solution)/shard_map/ppermute | solution.py:479
  78.0 2.6 %collective-permute-start.21 = (f32[64,512]{1,0:T(8,128)S(1)}, f32[64,512]{1,0:T(8,128)S(1)}, u32[]{:S(2)}, u32[]{:S(2)}) collective-permute-start(f32[64,512]{1,0:T(8,128)S(1)} %passed.2.refs_0_), channel_id=1, source_target_pairs={{0,24},{8,16},{16,8},{24,0},{1,25},{9,17},{17,9},{25,1},{2,26},{10... | collective-permute-start | bytes 393224 | tf_op jit(solution)/shard_map/ppermute | solution.py:479
  80.5 0.2 collective-permute-start.24
  80.8 0.3 collective-permute-start.23
  81.1 1.9 %collective-permute-start.19 = (f32[64,512]{1,0:T(8,128)S(1)}, f32[64,512]{1,0:T(8,128)S(1)}, u32[]{:S(2)}, u32[]{:S(2)}) collective-permute-start(f32[64,512]{1,0:T(8,128)S(1)} %passed.2.refs_0_), channel_id=1, source_target_pairs={{0,8},{8,0},{16,24},{24,16},{1,9},{9,1},{17,25},{25,17},{2,10},{10... | collective-permute-start | bytes 393224 | tf_op jit(solution)/shard_map/ppermute | solution.py:479
  83.0 11.7 %update_0.1 = (f32[64,64,1024]{2,1,0:T(8,128)}, bf16[64,64,1024]{2,1,0:T(8,128)(2,1)}, bf16[64,64,1024]{2,1,0:T(8,128)(2,1)}, f32[8,128]{1,0:T(8,128)S(1)}) custom-call(f32[64,1024]{1,0:T(8,128)S(1)} %get-tuple-element.31.refs_4_.refs_0_, f32[64,1024]{1,0:T(8,128)S(1)} %collective-permute-done.3.refs_5_.refs_1_, ...), custom_call_target="tpu_custom_call" | custom-call | flops 1000 | bytes 1000 | tf_op jit(solution)/shard_map/update_0/pallas_call | solution.py:681
  94.8 0.1 collective-permute-start.26
  94.9 0.5 collective-permute-start.27
  95.4 0.1 collective-permute-start.28
  95.4 0.4 collective-permute-start.29
  95.9 0.3 collective-permute-done.26.refs_12_
  96.2 0.2 collective-permute-done.27.refs_13_
  96.4 0.3 collective-permute-done.28.refs_14_
  96.7 0.2 collective-permute-done.29.refs_15_
  96.9 11.9 %update_1.1 = (f32[64,64,1024]{2,1,0:T(8,128)}, bf16[64,64,1024]{2,1,0:T(8,128)(2,1)}, bf16[64,64,1024]{2,1,0:T(8,128)(2,1)}, f32[8,128]{1,0:T(8,128)}) custom-call(f32[64,1024]{1,0:T(8,128)S(1)} %get-tuple-element.31.refs_4_.refs_0_, ...), custom_call_target="tpu_custom_call", output_to_operand_aliasing={{0}: (18, {}), {1}: (19, {}), {2}: (20, {})} | custom-call | flops 1000 | bytes 1000 | tf_op jit(solution)/shard_map/update_1/pallas_call | solution.py:681
  (63 shorter events, 0.2 us)
Async XLA Ops:
  7.4 13.1 %collective-permute-start = (f32[5,64,256]{2,1,0:T(8,128)S(1)}, f32[5,64,256]{2,1,0:T(8,128)S(1)}, u32[]{:S(2)}, u32[]{:S(2)}) collective-permute-start(f32[5,64,256]{2,1,0:T(8,128)S(1)} %get-tuple-element.26), channel_id=1, source_target_pairs={{0,2},{2,0},{4,6},{6,4},{1,3},{3,1},{5,7},{7,5},{8,10},{10,8},{12,... | collective-permute-start | bytes 983048 | tf_op jit(solution)/shard_map/ppermute | solution.py:479
  10.4 16.0 %collective-permute-start.1 = (f32[5,64,256]{2,1,0:T(8,128)S(1)}, f32[5,64,256]{2,1,0:T(8,128)S(1)}, u32[]{:S(2)}, u32[]{:S(2)}) collective-permute-start(f32[5,64,256]{2,1,0:T(8,128)S(1)} %get-tuple-element.27), channel_id=1, source_target_pairs={{0,6},{2,4},{4,2},{6,0},{1,7},{3,5},{5,3},{7,1},{8,14},{10,12},{12... | collective-permute-start | bytes 983048 | tf_op jit(solution)/shard_map/ppermute | solution.py:479
  11.9 8.6 %collective-permute-start.2 = (f32[4,64,256]{2,1,0:T(8,128)S(1)}, f32[4,64,256]{2,1,0:T(8,128)S(1)}, u32[]{:S(2)}, u32[]{:S(2)}) collective-permute-start(f32[4,64,256]{2,1,0:T(8,128)S(1)} %get-tuple-element.28.refs_0_), channel_id=1, source_target_pairs={{0,4},{2,6},{4,0},{6,2},{1,5},{3,7},{5,1},{7,3},{8,12},{10,14},{12... | collective-permute-start | bytes 786440 | tf_op jit(solution)/shard_map/ppermute | solution.py:479
  11.9 14.5 %copy-start.7 = (f32[16,16]{1,0:T(8,128)S(1)}, f32[16,16]{1,0:T(8,128)}, u32[]{:S(2)}) copy-start(f32[16,16]{1,0:T(8,128)} %constant.23.clone.fx_ref) | copy-start | bytes 3076
  17.8 12.5 %copy-start = (f32[64,64,1024]{2,1,0:T(8,128)}, f32[64,64,1024]{2,1,0:T(8,128)S(1)}, u32[]{:S(2)}) copy-start(f32[64,64,1024]{2,1,0:T(8,128)S(1)} %load.2.refs_4_.refs_16_) | copy-start | bytes 50331652
  17.8 19.7 %copy-start.3 = (f32[1,4,125,1,256]{4,3,2,1,0:T(1,128)S(1)}, f32[1,4,125,1,256]{4,3,2,1,0:T(1,128)}, u32[]{:S(2)}) copy-start(f32[1,4,125,1,256]{4,3,2,1,0:T(1,128)} %param.14) | copy-start | bytes 1536004
  17.8 19.7 %copy-start.4 = (f32[384,128]{1,0:T(8,128)S(1)}, f32[384,128]{1,0:T(8,128)}, u32[]{:S(2)}) copy-start(f32[384,128]{1,0:T(8,128)} %constant.18.clone.refs_5_.slopes_ref) | copy-start | bytes 589828
  17.8 19.7 %copy-start.5 = (f32[128,128]{1,0:T(8,128)S(1)}, f32[128,128]{1,0:T(8,128)}, u32[]{:S(2)}) copy-start(f32[128,128]{1,0:T(8,128)} %constant.20.clone.refs_6_.faces_ref) | copy-start | bytes 196612
  17.9 19.7 %copy-start.6 = (f32[64,128]{1,0:T(8,128)S(1)}, f32[64,128]{1,0:T(8,128)}, u32[]{:S(2)}) copy-start(f32[64,128]{1,0:T(8,128)} %constant.19.clone.refs_2_.to_grid_ref) | copy-start | bytes 98308
  17.9 19.7 %copy-start.8 = (s32[1,256]{1,0:T(1,128)S(1)}, s32[1,256]{1,0:T(1,128)}, u32[]{:S(2)}) copy-start(s32[1,256]{1,0:T(1,128)} %mask_ref.1) | copy-start | bytes 3076
  17.9 19.7 %copy-start.9 = (f32[1,256]{1,0:T(1,128)S(1)}, f32[1,256]{1,0:T(1,128)}, u32[]{:S(2)}) copy-start(f32[1,256]{1,0:T(1,128)} %damping_ref.1) | copy-start | bytes 3076
  17.9 24.1 %copy-start.1 = (bf16[4096,256]{1,0:T(8,128)(2,1)S(1)}, bf16[4096,256]{1,0:T(8,128)(2,1)}, u32[]{:S(2)}) copy-start(bf16[4096,256]{1,0:T(8,128)(2,1)} %constant.22.clone.refs_7_) | copy-start | bytes 6291460
  17.9 24.0 %copy-start.2 = (bf16[256,4096]{1,0:T(8,128)(2,1)S(1)}, bf16[256,4096]{1,0:T(8,128)(2,1)}, u32[]{:S(2)}) copy-start(bf16[256,4096]{1,0:T(8,128)(2,1)} %constant.21.clone.refs_6_) | copy-start | bytes 6291460
  17.9 24.0 %copy-start.10 = (f32[64]{0:T(128)S(1)}, f32[64]{0:T(128)}, u32[]{:S(2)}) copy-start(f32[64]{0:T(128)} %param.18) | copy-start | bytes 772
  30.4 21.8 %collective-permute-start.5 = (f32[64,1024]{1,0:T(8,128)S(1)}, f32[64,1024]{1,0:T(8,128)S(1)}, u32[]{:S(2)}, u32[]{:S(2)}) collective-permute-start(f32[64,1024]{1,0:T(8,128)S(1)} %get-tuple-element.31.refs_4_.refs_0_), channel_id=1, source_target_pairs={{0,24},{8,16},{16,8},{24,0},{1,25},{9,17},{17,9},{25,1},{2,26},{10... | collective-permute-start | bytes 786440 | tf_op jit(solution)/shard_map/ppermute | solution.py:479
  34.0 6.4 %collective-permute-start.12 = (bf16[64,1024]{1,0:T(8,128)(2,1)S(1)}, bf16[64,1024]{1,0:T(8,128)(2,1)S(1)}, u32[]{:S(2)}, u32[]{:S(2)}) collective-permute-start(bf16[64,1024]{1,0:T(8,128)(2,1)S(1)} %get-tuple-element.29.after_ref.refs_0_), channel_id=1, source_target_pairs={{0,6},{2,4},{4,2},{6,0},{1,7},{3,5},{5,3},{7,1},{8,14},{10,12},{12... | collective-permute-start | bytes 393224 | tf_op jit(solution)/shard_map/ppermute | solution.py:479
  35.5 6.3 %collective-permute-start.11 = (bf16[64,1024]{1,0:T(8,128)(2,1)S(1)}, bf16[64,1024]{1,0:T(8,128)(2,1)S(1)}, u32[]{:S(2)}, u32[]{:S(2)}) collective-permute-start(bf16[64,1024]{1,0:T(8,128)(2,1)S(1)} %get-tuple-element.29.after_ref.refs_0_), channel_id=1, source_target_pairs={{0,4},{2,6},{4,0},{6,2},{1,5},{3,7},{5,1},{7,3},{8,12},{10,14},{12... | collective-permute-start | bytes 393224 | tf_op jit(solution)/shard_map/ppermute | solution.py:479
  37.0 5.0 %collective-permute-start.10 = (bf16[64,1024]{1,0:T(8,128)(2,1)S(1)}, bf16[64,1024]{1,0:T(8,128)(2,1)S(1)}, u32[]{:S(2)}, u32[]{:S(2)}) collective-permute-start(bf16[64,1024]{1,0:T(8,128)(2,1)S(1)} %get-tuple-element.29.after_ref.refs_0_), channel_id=1, source_target_pairs={{0,2},{2,0},{4,6},{6,4},{1,3},{3,1},{5,7},{7,5},{8,10},{10,8},{12,... | collective-permute-start | bytes 393224 | tf_op jit(solution)/shard_map/ppermute | solution.py:479
  37.5 17.9 %collective-permute-start.4 = (f32[64,1024]{1,0:T(8,128)S(1)}, f32[64,1024]{1,0:T(8,128)S(1)}, u32[]{:S(2)}, u32[]{:S(2)}) collective-permute-start(f32[64,1024]{1,0:T(8,128)S(1)} %get-tuple-element.31.refs_4_.refs_0_), channel_id=1, source_target_pairs={{0,16},{8,24},{16,0},{24,8},{1,17},{9,25},{17,1},{25,9},{2,18},{10... | collective-permute-start | bytes 786440 | tf_op jit(solution)/shard_map/ppermute | solution.py:479
  40.5 20.9 %collective-permute-start.3 = (f32[64,1024]{1,0:T(8,128)S(1)}, f32[64,1024]{1,0:T(8,128)S(1)}, u32[]{:S(2)}, u32[]{:S(2)}) collective-permute-start(f32[64,1024]{1,0:T(8,128)S(1)} %get-tuple-element.31.refs_4_.refs_0_), channel_id=1, source_target_pairs={{0,8},{8,0},{16,24},{24,16},{1,9},{9,1},{17,25},{25,17},{2,10},{10... | collective-permute-start | bytes 786440 | tf_op jit(solution)/shard_map/ppermute | solution.py:479
  50.0 11.4 %collective-permute-start.15 = (f32[4,64,256]{2,1,0:T(8,128)S(1)}, f32[4,64,256]{2,1,0:T(8,128)S(1)}, u32[]{:S(2)}, u32[]{:S(2)}) collective-permute-start(f32[4,64,256]{2,1,0:T(8,128)S(1)} %backward.1.refs_2_.refs_0_), channel_id=1, source_target_pairs={{0,6},{2,4},{4,2},{6,0},{1,7},{3,5},{5,3},{7,1},{8,14},{10,12},{12... | collective-permute-start | bytes 786440 | tf_op jit(solution)/shard_map/ppermute | solution.py:479
  51.4 11.7 %collective-permute-start.14 = (f32[4,64,256]{2,1,0:T(8,128)S(1)}, f32[4,64,256]{2,1,0:T(8,128)S(1)}, u32[]{:S(2)}, u32[]{:S(2)}) collective-permute-start(f32[4,64,256]{2,1,0:T(8,128)S(1)} %backward.1.refs_2_.refs_0_), channel_id=1, source_target_pairs={{0,4},{2,6},{4,0},{6,2},{1,5},{3,7},{5,1},{7,3},{8,12},{10,14},{12... | collective-permute-start | bytes 786440 | tf_op jit(solution)/shard_map/ppermute | solution.py:479
  52.1 10.9 %collective-permute-start.13 = (f32[4,64,256]{2,1,0:T(8,128)S(1)}, f32[4,64,256]{2,1,0:T(8,128)S(1)}, u32[]{:S(2)}, u32[]{:S(2)}) collective-permute-start(f32[4,64,256]{2,1,0:T(8,128)S(1)} %backward.1.refs_2_.refs_0_), channel_id=1, source_target_pairs={{0,2},{2,0},{4,6},{6,4},{1,3},{3,1},{5,7},{7,5},{8,10},{10,8},{12,... | collective-permute-start | bytes 786440 | tf_op jit(solution)/shard_map/ppermute | solution.py:479
  55.4 10.3 %collective-permute-start.6 = (f32[64,1024]{1,0:T(8,128)S(1)}, f32[64,1024]{1,0:T(8,128)S(1)}, u32[]{:S(2)}, u32[]{:S(2)}) collective-permute-start(f32[64,1024]{1,0:T(8,128)S(1)} %get-tuple-element.31.refs_4_.refs_0_), channel_id=1, source_target_pairs={{0,1},{1,0},{2,3},{3,2},{4,5},{5,4},{6,7},{7,6},{8,9},{9,8},{10,11... | collective-permute-start | bytes 786440 | tf_op jit(solution)/shard_map/ppermute | solution.py:479
  63.1 19.9 %slice-start = ((s8[16777216]{0:T(1024)(128)(4,1)}), s8[4194304]{0:T(1024)(128)(4,1)S(1)}, s32[]{:S(2)}) async-start(s8[16777216]{0:T(1024)(128)(4,1)} %bitcast.11), calls=%async_computation | async-start | bytes 8388608
  63.1 19.9 %slice-start.1 = ((s8[16777216]{0:T(1024)(128)(4,1)}), s8[4194304]{0:T(1024)(128)(4,1)S(1)}, s32[]{:S(2)}) async-start(s8[16777216]{0:T(1024)(128)(4,1)} %bitcast.11), calls=%async_computation.1 | async-start | bytes 8388608
  63.1 19.9 %slice-start.2 = ((s8[16777216]{0:T(1024)(128)(4,1)}), s8[4194304]{0:T(1024)(128)(4,1)S(1)}, s32[]{:S(2)}) async-start(s8[16777216]{0:T(1024)(128)(4,1)} %bitcast.11), calls=%async_computation.2 | async-start | bytes 8388608
  64.1 8.0 %collective-permute-start.18 = (f32[64,512]{1,0:T(8,128)S(1)}, f32[64,512]{1,0:T(8,128)S(1)}, u32[]{:S(2)}, u32[]{:S(2)}) collective-permute-start(f32[64,512]{1,0:T(8,128)S(1)} %get-tuple-element.34.refs_1_.refs_8_), channel_id=1, source_target_pairs={{0,24},{8,16},{16,8},{24,0},{1,25},{9,17},{17,9},{25,1},{2,26},{10... | collective-permute-start | bytes 393224 | tf_op jit(solution)/shard_map/ppermute | solution.py:479
  65.0 12.9 %collective-permute-start.9 = (f32[64,1024]{1,0:T(8,128)S(1)}, f32[64,1024]{1,0:T(8,128)S(1)}, u32[]{:S(2)}, u32[]{:S(2)}) collective-permute-start(f32[64,1024]{1,0:T(8,128)S(1)} %collective-permute-done.5.refs_7_.refs_3_), channel_id=1, source_target_pairs={{0,1},{1,0},{2,3},{3,2},{4,5},{5,4},{6,7},{7,6},{8,9},{9,8},{10,11... | collective-permute-start | bytes 786440 | tf_op jit(solution)/shard_map/ppermute | solution.py:479
  65.2 15.4 %collective-permute-start.8 = (f32[64,1024]{1,0:T(8,128)S(1)}, f32[64,1024]{1,0:T(8,128)S(1)}, u32[]{:S(2)}, u32[]{:S(2)}) collective-permute-start(f32[64,1024]{1,0:T(8,128)S(1)} %collective-permute-done.4.refs_6_.refs_2_), channel_id=1, source_target_pairs={{0,1},{1,0},{2,3},{3,2},{4,5},{5,4},{6,7},{7,6},{8,9},{9,8},{10,11... | collective-permute-start | bytes 786440 | tf_op jit(solution)/shard_map/ppermute | solution.py:479
  65.5 15.2 %collective-permute-start.7 = (f32[64,1024]{1,0:T(8,128)S(1)}, f32[64,1024]{1,0:T(8,128)S(1)}, u32[]{:S(2)}, u32[]{:S(2)}) collective-permute-start(f32[64,1024]{1,0:T(8,128)S(1)} %collective-permute-done.3.refs_5_.refs_1_), channel_id=1, source_target_pairs={{0,1},{1,0},{2,3},{3,2},{4,5},{5,4},{6,7},{7,6},{8,9},{9,8},{10,11... | collective-permute-start | bytes 786440 | tf_op jit(solution)/shard_map/ppermute | solution.py:479
  65.7 10.9 %collective-permute-start.17 = (f32[64,512]{1,0:T(8,128)S(1)}, f32[64,512]{1,0:T(8,128)S(1)}, u32[]{:S(2)}, u32[]{:S(2)}) collective-permute-start(f32[64,512]{1,0:T(8,128)S(1)} %get-tuple-element.34.refs_1_.refs_8_), channel_id=1, source_target_pairs={{0,16},{8,24},{16,0},{24,8},{1,17},{9,25},{17,1},{25,9},{2,18},{10... | collective-permute-start | bytes 393224 | tf_op jit(solution)/shard_map/ppermute | solution.py:479
  72.1 5.9 %collective-permute-start.16 = (f32[64,512]{1,0:T(8,128)S(1)}, f32[64,512]{1,0:T(8,128)S(1)}, u32[]{:S(2)}, u32[]{:S(2)}) collective-permute-start(f32[64,512]{1,0:T(8,128)S(1)} %get-tuple-element.34.refs_1_.refs_8_), channel_id=1, source_target_pairs={{0,8},{8,0},{16,24},{24,16},{1,9},{9,1},{17,25},{25,17},{2,10},{10... | collective-permute-start | bytes 393224 | tf_op jit(solution)/shard_map/ppermute | solution.py:479
  76.6 4.5 %collective-permute-start.22 = (f32[64,512]{1,0:T(8,128)S(1)}, f32[64,512]{1,0:T(8,128)S(1)}, u32[]{:S(2)}, u32[]{:S(2)}) collective-permute-start(f32[64,512]{1,0:T(8,128)S(1)} %get-tuple-element.34.refs_1_.refs_8_), channel_id=1, source_target_pairs={{0,1},{1,0},{2,3},{3,2},{4,5},{5,4},{6,7},{7,6},{8,9},{9,8},{10,11... | collective-permute-start | bytes 393224 | tf_op jit(solution)/shard_map/ppermute | solution.py:479
  77.9 3.1 %collective-permute-start.25 = (f32[64,512]{1,0:T(8,128)S(1)}, f32[64,512]{1,0:T(8,128)S(1)}, u32[]{:S(2)}, u32[]{:S(2)}) collective-permute-start(f32[64,512]{1,0:T(8,128)S(1)} %collective-permute-done.18.refs_4_.refs_11_), channel_id=1, source_target_pairs={{0,1},{1,0},{2,3},{3,2},{4,5},{5,4},{6,7},{7,6},{8,9},{9,8},{10,11... | collective-permute-start | bytes 393224 | tf_op jit(solution)/shard_map/ppermute | solution.py:479
  77.9 19.0 %slice-start.4 = ((s8[16777216]{0:T(1024)(128)(4,1)}), s8[4194304]{0:T(1024)(128)(4,1)S(1)}, s32[]{:S(2)}) async-start(s8[16777216]{0:T(1024)(128)(4,1)} %bitcast.13), calls=%async_computation.4 | async-start | bytes 8388608
  77.9 19.0 %slice-start.5 = ((s8[16777216]{0:T(1024)(128)(4,1)}), s8[4194304]{0:T(1024)(128)(4,1)S(1)}, s32[]{:S(2)}) async-start(s8[16777216]{0:T(1024)(128)(4,1)} %bitcast.13), calls=%async_computation.5 | async-start | bytes 8388608
  77.9 19.0 %slice-start.6 = ((s8[16777216]{0:T(1024)(128)(4,1)}), s8[4194304]{0:T(1024)(128)(4,1)S(1)}, s32[]{:S(2)}) async-start(s8[16777216]{0:T(1024)(128)(4,1)} %bitcast.13), calls=%async_computation.6 | async-start | bytes 8388608
  78.0 18.9 %slice-start.7 = ((s8[16777216]{0:T(1024)(128)(4,1)}), s8[4194304]{0:T(1024)(128)(4,1)S(1)}, s32[]{:S(2)}) async-start(s8[16777216]{0:T(1024)(128)(4,1)} %bitcast.13), calls=%async_computation.7 | async-start | bytes 8388608
  78.0 16.8 %collective-permute-start.21 = (f32[64,512]{1,0:T(8,128)S(1)}, f32[64,512]{1,0:T(8,128)S(1)}, u32[]{:S(2)}, u32[]{:S(2)}) collective-permute-start(f32[64,512]{1,0:T(8,128)S(1)} %passed.2.refs_0_), channel_id=1, source_target_pairs={{0,24},{8,16},{16,8},{24,0},{1,25},{9,17},{17,9},{25,1},{2,26},{10... | collective-permute-start | bytes 393224 | tf_op jit(solution)/shard_map/ppermute | solution.py:479
  80.5 2.4 %collective-permute-start.24 = (f32[64,512]{1,0:T(8,128)S(1)}, f32[64,512]{1,0:T(8,128)S(1)}, u32[]{:S(2)}, u32[]{:S(2)}) collective-permute-start(f32[64,512]{1,0:T(8,128)S(1)} %collective-permute-done.17.refs_3_.refs_10_), channel_id=1, source_target_pairs={{0,1},{1,0},{2,3},{3,2},{4,5},{5,4},{6,7},{7,6},{8,9},{9,8},{10,11... | collective-permute-start | bytes 393224 | tf_op jit(solution)/shard_map/ppermute | solution.py:479
  80.8 2.2 %collective-permute-start.23 = (f32[64,512]{1,0:T(8,128)S(1)}, f32[64,512]{1,0:T(8,128)S(1)}, u32[]{:S(2)}, u32[]{:S(2)}) collective-permute-start(f32[64,512]{1,0:T(8,128)S(1)} %collective-permute-done.16.refs_2_.refs_9_), channel_id=1, source_target_pairs={{0,1},{1,0},{2,3},{3,2},{4,5},{5,4},{6,7},{7,6},{8,9},{9,8},{10,11... | collective-permute-start | bytes 393224 | tf_op jit(solution)/shard_map/ppermute | solution.py:479
  81.1 13.7 %collective-permute-start.20 = (f32[64,512]{1,0:T(8,128)S(1)}, f32[64,512]{1,0:T(8,128)S(1)}, u32[]{:S(2)}, u32[]{:S(2)}) collective-permute-start(f32[64,512]{1,0:T(8,128)S(1)} %passed.2.refs_0_), channel_id=1, source_target_pairs={{0,16},{8,24},{16,0},{24,8},{1,17},{9,25},{17,1},{25,9},{2,18},{10... | collective-permute-start | bytes 393224 | tf_op jit(solution)/shard_map/ppermute | solution.py:479
  81.1 13.7 %collective-permute-start.19 = (f32[64,512]{1,0:T(8,128)S(1)}, f32[64,512]{1,0:T(8,128)S(1)}, u32[]{:S(2)}, u32[]{:S(2)}) collective-permute-start(f32[64,512]{1,0:T(8,128)S(1)} %passed.2.refs_0_), channel_id=1, source_target_pairs={{0,8},{8,0},{16,24},{24,16},{1,9},{9,1},{17,25},{25,17},{2,10},{10... | collective-permute-start | bytes 393224 | tf_op jit(solution)/shard_map/ppermute | solution.py:479
  94.8 1.4 %collective-permute-start.26 = (f32[64,512]{1,0:T(8,128)S(1)}, f32[64,512]{1,0:T(8,128)S(1)}, u32[]{:S(2)}, u32[]{:S(2)}) collective-permute-start(f32[64,512]{1,0:T(8,128)S(1)} %get-tuple-element.36.refs_8_), channel_id=1, source_target_pairs={{0,1},{1,0},{2,3},{3,2},{4,5},{5,4},{6,7},{7,6},{8,9},{9,8},{10,11... | collective-permute-start | bytes 393224 | tf_op jit(solution)/shard_map/ppermute | solution.py:479
  94.9 1.5 %collective-permute-start.27 = (f32[64,512]{1,0:T(8,128)S(1)}, f32[64,512]{1,0:T(8,128)S(1)}, u32[]{:S(2)}, u32[]{:S(2)}) collective-permute-start(f32[64,512]{1,0:T(8,128)S(1)} %get-tuple-element.37.refs_9_), channel_id=1, source_target_pairs={{0,1},{1,0},{2,3},{3,2},{4,5},{5,4},{6,7},{7,6},{8,9},{9,8},{10,11... | collective-permute-start | bytes 393224 | tf_op jit(solution)/shard_map/ppermute | solution.py:479
  95.4 1.3 %collective-permute-start.28 = (f32[64,512]{1,0:T(8,128)S(1)}, f32[64,512]{1,0:T(8,128)S(1)}, u32[]{:S(2)}, u32[]{:S(2)}) collective-permute-start(f32[64,512]{1,0:T(8,128)S(1)} %get-tuple-element.38.refs_10_), channel_id=1, source_target_pairs={{0,1},{1,0},{2,3},{3,2},{4,5},{5,4},{6,7},{7,6},{8,9},{9,8},{10,11... | collective-permute-start | bytes 393224 | tf_op jit(solution)/shard_map/ppermute | solution.py:479
  95.4 1.5 %collective-permute-start.29 = (f32[64,512]{1,0:T(8,128)S(1)}, f32[64,512]{1,0:T(8,128)S(1)}, u32[]{:S(2)}, u32[]{:S(2)}) collective-permute-start(f32[64,512]{1,0:T(8,128)S(1)} %get-tuple-element.39.refs_11_), channel_id=1, source_target_pairs={{0,1},{1,0},{2,3},{3,2},{4,5},{5,4},{6,7},{7,6},{8,9},{9,8},{10,11... | collective-permute-start | bytes 393224 | tf_op jit(solution)/shard_map/ppermute | solution.py:479
  (1 other events, 5.1 us)
